TPU v7x, 128 devices: a whole 4x4x4 slice. The times are simulated.
128 devices in a mesh: gx: 16 (over x_hi, y, core), gy: 8 (over z, x_lo).
Axes of the slice: x: 4 (x_hi: 2, x_lo: 2; x = x_hi * 2 + x_lo), y: 4, z: 4, core: 2. Of those that a mesh axis runs over, the one named last changes fastest.
Arguments:
- te_init: float32 [768, 256, 128], P(('gx', 'gy')), may hold values from 0.5 to 3
- source: float32 [768, 256, 128], P(('gx', 'gy')), may hold values from 0.01 to 0.5
- velocities: float32 [3, 16, 8, 16384], P(None, 'gx', 'gy'), may hold values from -6 to 6
- noise: float32 [3, 16, 8, 16384], P(None, 'gx', 'gy'), may hold values from -6 to 6
- cell_index: int32 [16, 8, 16384], P('gx', 'gy'), may hold values from 0 to 1535
- cell_lane: int32 [16, 8, 16384], P('gx', 'gy'), may hold values from 0 to 127
- brick_atoms: int32 [16, 8], P('gx', 'gy'), may hold values from 2048 to 16384, as said below
Outputs:
- electron_temp: float32 [768, 256, 128], P(('gx', 'gy'))
- forces: float32 [3, 16, 8, 16384], P(None, 'gx', 'gy')
Inputs may be any that keep to these rules, and one draw needn't show every extreme that they name: `cell_index`: cell columns are depth-major within the brick: d * 32 + y. `brick_atoms`: live atoms fill slots 0 to count - 1 of their brick; at least one brick is full.
All inputs are finite; a program needn't handle non-finite values.
Results may differ from a plain program's by a relative error of at most 0.00011.
Values sent between devices are 32-bit elements; how exact they have to be, the bound alone decides.
No kernel may reach another device: no remote copies, remote signals or barrier semaphores. Data moves between devices by JAX's collectives and lax.ppermute only.
A program may use at most 64 MiB of HBM per device.

v0:
```python
import functools

import jax
import jax.numpy as jnp
from jax import lax
from jax.experimental import pallas as pl
from jax.experimental.pallas import tpu as pltpu
from jax.sharding import PartitionSpec as P

CX = 48
CY = 32
NZ = 128
CONDUCTIVITY = 0.08
COUPLING = 0.1
FRICTION = 0.5

HALO = 4
NEAR = HALO - 1
ROWS = CY + 2 * HALO
COLS = CX * CY
GROUP = 6
BLOCK = 2048
MIB = 1024 * 1024

VMEM = pl.BlockSpec(memory_space=pltpu.VMEM)
SMEM = pl.BlockSpec(memory_space=pltpu.SMEM)


def params(mib):
    return pltpu.CompilerParams(vmem_limit_bytes=mib * MIB)


def f32(*shape):
    return jax.ShapeDtypeStruct(shape, jnp.float32)


def inverse(value):
    return 1.0 / value


def flux(u, r, v, q):
    return (v - u) * inverse(r + q)


def renewed(u, c, r, below, above, heat, load):
    rows = u.shape[0]
    side = flux(u, r, pltpu.roll(u, rows - 1, 0), pltpu.roll(r, rows - 1, 0))
    lane = flux(u, r, pltpu.roll(u, NZ - 1, 1), pltpu.roll(r, NZ - 1, 1))
    total = (above - below) + (side - pltpu.roll(side, 1, 0)) + (lane - pltpu.roll(lane, 1, 1))
    return (u * c + (2.0 * CONDUCTIVITY) * total + heat) * inverse(c + load)


def with_root(u):
    c = 1.0 + u * u
    return c, lax.rsqrt(c)


def interior_kernel(te, heat, load, out, first, second):
    def step(source, target, shift):
        below_u = source[0]
        _, below_r = with_root(below_u)
        u = source[1]
        c, r = with_root(u)

        def turn(i, carry):
            u, c, r, below = carry
            for g in range(GROUP):
                layer = i * GROUP + g
                v = source[layer + 2]
                cv, rv = with_root(v)
                above = flux(u, r, v, rv)
                target[layer + shift] = renewed(u, c, r, below, above, heat[layer], load[layer])
                u, c, r, below = v, cv, rv, above
            return u, c, r, below

        lax.fori_loop(0, CX // GROUP, turn, (u, c, r, flux(below_u, below_r, u, r)))

    first[pl.ds(1, CX)] = te[...]
    for buffer in (first, second):
        buffer[0] = te[0]
        buffer[CX + 1] = te[CX - 1]
    step(first, second, 1)
    step(second, first, 1)
    step(first, second, 1)
    step(second, out, 0)


def interior(te, heat, load):
    return pl.pallas_call(
        interior_kernel,
        out_shape=f32(CX, ROWS, NZ),
        in_specs=[VMEM] * 3,
        out_specs=VMEM,
        scratch_shapes=[pltpu.VMEM((CX + 2, ROWS, NZ), jnp.float32)] * 2,
        compiler_params=params(32),
        cost_estimate=pl.CostEstimate(flops=0, bytes_accessed=25_000_000, transcendentals=0),
        name="interior",
    )(te, heat, load)


def band_steps(us, heats, loads, closed_face, closed):
    for step in range(1, HALO + 1):
        us = list(us)
        roots = [with_root(u) for u in us]
        faces = []
        for i in range(len(us) - 1):
            face = flux(us[i], roots[i][1], us[i + 1], roots[i + 1][1])
            if i + step - 1 == closed_face:
                face = jnp.where(closed, 0.0, face)
            faces.append(face)
        us = [
            renewed(
                us[i],
                *roots[i],
                faces[i - 1],
                faces[i],
                heats[i + step - 2],
                loads[i + step - 2],
            )
            for i in range(1, len(us) - 1)
        ]
    return us


def bands_kernel(last, place, te, heat, load, te_lo, te_hi, lo, hi, inner, out, *faces):
    many = 2 * HALO
    near = HALO + NEAR
    low = band_steps(
        [te_lo[i] for i in range(HALO)] + [te[i] for i in range(many)],
        [lo[HALO + i] for i in range(NEAR)] + [heat[i] for i in range(near)],
        [lo[HALO + NEAR + i] for i in range(NEAR)] + [load[i] for i in range(near)],
        HALO - 1,
        place[0] == 1,
    )
    high = band_steps(
        [te[CX - many + i] for i in range(many)] + [te_hi[i] for i in range(HALO)],
        [heat[CX - near + i] for i in range(near)] + [hi[HALO + i] for i in range(NEAR)],
        [load[CX - near + i] for i in range(near)] + [hi[HALO + NEAR + i] for i in range(NEAR)],
        many - 1,
        place[1] == 1,
    )
    out[pl.ds(HALO, CX - many)] = inner[pl.ds(HALO, CX - many), :CY]
    for i in range(HALO):
        out[i] = low[i][:CY]
        out[CX - HALO + i] = high[i][:CY]
    if not last:
        head, tail = faces
        half = CX // 2
        head[:, :HALO] = out[:half, :HALO]
        head[:, HALO:] = out[half:, :HALO]
        tail[:, :HALO] = out[:half, CY - HALO :]
        tail[:, HALO:] = out[half:, CY - HALO :]


def bands(last, place, te, heat, load, te_lo, te_hi, lo, hi, inner):
    face = f32(CX // 2, 2 * HALO, NZ)
    shapes = [f32(CX, CY, NZ)] + ([] if last else [face, face])
    return pl.pallas_call(
        functools.partial(bands_kernel, last),
        out_shape=shapes,
        in_specs=[SMEM] + [VMEM] * 8,
        out_specs=[VMEM] * len(shapes),
        compiler_params=params(32),
        cost_estimate=pl.CostEstimate(flops=0, bytes_accessed=8_000_000, transcendentals=0),
        name="bands",
    )(place, te, heat, load, te_lo, te_hi, lo, hi, inner)


def first_kernel(parts, fields, load_in, kinetic, before, after, te, heat, load, head, tail):
    layers = CX // parts
    for j in range(parts):
        te[pl.ds(j * layers, layers)] = fields[pl.ds(2 * j * layers, layers)]
        span = pl.ds(j * layers, layers)
        source = pl.ds((2 * j + 1) * layers, layers)
        heat[span, :CY] = fields[source, :CY] + kinetic[span]
        heat[span, CY:] = fields[source, CY:] + jnp.concatenate(
            [after[span, HALO:], before[span, HALO:]], 1
        )
        load[span, :CY] = load_in[span]
        load[span, CY:] = jnp.concatenate([after[span, :HALO], before[span, :HALO]], 1)
    head[:HALO] = te[:HALO]
    tail[:HALO] = te[CX - HALO :]
    for place, field in ((HALO, heat), (HALO + NEAR, load)):
        head[pl.ds(place, NEAR)] = field[:NEAR]
        tail[pl.ds(place, NEAR)] = field[CX - NEAR :]


def first_brick(parts, fields, load, kinetic, before, after):
    whole = f32(CX, ROWS, NZ)
    edge = f32(HALO + 2 * NEAR, ROWS, NZ)
    return pl.pallas_call(
        functools.partial(first_kernel, parts),
        out_shape=[whole, whole, whole, edge, edge],
        in_specs=[VMEM] * 5,
        out_specs=[VMEM] * 5,
        compiler_params=params(32),
        cost_estimate=pl.CostEstimate(flops=0, bytes_accessed=4_000_000, transcendentals=0),
        name="first_brick",
    )(fields, load, kinetic, before, after)


def second_kernel(middle, before, after, te, head, tail):
    half = CX // 2
    te[:, :CY] = middle[...]
    te[:half, CY:] = jnp.concatenate([after[:, :HALO], before[:, :HALO]], 1)
    te[half:, CY:] = jnp.concatenate([after[:, HALO:], before[:, HALO:]], 1)
    head[...] = te[:HALO]
    tail[...] = te[CX - HALO :]


def second_brick(middle, before, after):
    edge = f32(HALO, ROWS, NZ)
    return pl.pallas_call(
        second_kernel,
        out_shape=[f32(CX, ROWS, NZ), edge, edge],
        in_specs=[VMEM] * 3,
        out_specs=[VMEM] * 3,
        compiler_params=params(32),
        cost_estimate=pl.CostEstimate(flops=0, bytes_accessed=4_000_000, transcendentals=0),
        name="second_brick",
    )(middle, before, after)


def column_hot(column):
    ids = lax.broadcasted_iota(jnp.int16, (COLS, column.shape[1]), 0)
    hot = ids == column.astype(jnp.int16)
    return jnp.where(hot, jnp.bfloat16(1), jnp.bfloat16(0))


def lane_mask(lane):
    return lax.broadcasted_iota(jnp.int32, (NZ, lane.shape[1]), 0) == lane


def living_of(count, block):
    slot = pl.program_id(0) * block + lax.broadcasted_iota(jnp.int32, (1, block), 1)
    return jnp.where(slot < count[0, 0], 1.0, 0.0)


def bin_kernel(block, count, column, lane, velocities, load, kinetic, head, tail, sums):
    @pl.when(pl.program_id(0) == 0)
    def _():
        sums[...] = jnp.zeros_like(sums)

    living = living_of(count, block)
    moving = velocities[...]
    energy = living * (moving[0] * moving[0] + moving[1] * moving[1] + moving[2] * moving[2]) / 3.0
    mask = lane_mask(lane[...])
    spread = jnp.where(mask, energy, 0.0)
    high = spread.astype(jnp.bfloat16)
    low = (spread - high.astype(jnp.float32)).astype(jnp.bfloat16)
    weighted = jnp.concatenate([jnp.where(mask, living, 0.0).astype(jnp.bfloat16), high, low], 0)
    term = lax.dot_general(
        weighted,
        column_hot(column[...]),
        (((1,), (1,)), ((), ())),
        preferred_element_type=jnp.float32,
    )
    sums[:NZ] += term[:NZ]
    sums[NZ:] += term[NZ : 2 * NZ] + term[2 * NZ :]

    @pl.when(pl.program_id(0) == pl.num_programs(0) - 1)
    def _():
        layers = NZ // CY
        for j in range(COLS // NZ):
            part = pl.ds(j * NZ, NZ)
            span = pl.ds(j * layers, layers)
            tally = sums[:NZ, part]
            heat = sums[NZ:, part]
            load[span] = (COUPLING * tally.T).reshape(layers, CY, NZ)
            kinetic[span] = (COUPLING * heat.T).reshape(layers, CY, NZ)
        head[:, :HALO] = load[:, :HALO]
        head[:, HALO:] = kinetic[:, :HALO]
        tail[:, :HALO] = load[:, CY - HALO :]
        tail[:, HALO:] = kinetic[:, CY - HALO :]


def blocks_of(shape, block):
    return pl.BlockSpec(shape + (block,), lambda i: (0,) * len(shape) + (i,))


def whole_of(*shape):
    return pl.BlockSpec(shape, lambda i: (0,) * len(shape))


def bin_atoms(count, column, lane, velocities):
    slots = column.shape[1]
    block = min(BLOCK, slots)
    brick = (CX, CY, NZ)
    face = (CX, 2 * HALO, NZ)
    return pl.pallas_call(
        functools.partial(bin_kernel, block),
        grid=(slots // block,),
        out_shape=[f32(*brick), f32(*brick), f32(*face), f32(*face)],
        in_specs=[SMEM, blocks_of((1,), block), blocks_of((1,), block), blocks_of((3, 1), block)],
        out_specs=[whole_of(*brick), whole_of(*brick), whole_of(*face), whole_of(*face)],
        scratch_shapes=[pltpu.VMEM((2 * NZ, COLS), jnp.float32)],
        compiler_params=params(48),
        cost_estimate=pl.CostEstimate(
            flops=6 * slots * COLS * NZ, bytes_accessed=4_000_000, transcendentals=0
        ),
        name="bin_atoms",
    )(count, column, lane, velocities)


def read_kernel(block, count, te, column, lane, velocities, noise, forces, pair):
    @pl.when(pl.program_id(0) == 0)
    def _():
        table = te[...].T
        high = table.astype(jnp.bfloat16)
        pair[:NZ] = high
        pair[NZ:] = (table - high.astype(jnp.float32)).astype(jnp.bfloat16)

    rows = jnp.dot(pair[...], column_hot(column[...]), preferred_element_type=jnp.float32)
    picked = jnp.where(lane_mask(lane[...]), rows[:NZ] + rows[NZ:], 0.0)
    te_atom = jnp.sum(picked, axis=0, keepdims=True)
    drive = jnp.sqrt(2.0 * FRICTION * te_atom)
    forces[...] = living_of(count, block) * (-FRICTION * velocities[...] + drive * noise[...])


def read_atoms(count, te, column, lane, velocities, noise):
    slots = column.shape[1]
    block = min(BLOCK, slots)
    return pl.pallas_call(
        functools.partial(read_kernel, block),
        grid=(slots // block,),
        out_shape=f32(3, 1, slots),
        in_specs=[
            SMEM,
            whole_of(COLS, NZ),
            blocks_of((1,), block),
            blocks_of((1,), block),
            blocks_of((3, 1), block),
            blocks_of((3, 1), block),
        ],
        out_specs=blocks_of((3, 1), block),
        scratch_shapes=[pltpu.VMEM((2 * NZ, COLS), jnp.bfloat16)],
        compiler_params=params(48),
        cost_estimate=pl.CostEstimate(
            flops=4 * slots * COLS * NZ, bytes_accessed=4_000_000, transcendentals=0
        ),
        name="read_atoms",
    )(count, te, column, lane, velocities, noise)


def widened(field, parts):
    layers = field.shape[0]
    blocks = field.reshape(layers, parts, CY, NZ).transpose(1, 0, 2, 3)
    after = jnp.roll(blocks, -1, 0)[:, :, :HALO]
    before = jnp.roll(blocks, 1, 0)[:, :, CY - HALO :]
    return jnp.concatenate([blocks, after, before], 2)


def to_both_sides(head, tail, axis):
    count = lax.axis_size(axis)
    from_before = lax.ppermute(tail, axis, [(i, (i + 1) % count) for i in range(count)])
    from_after = lax.ppermute(head, axis, [((i + 1) % count, i) for i in range(count)])
    return from_before, from_after


def exchanged(blocks):
    return lax.all_to_all(blocks, "gy", split_axis=0, concat_axis=0, tiled=True)


def on_device(te_init, source, velocities, noise, cell_index, cell_lane, brick_atoms):
    parts = lax.axis_size("gy")
    layers = te_init.shape[0]
    fields = jnp.concatenate([widened(te_init, parts), widened(source, parts)], 1)
    fields = exchanged(fields.reshape(2 * parts * layers, ROWS, NZ))

    column = cell_index[0]
    lane = cell_lane[0]
    moving = velocities[:, 0]
    load, kinetic, head, tail = bin_atoms(brick_atoms, column, lane, moving)
    before, after = to_both_sides(head, tail, "gy")

    position = lax.axis_index("gx")
    final = lax.axis_size("gx") - 1
    place = jnp.stack([position == 0, position == final]).astype(jnp.int32)
    te, heat, load, head, tail = first_brick(parts, fields, load, kinetic, before, after)
    lo, hi = to_both_sides(head, tail, "gx")
    inner = interior(te, heat, load)
    middle, head, tail = bands(False, place, te, heat, load, lo, hi, lo, hi, inner)

    before, after = to_both_sides(head, tail, "gy")
    te, head, tail = second_brick(middle, before, after)
    te_lo, te_hi = to_both_sides(head, tail, "gx")
    inner = interior(te, heat, load)
    (te,) = bands(True, place, te, heat, load, te_lo, te_hi, lo, hi, inner)

    electron = exchanged(te).reshape(parts, layers, CY, NZ).transpose(1, 0, 2, 3)
    electron = electron.reshape(layers, parts * CY, NZ)
    forces = read_atoms(brick_atoms, te.reshape(COLS, NZ), column, lane, moving, noise[:, 0])
    return (electron, forces[:, None])


def solution(mesh):
    return jax.shard_map(
        on_device,
        mesh=mesh,
        in_specs=(
            P(("gx", "gy"), None, None),
            P(("gx", "gy"), None, None),
            P(None, "gx", "gy", None),
            P(None, "gx", "gy", None),
            P("gx", "gy", None),
            P("gx", "gy", None),
            P("gx", "gy"),
        ),
        out_specs=(P(("gx", "gy"), None, None), P(None, "gx", "gy", None)),
        check_vma=False,
    )
```

profile of v0, /device:TPU:4, one launch (start us, length us, event | category | flops | bytes accessed | tf_op | source)
XLA Modules:
  0.0 115.0 jit_solution(14145053499199269653)
XLA Ops:
  0.6 1.5 %copy_bitcast_fusion = (f32[8,6,32,128]{3,2,1,0:T(8,128)S(1)}, f32[8,6,32,128]{3,2,1,0:T(8,128)S(1)}) fusion(f32[6,8,32,128]{3,2,1,0:T(8,128)} %bitcast.31, f32[6,8,32,128]{3,2,1,0:T(8,128)} %bitcast.32), kind=kLoop, calls=%fused_computation.18 | loop fusion | bytes 3145728 | tf_op jit(solution)/shard_map/transpose | solution.py:347
  2.1 0.2 fusion.9
  2.3 0.2 fusion.11
  2.5 1.5 %fusion.5 = f32[8,12,40,128]{3,2,1,0:T(8,128)} fusion(f32[7,6,32,128]{3,2,1,0:T(8,128)S(1)} %get-tuple-element.39, f32[1,6,32,128]{3,2,1,0:T(8,128)S(1)} %get-tuple-element.41, f32[1,6,32,128]{3,2,1,0:T(8,128)S(1)} %get-tuple-element.40, f32[7,6,32,128]{3,2,1,0:T(8,128)S(1)} %get-tuple-element.38, f32[7,6,32,128]{3,2,1,0:T(8,128)S(1)} %get-tuple-element.35, ...), kind=kLoop, calls=%fused_computation.8 | loop fusion | flops 17694720 | bytes 6684672 | tf_op jit(solution)/shard_map/concatenate | solution.py:367
  4.0 0.0 copy-start.6
  4.0 0.0 copy-start.8
  4.0 0.0 copy-start.10
  4.0 6.1 %all-to-all-start = ((f32[96,40,128]{2,1,0:T(8,128)}), f32[96,40,128]{2,1,0:T(8,128)S(1)}, u32[]{:S(2)}, u32[]{:S(2)}) async-start(f32[96,40,128]{2,1,0:T(8,128)} %bitcast.28), calls=%async_computation | async-start | bytes 3932160 | tf_op jit(solution)/shard_map/all_to_all | solution.py:361
  10.7 0.0 copy-done.6
  10.7 0.0 copy-done.8
  10.7 0.0 copy-done.10
  10.7 21.9 %bin_atoms.1 = (f32[48,32,128]{2,1,0:T(8,128)S(1)}, f32[48,32,128]{2,1,0:T(8,128)S(1)}, f32[48,8,128]{2,1,0:T(8,128)S(1)}, f32[48,8,128]{2,1,0:T(8,128)S(1)}) custom-call(s32[1,1]{1,0:T(1,128)S(6)} %copy.15.count, s32[1,16384]{1,0:T(1,128)S(1)} %bitcast.24, s32[1,16384]{1,0:T(1,128)S(1)} %bitcast.26, f32[3,1,16384]{2,1,0:T(1,128)S(1)} %bitcast.21), custom_call_target="tpu_custom_call" | custom-call | flops 19327352832 | bytes 4000000 | tf_op jit(solution)/shard_map/bin_atoms/pallas_call | solution.py:290
  32.7 0.0 copy-start.2
  32.7 0.9 copy-done.2
  33.5 0.0 copy-start.4
  33.5 0.9 copy-done.4
  34.4 2.0 %collective-permute-start = (f32[48,8,128]{2,1,0:T(8,128)S(1)}, f32[48,8,128]{2,1,0:T(8,128)S(1)}, u32[]{:S(2)}, u32[]{:S(2)}) collective-permute-start(f32[48,8,128]{2,1,0:T(8,128)S(1)} %get-tuple-element.19), channel_id=1, source_target_pairs={{0,1},{1,2},{2,3},{3,4},{4,5},{5,6},{6,7},{7,0},{8,9},{9,10},{10,1... | collective-permute-start | bytes 589832 | tf_op jit(solution)/shard_map/ppermute | solution.py:355
  36.4 2.1 %collective-permute-start.1 = (f32[48,8,128]{2,1,0:T(8,128)S(1)}, f32[48,8,128]{2,1,0:T(8,128)S(1)}, u32[]{:S(2)}, u32[]{:S(2)}) collective-permute-start(f32[48,8,128]{2,1,0:T(8,128)S(1)} %get-tuple-element.20), channel_id=1, source_target_pairs={{1,0},{2,1},{3,2},{4,3},{5,4},{6,5},{7,6},{0,7},{9,8},{10,9},{11,1... | collective-permute-start | bytes 589832 | tf_op jit(solution)/shard_map/ppermute | solution.py:356
  38.6 5.8 %collective-permute-done.before = f32[48,8,128]{2,1,0:T(8,128)S(1)} collective-permute-done((f32[48,8,128]{2,1,0:T(8,128)S(1)}, f32[48,8,128]{2,1,0:T(8,128)S(1)}, u32[]{:S(2)}, u32[]{:S(2)}) %collective-permute-start) | collective-permute-done | bytes 196640 | tf_op jit(solution)/shard_map/ppermute | solution.py:355
  44.4 1.8 %collective-permute-done.1.after = f32[48,8,128]{2,1,0:T(8,128)S(1)} collective-permute-done((f32[48,8,128]{2,1,0:T(8,128)S(1)}, f32[48,8,128]{2,1,0:T(8,128)S(1)}, u32[]{:S(2)}, u32[]{:S(2)}) %collective-permute-start.1) | collective-permute-done | bytes 196640 | tf_op jit(solution)/shard_map/ppermute | solution.py:356
  46.2 0.0 all-to-all-done.fields
  46.2 0.0 copy-start
  46.2 1.3 %copy-done = f32[96,40,128]{2,1,0:T(8,128)} copy-done((f32[96,40,128]{2,1,0:T(8,128)}, f32[96,40,128]{2,1,0:T(8,128)S(1)}, u32[]{:S(2)}) %copy-start) | copy-done | bytes 1966104
  47.5 0.0 copy-start.1
  47.5 1.5 %copy-done.1 = f32[96,40,128]{2,1,0:T(8,128)S(1)} copy-done((f32[96,40,128]{2,1,0:T(8,128)S(1)}, f32[96,40,128]{2,1,0:T(8,128)}, u32[]{:S(2)}) %copy-start.1) | copy-done | bytes 1966104
  49.0 0.0 copy-start.3
  49.0 1.1 copy-done.3
  50.1 0.0 copy-start.5
  50.1 1.1 copy-done.5
  51.3 1.0 first_brick.1
  52.3 0.0 collective-permute-start.2
  52.3 5.4 %collective-permute-start.3 = (f32[10,40,128]{2,1,0:T(8,128)}, f32[10,40,128]{2,1,0:T(8,128)S(1)}, u32[]{:S(2)}, u32[]{:S(2)}) collective-permute-start(f32[10,40,128]{2,1,0:T(8,128)} %get-tuple-element.25), channel_id=1, source_target_pairs={{8,0},{16,8},{24,16},{32,24},{40,32},{48,40},{56,48},{64,56},{72,6... | collective-permute-start | bytes 614408 | tf_op jit(solution)/shard_map/ppermute | solution.py:356
  57.6 0.1 add_convert_fusion.place
  57.7 7.2 %interior.2.inner = f32[48,40,128]{2,1,0:T(8,128)S(1)} custom-call(f32[48,40,128]{2,1,0:T(8,128)S(1)} %get-tuple-element.21.te, f32[48,40,128]{2,1,0:T(8,128)S(1)} %get-tuple-element.22.heat, f32[48,40,128]{2,1,0:T(8,128)S(1)} %get-tuple-element.23.load), custom_call_target="tpu_custom_call" | custom-call | bytes 25000000 | tf_op jit(solution)/shard_map/interior/pallas_call | solution.py:89
  64.9 0.0 collective-permute-done.2.te_lo.lo
  65.0 0.0 collective-permute-done.3.te_hi.hi
  65.0 3.0 %bands.2 = (f32[48,32,128]{2,1,0:T(8,128)S(1)}, f32[24,8,128]{2,1,0:T(8,128)S(1)}, f32[24,8,128]{2,1,0:T(8,128)S(1)}) custom-call(s32[2]{0:T(128)S(1)} %add_convert_fusion.place, f32[48,40,128]{2,1,0:T(8,128)S(1)} %get-tuple-element.21.te, f32[48,40,128]{2,1,0:T(8,128)S(1)} %get-tuple-element.22.heat, f32[48,40,128]{2,1,0:T(8,128)S(1)} %get-tuple-element.23.load, ...), custom_call_target="tpu_custom_call" | custom-call | bytes 8000000 | tf_op jit(solution)/shard_map/bands/pallas_call | solution.py:158
  68.0 1.5 %collective-permute-start.4 = (f32[24,8,128]{2,1,0:T(8,128)S(1)}, f32[24,8,128]{2,1,0:T(8,128)S(1)}, u32[]{:S(2)}, u32[]{:S(2)}) collective-permute-start(f32[24,8,128]{2,1,0:T(8,128)S(1)} %get-tuple-element.27), channel_id=1, source_target_pairs={{0,1},{1,2},{2,3},{3,4},{4,5},{5,6},{6,7},{7,0},{8,9},{9,10},{10,1... | collective-permute-start | bytes 294920 | tf_op jit(solution)/shard_map/ppermute | solution.py:355
  69.5 2.7 %collective-permute-start.5 = (f32[24,8,128]{2,1,0:T(8,128)S(1)}, f32[24,8,128]{2,1,0:T(8,128)S(1)}, u32[]{:S(2)}, u32[]{:S(2)}) collective-permute-start(f32[24,8,128]{2,1,0:T(8,128)S(1)} %get-tuple-element.28), channel_id=1, source_target_pairs={{1,0},{2,1},{3,2},{4,3},{5,4},{6,5},{7,6},{0,7},{9,8},{10,9},{11,1... | collective-permute-start | bytes 294920 | tf_op jit(solution)/shard_map/ppermute | solution.py:356
  72.2 2.6 %collective-permute-done.4.before = f32[24,8,128]{2,1,0:T(8,128)S(1)} collective-permute-done((f32[24,8,128]{2,1,0:T(8,128)S(1)}, f32[24,8,128]{2,1,0:T(8,128)S(1)}, u32[]{:S(2)}, u32[]{:S(2)}) %collective-permute-start.4) | collective-permute-done | bytes 98336 | tf_op jit(solution)/shard_map/ppermute | solution.py:355
  74.8 0.0 collective-permute-done.5.after
  74.8 0.1 second_brick.1
  74.9 0.1 collective-permute-start.6
  75.0 5.3 %collective-permute-start.7 = (f32[4,40,128]{2,1,0:T(8,128)S(1)}, f32[4,40,128]{2,1,0:T(8,128)S(1)}, u32[]{:S(2)}, u32[]{:S(2)}) collective-permute-start(f32[4,40,128]{2,1,0:T(8,128)S(1)} %get-tuple-element.31), channel_id=1, source_target_pairs={{8,0},{16,8},{24,16},{32,24},{40,32},{48,40},{56,48},{64,56},{72,6... | collective-permute-start | bytes 245768 | tf_op jit(solution)/shard_map/ppermute | solution.py:356
  80.3 7.2 %interior.3.inner = f32[48,40,128]{2,1,0:T(8,128)S(1)} custom-call(f32[48,40,128]{2,1,0:T(8,128)S(1)} %get-tuple-element.29.te, f32[48,40,128]{2,1,0:T(8,128)S(1)} %get-tuple-element.22.heat, f32[48,40,128]{2,1,0:T(8,128)S(1)} %get-tuple-element.23.load), custom_call_target="tpu_custom_call" | custom-call | bytes 25000000 | tf_op jit(solution)/shard_map/interior/pallas_call | solution.py:89
  87.5 0.0 copy-start.7
  87.5 0.0 copy-start.9
  87.5 0.0 copy-start.11
  87.6 0.0 collective-permute-done.6.te_lo
  87.6 0.0 collective-permute-done.7.te_hi
  87.6 3.8 %bands.3 = f32[48,32,128]{2,1,0:T(8,128)} custom-call(s32[2]{0:T(128)S(1)} %add_convert_fusion.place, f32[48,40,128]{2,1,0:T(8,128)S(1)} %get-tuple-element.29.te, f32[48,40,128]{2,1,0:T(8,128)S(1)} %get-tuple-element.22.heat, f32[48,40,128]{2,1,0:T(8,128)S(1)} %get-tuple-element.23.load, f32[4,40,128]{2,1,0:T(8,128)S(1)} %collective-permute-done.6.te_lo, ...), custom_call_target="tpu_custom_call" | custom-call | bytes 8000000 | tf_op jit(solution)/shard_map/bands/pallas_call | solution.py:158
  91.4 5.4 %all-to-all-start.1 = ((f32[48,32,128]{2,1,0:T(8,128)}), f32[48,32,128]{2,1,0:T(8,128)S(1)}, u32[]{:S(2)}, u32[]{:S(2)}) async-start(f32[48,32,128]{2,1,0:T(8,128)} %bands.3), calls=%async_computation.1 | async-start | bytes 1572864 | tf_op jit(solution)/shard_map/all_to_all | solution.py:361
  96.8 0.0 copy-done.7
  96.8 0.0 copy-done.9
  96.8 0.0 copy-done.11
  96.9 17.2 %read_atoms.1 = f32[3,1,16384]{2,1,0:T(1,128)} custom-call(s32[1,1]{1,0:T(1,128)S(6)} %copy.15.count, f32[1536,128]{1,0:T(8,128)} %bitcast.13.te, s32[1,16384]{1,0:T(1,128)S(1)} %bitcast.25, s32[1,16384]{1,0:T(1,128)S(1)} %bitcast.27, f32[3,1,16384]{2,1,0:T(1,128)S(1)} %bitcast.22, f32[3,1,16384]{2,1,0:T(1,128)S(1)} %bitcast.23), custom_call_target="tpu_custom_call" | custom-call | flops 12884901888 | bytes 4000000 | tf_op jit(solution)/shard_map/read_atoms/pallas_call | solution.py:323
  114.0 0.0 all-to-all-done.1
  114.0 0.9 copy.11
  (2 shorter events, 0.0 us)
Async XLA Ops:
  4.0 6.7 %copy-start.6 = (f32[3,1,1,16384]{3,2,1,0:T(1,128)S(1)}, f32[3,1,1,16384]{3,2,1,0:T(1,128)}, u32[]{:S(2)}) copy-start(f32[3,1,1,16384]{3,2,1,0:T(1,128)} %param.9) | copy-start | bytes 589828
  4.0 6.7 %copy-start.8 = (s32[1,1,16384]{2,1,0:T(1,128)S(1)}, s32[1,1,16384]{2,1,0:T(1,128)}, u32[]{:S(2)}) copy-start(s32[1,1,16384]{2,1,0:T(1,128)} %param.11) | copy-start | bytes 196612
  4.0 6.8 %copy-start.10 = (s32[1,1,16384]{2,1,0:T(1,128)S(1)}, s32[1,1,16384]{2,1,0:T(1,128)}, u32[]{:S(2)}) copy-start(s32[1,1,16384]{2,1,0:T(1,128)} %param.12) | copy-start | bytes 196612
  4.0 42.2 %all-to-all-start = ((f32[96,40,128]{2,1,0:T(8,128)}), f32[96,40,128]{2,1,0:T(8,128)S(1)}, u32[]{:S(2)}, u32[]{:S(2)}) async-start(f32[96,40,128]{2,1,0:T(8,128)} %bitcast.28), calls=%async_computation | async-start | bytes 3932160 | tf_op jit(solution)/shard_map/all_to_all | solution.py:361
  32.7 0.9 copy-start.2
  33.5 0.9 copy-start.4
  34.4 9.9 %collective-permute-start = (f32[48,8,128]{2,1,0:T(8,128)S(1)}, f32[48,8,128]{2,1,0:T(8,128)S(1)}, u32[]{:S(2)}, u32[]{:S(2)}) collective-permute-start(f32[48,8,128]{2,1,0:T(8,128)S(1)} %get-tuple-element.19), channel_id=1, source_target_pairs={{0,1},{1,2},{2,3},{3,4},{4,5},{5,6},{6,7},{7,0},{8,9},{9,10},{10,1... | collective-permute-start | bytes 589832 | tf_op jit(solution)/shard_map/ppermute | solution.py:355
  36.4 9.7 %collective-permute-start.1 = (f32[48,8,128]{2,1,0:T(8,128)S(1)}, f32[48,8,128]{2,1,0:T(8,128)S(1)}, u32[]{:S(2)}, u32[]{:S(2)}) collective-permute-start(f32[48,8,128]{2,1,0:T(8,128)S(1)} %get-tuple-element.20), channel_id=1, source_target_pairs={{1,0},{2,1},{3,2},{4,3},{5,4},{6,5},{7,6},{0,7},{9,8},{10,9},{11,1... | collective-permute-start | bytes 589832 | tf_op jit(solution)/shard_map/ppermute | solution.py:356
  46.2 1.3 %copy-start = (f32[96,40,128]{2,1,0:T(8,128)}, f32[96,40,128]{2,1,0:T(8,128)S(1)}, u32[]{:S(2)}) copy-start(f32[96,40,128]{2,1,0:T(8,128)S(1)} %all-to-all-done.fields) | copy-start | bytes 5898244
  47.5 1.5 %copy-start.1 = (f32[96,40,128]{2,1,0:T(8,128)S(1)}, f32[96,40,128]{2,1,0:T(8,128)}, u32[]{:S(2)}) copy-start(f32[96,40,128]{2,1,0:T(8,128)} %copy-done) | copy-start | bytes 5898244
  49.0 1.1 copy-start.3
  50.1 1.1 copy-start.5
  52.3 12.7 %collective-permute-start.2 = (f32[10,40,128]{2,1,0:T(8,128)}, f32[10,40,128]{2,1,0:T(8,128)S(1)}, u32[]{:S(2)}, u32[]{:S(2)}) collective-permute-start(f32[10,40,128]{2,1,0:T(8,128)} %get-tuple-element.24), channel_id=1, source_target_pairs={{0,8},{8,16},{16,24},{24,32},{32,40},{40,48},{48,56},{56,64},{64,7... | collective-permute-start | bytes 614408 | tf_op jit(solution)/shard_map/ppermute | solution.py:355
  52.3 12.7 %collective-permute-start.3 = (f32[10,40,128]{2,1,0:T(8,128)}, f32[10,40,128]{2,1,0:T(8,128)S(1)}, u32[]{:S(2)}, u32[]{:S(2)}) collective-permute-start(f32[10,40,128]{2,1,0:T(8,128)} %get-tuple-element.25), channel_id=1, source_target_pairs={{8,0},{16,8},{24,16},{32,24},{40,32},{48,40},{56,48},{64,56},{72,6... | collective-permute-start | bytes 614408 | tf_op jit(solution)/shard_map/ppermute | solution.py:356
  68.0 6.8 %collective-permute-start.4 = (f32[24,8,128]{2,1,0:T(8,128)S(1)}, f32[24,8,128]{2,1,0:T(8,128)S(1)}, u32[]{:S(2)}, u32[]{:S(2)}) collective-permute-start(f32[24,8,128]{2,1,0:T(8,128)S(1)} %get-tuple-element.27), channel_id=1, source_target_pairs={{0,1},{1,2},{2,3},{3,4},{4,5},{5,6},{6,7},{7,0},{8,9},{9,10},{10,1... | collective-permute-start | bytes 294920 | tf_op jit(solution)/shard_map/ppermute | solution.py:355
  69.5 5.3 %collective-permute-start.5 = (f32[24,8,128]{2,1,0:T(8,128)S(1)}, f32[24,8,128]{2,1,0:T(8,128)S(1)}, u32[]{:S(2)}, u32[]{:S(2)}) collective-permute-start(f32[24,8,128]{2,1,0:T(8,128)S(1)} %get-tuple-element.28), channel_id=1, source_target_pairs={{1,0},{2,1},{3,2},{4,3},{5,4},{6,5},{7,6},{0,7},{9,8},{10,9},{11,1... | collective-permute-start | bytes 294920 | tf_op jit(solution)/shard_map/ppermute | solution.py:356
  74.9 12.7 %collective-permute-start.6 = (f32[4,40,128]{2,1,0:T(8,128)S(1)}, f32[4,40,128]{2,1,0:T(8,128)S(1)}, u32[]{:S(2)}, u32[]{:S(2)}) collective-permute-start(f32[4,40,128]{2,1,0:T(8,128)S(1)} %get-tuple-element.30), channel_id=1, source_target_pairs={{0,8},{8,16},{16,24},{24,32},{32,40},{40,48},{48,56},{56,64},{64,7... | collective-permute-start | bytes 245768 | tf_op jit(solution)/shard_map/ppermute | solution.py:355
  75.0 12.6 %collective-permute-start.7 = (f32[4,40,128]{2,1,0:T(8,128)S(1)}, f32[4,40,128]{2,1,0:T(8,128)S(1)}, u32[]{:S(2)}, u32[]{:S(2)}) collective-permute-start(f32[4,40,128]{2,1,0:T(8,128)S(1)} %get-tuple-element.31), channel_id=1, source_target_pairs={{8,0},{16,8},{24,16},{32,24},{40,32},{48,40},{56,48},{64,56},{72,6... | collective-permute-start | bytes 245768 | tf_op jit(solution)/shard_map/ppermute | solution.py:356
  87.5 9.3 %copy-start.7 = (f32[3,1,1,16384]{3,2,1,0:T(1,128)S(1)}, f32[3,1,1,16384]{3,2,1,0:T(1,128)}, u32[]{:S(2)}) copy-start(f32[3,1,1,16384]{3,2,1,0:T(1,128)} %param.10) | copy-start | bytes 589828
  87.5 9.3 %copy-start.9 = (s32[1,1,16384]{2,1,0:T(1,128)S(1)}, s32[1,1,16384]{2,1,0:T(1,128)}, u32[]{:S(2)}) copy-start(s32[1,1,16384]{2,1,0:T(1,128)} %param.11) | copy-start | bytes 196612
  87.5 9.3 %copy-start.11 = (s32[1,1,16384]{2,1,0:T(1,128)S(1)}, s32[1,1,16384]{2,1,0:T(1,128)}, u32[]{:S(2)}) copy-start(s32[1,1,16384]{2,1,0:T(1,128)} %param.12) | copy-start | bytes 196612
  91.4 22.6 %all-to-all-start.1 = ((f32[48,32,128]{2,1,0:T(8,128)}), f32[48,32,128]{2,1,0:T(8,128)S(1)}, u32[]{:S(2)}, u32[]{:S(2)}) async-start(f32[48,32,128]{2,1,0:T(8,128)} %bands.3), calls=%async_computation.1 | async-start | bytes 1572864 | tf_op jit(solution)/shard_map/all_to_all | solution.py:361
where the time goes:
time: 116 us; the launch traced here: 115 us
  Pallas kernels  61.5 us (53%)
  starting transfers between devices  30.6 us (26%)
  waiting for transfers between devices  10.2 us (9%)
  local copies, waits for them, and re-layouts  9.68 us (8%)
  other arithmetic  1.53 us (1%)
  between operations  1.48 us (1%)
    pallas_call x1, Pallas kernels, bin_atoms(): pl.pallas_call(functools.partial(bin_kernel, block), grid=(slots // block...  21.9 us
    pallas_call x1, Pallas kernels, read_atoms(): pl.pallas_call(functools.partial(read_kernel, block), grid=(slots // bloc...  17.2 us
    ppermute x4, starting transfers between devices, to_both_sides(): lax.ppermute(head, axis, [((i + 1) % count, i) for i in range(count)])  15.5 us
    pallas_call x2, Pallas kernels, interior(): pl.pallas_call(interior_kernel, out_shape=f32(CX, ROWS, NZ), in_specs=[VM...  14.4 us
    all_to_all x2, starting transfers between devices, exchanged(): return lax.all_to_all(blocks, 'gy', split_axis=0, concat_axis=0, tiled=True)  11.5 us
    ppermute x4, waiting for transfers between devices, to_both_sides(): lax.ppermute(tail, axis, [(i, (i + 1) % count) for i in range(count)])  8.39 us
    unnamed x24, local copies, waits for them, and re-layouts  6.89 us
    pallas_call x2, Pallas kernels, bands(): pl.pallas_call(functools.partial(bands_kernel, last), out_shape=shapes, i...  6.86 us
  transfers between devices with their start and end apart: 10, of which 3 were waited for; matrix products, arithmetic and copies ran while one was open for 0% of the time, Pallas kernels for 47%

commit v1 on v0

--- a/solution.py
+++ b/solution.py
@@ -19,11 +19,12 @@
 ROWS = CY + 2 * HALO
 COLS = CX * CY
 GROUP = 6
-BLOCK = 2048
+BLOCK = 4096
 MIB = 1024 * 1024
 
 VMEM = pl.BlockSpec(memory_space=pltpu.VMEM)
 SMEM = pl.BlockSpec(memory_space=pltpu.SMEM)
+ANY = pl.BlockSpec(memory_space=pl.ANY)
 
 
 def params(mib):
@@ -55,7 +56,7 @@
     return c, lax.rsqrt(c)
 
 
-def interior_kernel(te, heat, load, out, first, second):
+def interior_steps(first, second, heat, load, out):
     def step(source, target, shift):
         below_u = source[0]
         _, below_r = with_root(below_u)
@@ -75,27 +76,87 @@
 
         lax.fori_loop(0, CX // GROUP, turn, (u, c, r, flux(below_u, below_r, u, r)))
 
-    first[pl.ds(1, CX)] = te[...]
     for buffer in (first, second):
-        buffer[0] = te[0]
-        buffer[CX + 1] = te[CX - 1]
+        buffer[0] = first[1]
+        buffer[CX + 1] = first[CX]
     step(first, second, 1)
     step(second, first, 1)
     step(first, second, 1)
     step(second, out, 0)
 
 
-def interior(te, heat, load):
-    return pl.pallas_call(
-        interior_kernel,
+def padded_brick():
+    return pltpu.VMEM((CX + 2, ROWS, NZ), jnp.float32)
+
+
+def second_interior_kernel(te, heat, load, out, first, second):
+    first[pl.ds(1, CX)] = te[...]
+    interior_steps(first, second, heat, load, out)
+
+
+def second_interior(te, heat, load):
+    return pl.pallas_call(
+        second_interior_kernel,
         out_shape=f32(CX, ROWS, NZ),
         in_specs=[VMEM] * 3,
         out_specs=VMEM,
-        scratch_shapes=[pltpu.VMEM((CX + 2, ROWS, NZ), jnp.float32)] * 2,
+        scratch_shapes=[padded_brick()] * 2,
         compiler_params=params(32),
         cost_estimate=pl.CostEstimate(flops=0, bytes_accessed=25_000_000, transcendentals=0),
         name="interior",
     )(te, heat, load)
+
+
+def first_interior_kernel(
+    parts, own_head, own_tail, load_in, kinetic, before, after, fields, out, heat, load, *scratch
+):
+    first, second, source, sems = scratch
+    layers = CX // parts
+    fetches = []
+    for j in range(parts):
+        at = 2 * j * layers
+        te_here = first.at[pl.ds(1 + j * layers, layers)]
+        source_here = source.at[pl.ds(j * layers, layers)]
+        for k, here in enumerate((te_here, source_here)):
+            there = fields.at[pl.ds(at + k * layers, layers)]
+            fetches.append(pltpu.make_async_copy(there, here, sems.at[2 * j + k]))
+    for fetch in fetches:
+        fetch.start()
+    for i in range(parts):
+        span = pl.ds(i * layers, layers)
+        load[span] = side_by_side(own_head, load_in, own_tail, after, before, span, 0)
+    for fetch in fetches:
+        fetch.wait()
+    for i in range(parts):
+        span = pl.ds(i * layers, layers)
+        heat[span] = source[span] + side_by_side(
+            own_head, kinetic, own_tail, after, before, span, HALO
+        )
+    interior_steps(first, second, heat, load, out)
+
+
+def side_by_side(own_head, inner, own_tail, after, before, span, row):
+    rows = slice(row, row + HALO)
+    return jnp.concatenate(
+        [own_head[span, rows], inner[span], own_tail[span, rows], after[span, rows], before[span, rows]],
+        1,
+    )
+
+
+def first_interior(parts, *arrays):
+    whole = f32(CX, ROWS, NZ)
+    return pl.pallas_call(
+        functools.partial(first_interior_kernel, parts),
+        out_shape=[whole] * 3,
+        in_specs=[VMEM] * 6 + [ANY],
+        out_specs=[VMEM] * 3,
+        scratch_shapes=[padded_brick()] * 2
+        + [pltpu.VMEM((CX, ROWS, NZ), jnp.float32)]
+        + [pltpu.SemaphoreType.DMA((2 * parts,))],
+        compiler_params=params(32),
+        cost_estimate=pl.CostEstimate(flops=0, bytes_accessed=30_000_000, transcendentals=0),
+        name="first_interior",
+    )(*arrays)
 
 
 def band_steps(us, heats, loads, closed_face, closed):
@@ -133,7 +194,7 @@
         place[0] == 1,
     )
     high = band_steps(
-        [te[CX - many + i] for i in range(many)] + [te_hi[i] for i in range(HALO)],
+        [te[te.shape[0] - many + i] for i in range(many)] + [te_hi[i] for i in range(HALO)],
         [heat[CX - near + i] for i in range(near)] + [hi[HALO + i] for i in range(NEAR)],
         [load[CX - near + i] for i in range(near)] + [hi[HALO + NEAR + i] for i in range(NEAR)],
         many - 1,
@@ -166,37 +227,113 @@
     )(place, te, heat, load, te_lo, te_hi, lo, hi, inner)
 
 
-def first_kernel(parts, fields, load_in, kinetic, before, after, te, heat, load, head, tail):
+def edges_kernel(parts, *refs):
+    inside, (fields, ends, head, tail, here, source, sems) = refs[:6], refs[6:]
     layers = CX // parts
-    for j in range(parts):
-        te[pl.ds(j * layers, layers)] = fields[pl.ds(2 * j * layers, layers)]
-        span = pl.ds(j * layers, layers)
-        source = pl.ds((2 * j + 1) * layers, layers)
-        heat[span, :CY] = fields[source, :CY] + kinetic[span]
-        heat[span, CY:] = fields[source, CY:] + jnp.concatenate(
-            [after[span, HALO:], before[span, HALO:]], 1
+    many = 2 * HALO
+    fetches = []
+
+    def fetch(there, here):
+        copy = pltpu.make_async_copy(there, here, sems.at[len(fetches)])
+        copy.start()
+        fetches.append(copy)
+
+    for k, first in enumerate((0, CX - many)):
+        layer = first
+        while layer < first + many:
+            part = layer // layers
+            count = min(first + many, (part + 1) * layers) - layer
+            there = fields.at[pl.ds(layer + part * layers, count)]
+            fetch(there, here.at[pl.ds(k * many + layer - first, count)])
+            layer += count
+    for k, first in enumerate((0, CX - NEAR)):
+        layer = first
+        while layer < first + NEAR:
+            part = layer // layers
+            count = min(first + NEAR, (part + 1) * layers) - layer
+            there = fields.at[pl.ds(layer + (part + 1) * layers, count)]
+            fetch(there, source.at[k, pl.ds(layer - first, count)])
+            layer += count
+    for copy in fetches:
+        copy.wait()
+    ends[...] = here[...]
+    for k, (target, at) in enumerate(((head, 0), (tail, 2 * many - HALO))):
+        own_head, own_tail, load_in, kinetic, before, after = inside
+        span = pl.ds((0, CX - NEAR)[k], NEAR)
+        target[:HALO] = here[pl.ds(at, HALO)]
+        target[pl.ds(HALO, NEAR)] = source[k] + side_by_side(
+            own_head, kinetic, own_tail, after, before, span, HALO
         )
-        load[span, :CY] = load_in[span]
-        load[span, CY:] = jnp.concatenate([after[span, :HALO], before[span, :HALO]], 1)
-    head[:HALO] = te[:HALO]
-    tail[:HALO] = te[CX - HALO :]
-    for place, field in ((HALO, heat), (HALO + NEAR, load)):
-        head[pl.ds(place, NEAR)] = field[:NEAR]
-        tail[pl.ds(place, NEAR)] = field[CX - NEAR :]
-
-
-def first_brick(parts, fields, load, kinetic, before, after):
-    whole = f32(CX, ROWS, NZ)
+        target[pl.ds(HALO + NEAR, NEAR)] = side_by_side(
+            own_head, load_in, own_tail, after, before, span, 0
+        )
+
+
+def edges(parts, *arrays):
     edge = f32(HALO + 2 * NEAR, ROWS, NZ)
-    return pl.pallas_call(
-        functools.partial(first_kernel, parts),
-        out_shape=[whole, whole, whole, edge, edge],
-        in_specs=[VMEM] * 5,
-        out_specs=[VMEM] * 5,
+    ends = (4 * HALO, ROWS, NZ)
+    return pl.pallas_call(
+        functools.partial(edges_kernel, parts),
+        out_shape=[f32(*ends), edge, edge],
+        in_specs=[VMEM] * 6 + [ANY],
+        out_specs=[VMEM] * 3,
+        scratch_shapes=[
+            pltpu.VMEM(ends, jnp.float32),
+            pltpu.VMEM((2, NEAR, ROWS, NZ), jnp.float32),
+            pltpu.SemaphoreType.DMA((16,)),
+        ],
         compiler_params=params(32),
+        cost_estimate=pl.CostEstimate(flops=0, bytes_accessed=2_000_000, transcendentals=0),
+        name="edges",
+    )(*arrays)
+
+
+def widen_kernel(parts, te, source, out, here, halo, in_sems, out_sems):
+    layers = te.shape[0]
+    fetches = [
+        pltpu.make_async_copy(field, here.at[f], in_sems.at[f])
+        for f, field in enumerate((te, source))
+    ]
+    for fetch in fetches:
+        fetch.start()
+    sends = []
+    for f in range(2):
+        fetches[f].wait()
+        span = pl.ds(f * layers, layers)
+        for j in range(parts):
+            after = (j + 1) % parts * CY
+            before = (j - 1) % parts * CY + CY - HALO
+            halo[j, span] = jnp.concatenate(
+                [here[f, :, pl.ds(after, HALO)], here[f, :, pl.ds(before, HALO)]], 1
+            )
+            own = here.at[f, :, pl.ds(j * CY, CY)]
+            for k, (piece, rows) in enumerate(
+                ((own, pl.ds(0, CY)), (halo.at[j, span], pl.ds(CY, 2 * HALO)))
+            ):
+                send = pltpu.make_async_copy(piece, out.at[j, span, rows], out_sems.at[f, j, k])
+                send.start()
+                sends.append(send)
+    for send in sends:
+        send.wait()
+
+
+def widened(te, source, parts):
+    layers = te.shape[0]
+    return pl.pallas_call(
+        functools.partial(widen_kernel, parts),
+        out_shape=f32(parts, 2 * layers, ROWS, NZ),
+        in_specs=[ANY] * 2,
+        out_specs=ANY,
+        scratch_shapes=[
+            pltpu.VMEM((2,) + te.shape, jnp.float32),
+            pltpu.VMEM((parts, 2 * layers, 2 * HALO, NZ), jnp.float32),
+            pltpu.SemaphoreType.DMA((2,)),
+            pltpu.SemaphoreType.DMA((2, parts, 2)),
+        ],
+        compiler_params=params(63),
         cost_estimate=pl.CostEstimate(flops=0, bytes_accessed=4_000_000, transcendentals=0),
-        name="first_brick",
-    )(fields, load, kinetic, before, after)
+        name="widen",
+    )(te, source)
 
 
 def second_kernel(middle, before, after, te, head, tail):
@@ -221,10 +358,25 @@
     )(middle, before, after)
 
 
-def column_hot(column):
-    ids = lax.broadcasted_iota(jnp.int16, (COLS, column.shape[1]), 0)
+INNER = CY - 2 * HALO
+
+
+def column_hot(column, columns):
+    ids = lax.broadcasted_iota(jnp.int16, (columns, column.shape[1]), 0)
     hot = ids == column.astype(jnp.int16)
     return jnp.where(hot, jnp.bfloat16(1), jnp.bfloat16(0))
+
+
+def face_column(column):
+    layer, row = column // CY, column % CY
+    side = jnp.where(row < HALO, row, jnp.where(row >= CY - HALO, row - INNER, -1))
+    return jnp.where(side < 0, -1, layer * 2 * HALO + side)
+
+
+def inner_column(column):
+    layer, row = column // CY, column % CY
+    inside = (row >= HALO) & (row < CY - HALO)
+    return jnp.where(inside, layer * INNER + row - HALO, -1)
 
 
 def lane_mask(lane):
@@ -236,7 +388,7 @@
     return jnp.where(slot < count[0, 0], 1.0, 0.0)
 
 
-def bin_kernel(block, count, column, lane, velocities, load, kinetic, head, tail, sums):
+def bin_kernel(block, faces, count, column, lane, velocities, first, second, sums):
     @pl.when(pl.program_id(0) == 0)
     def _():
         sums[...] = jnp.zeros_like(sums)
@@ -244,14 +396,18 @@
     living = living_of(count, block)
     moving = velocities[...]
     energy = living * (moving[0] * moving[0] + moving[1] * moving[1] + moving[2] * moving[2]) / 3.0
-    mask = lane_mask(lane[...])
-    spread = jnp.where(mask, energy, 0.0)
-    high = spread.astype(jnp.bfloat16)
-    low = (spread - high.astype(jnp.float32)).astype(jnp.bfloat16)
-    weighted = jnp.concatenate([jnp.where(mask, living, 0.0).astype(jnp.bfloat16), high, low], 0)
+    lanes = lax.broadcasted_iota(jnp.int16, (NZ, block), 0)
+    mask = lanes == lane[...].astype(jnp.int16)
+    high = energy.astype(jnp.bfloat16)
+    low = (energy - high.astype(jnp.float32)).astype(jnp.bfloat16)
+    weighted = jnp.concatenate(
+        [jnp.where(mask, w, jnp.bfloat16(0)) for w in (living.astype(jnp.bfloat16), high, low)], 0
+    )
+    columns = sums.shape[1]
+    place = face_column(column[...]) if faces else inner_column(column[...])
     term = lax.dot_general(
         weighted,
-        column_hot(column[...]),
+        column_hot(place, columns),
         (((1,), (1,)), ((), ())),
         preferred_element_type=jnp.float32,
     )
@@ -260,18 +416,20 @@
 
     @pl.when(pl.program_id(0) == pl.num_programs(0) - 1)
     def _():
-        layers = NZ // CY
-        for j in range(COLS // NZ):
-            part = pl.ds(j * NZ, NZ)
-            span = pl.ds(j * layers, layers)
-            tally = sums[:NZ, part]
-            heat = sums[NZ:, part]
-            load[span] = (COUPLING * tally.T).reshape(layers, CY, NZ)
-            kinetic[span] = (COUPLING * heat.T).reshape(layers, CY, NZ)
-        head[:, :HALO] = load[:, :HALO]
-        head[:, HALO:] = kinetic[:, :HALO]
-        tail[:, :HALO] = load[:, CY - HALO :]
-        tail[:, HALO:] = kinetic[:, CY - HALO :]
+        rows = columns // CX
+        layers = NZ // (2 * HALO)
+        for layer in range(0, CX, layers):
+            part = pl.ds(layer * rows, layers * rows)
+            span = pl.ds(layer, layers)
+            load = (COUPLING * sums[:NZ, part].T).reshape(layers, rows, NZ)
+            kinetic = (COUPLING * sums[NZ:, part].T).reshape(layers, rows, NZ)
+            if faces:
+                for target, side in ((first, slice(0, HALO)), (second, slice(HALO, 2 * HALO))):
+                    target[span, :HALO] = load[:, side]
+                    target[span, HALO:] = kinetic[:, side]
+            else:
+                first[span] = load
+                second[span] = kinetic
 
 
 def blocks_of(shape, block):
@@ -282,23 +440,23 @@
     return pl.BlockSpec(shape, lambda i: (0,) * len(shape))
 
 
-def bin_atoms(count, column, lane, velocities):
+def bin_atoms(faces, count, column, lane, velocities):
     slots = column.shape[1]
     block = min(BLOCK, slots)
-    brick = (CX, CY, NZ)
-    face = (CX, 2 * HALO, NZ)
-    return pl.pallas_call(
-        functools.partial(bin_kernel, block),
+    rows = 2 * HALO if faces else INNER
+    result = (CX, rows, NZ)
+    return pl.pallas_call(
+        functools.partial(bin_kernel, block, faces),
         grid=(slots // block,),
-        out_shape=[f32(*brick), f32(*brick), f32(*face), f32(*face)],
+        out_shape=[f32(*result)] * 2,
         in_specs=[SMEM, blocks_of((1,), block), blocks_of((1,), block), blocks_of((3, 1), block)],
-        out_specs=[whole_of(*brick), whole_of(*brick), whole_of(*face), whole_of(*face)],
-        scratch_shapes=[pltpu.VMEM((2 * NZ, COLS), jnp.float32)],
-        compiler_params=params(48),
+        out_specs=[whole_of(*result)] * 2,
+        scratch_shapes=[pltpu.VMEM((2 * NZ, CX * rows), jnp.float32)],
+        compiler_params=params(63 if faces else 48),
         cost_estimate=pl.CostEstimate(
-            flops=6 * slots * COLS * NZ, bytes_accessed=4_000_000, transcendentals=0
+            flops=6 * slots * CX * rows * NZ, bytes_accessed=4_000_000, transcendentals=0
         ),
-        name="bin_atoms",
+        name="bin_faces" if faces else "bin_inner",
     )(count, column, lane, velocities)
 
 
@@ -310,7 +468,7 @@
         pair[:NZ] = high
         pair[NZ:] = (table - high.astype(jnp.float32)).astype(jnp.bfloat16)
 
-    rows = jnp.dot(pair[...], column_hot(column[...]), preferred_element_type=jnp.float32)
+    rows = jnp.dot(pair[...], column_hot(column[...], COLS), preferred_element_type=jnp.float32)
     picked = jnp.where(lane_mask(lane[...]), rows[:NZ] + rows[NZ:], 0.0)
     te_atom = jnp.sum(picked, axis=0, keepdims=True)
     drive = jnp.sqrt(2.0 * FRICTION * te_atom)
@@ -342,14 +500,6 @@
     )(count, te, column, lane, velocities, noise)
 
 
-def widened(field, parts):
-    layers = field.shape[0]
-    blocks = field.reshape(layers, parts, CY, NZ).transpose(1, 0, 2, 3)
-    after = jnp.roll(blocks, -1, 0)[:, :, :HALO]
-    before = jnp.roll(blocks, 1, 0)[:, :, CY - HALO :]
-    return jnp.concatenate([blocks, after, before], 2)
-
-
 def to_both_sides(head, tail, axis):
     count = lax.axis_size(axis)
     from_before = lax.ppermute(tail, axis, [(i, (i + 1) % count) for i in range(count)])
@@ -364,27 +514,29 @@
 def on_device(te_init, source, velocities, noise, cell_index, cell_lane, brick_atoms):
     parts = lax.axis_size("gy")
     layers = te_init.shape[0]
-    fields = jnp.concatenate([widened(te_init, parts), widened(source, parts)], 1)
+    fields = widened(te_init, source, parts)
     fields = exchanged(fields.reshape(2 * parts * layers, ROWS, NZ))
 
     column = cell_index[0]
     lane = cell_lane[0]
     moving = velocities[:, 0]
-    load, kinetic, head, tail = bin_atoms(brick_atoms, column, lane, moving)
-    before, after = to_both_sides(head, tail, "gy")
+    own_head, own_tail = bin_atoms(True, brick_atoms, column, lane, moving)
+    before, after = to_both_sides(own_head, own_tail, "gy")
+    load, kinetic = bin_atoms(False, brick_atoms, column, lane, moving)
 
     position = lax.axis_index("gx")
     final = lax.axis_size("gx") - 1
     place = jnp.stack([position == 0, position == final]).astype(jnp.int32)
-    te, heat, load, head, tail = first_brick(parts, fields, load, kinetic, before, after)
+    arrays = (own_head, own_tail, load, kinetic, before, after, fields)
+    ends, head, tail = edges(parts, *arrays)
     lo, hi = to_both_sides(head, tail, "gx")
-    inner = interior(te, heat, load)
-    middle, head, tail = bands(False, place, te, heat, load, lo, hi, lo, hi, inner)
+    inner, heat, load = first_interior(parts, *arrays)
+    middle, head, tail = bands(False, place, ends, heat, load, lo, hi, lo, hi, inner)
 
     before, after = to_both_sides(head, tail, "gy")
     te, head, tail = second_brick(middle, before, after)
     te_lo, te_hi = to_both_sides(head, tail, "gx")
-    inner = interior(te, heat, load)
+    inner = second_interior(te, heat, load)
     (te,) = bands(True, place, te, heat, load, te_lo, te_hi, lo, hi, inner)
 
     electron = exchanged(te).reshape(parts, layers, CY, NZ).transpose(1, 0, 2, 3)

time: 116 us -> 108 us (0.931)
  Pallas kernels: 61.5 us -> 70.7 us
  local copies, waits for them, and re-layouts: 9.68 us -> 0.98 us
  waiting for transfers between devices: 10.2 us -> 3.46 us
  other arithmetic: 1.53 us -> 0.07 us
    pallas_call x4 -> x6, Pallas kernels: 37.4 us -> 47.4 us  [the longest x2 27 us: bin_atoms(): pl.pallas_call(functools.partial(bin_kernel, block, faces), grid=(slots /...]
    unnamed x24 -> x12, local copies, waits for them, and re-layouts: 6.89 us -> 0.03 us
    ppermute x4, waiting for transfers between devices: 8.39 us -> 2.6 us  [to_both_sides(): lax.ppermute(tail, axis, [(i, (i + 1) % count) for i in range(count)])]
    transpose x1 -> x0, local copies, waits for them, and re-layouts: 1.49 us -> none  [widened(): blocks = field.reshape(layers, parts, CY, NZ).transpose(1, 0, 2, 3)]
    concatenate x1 -> x0, other arithmetic: 1.46 us -> none  [on_device(): jnp.concatenate([widened(te_init, parts), widened(source, parts)], 1)]
  transfers between devices with their start and end apart: 10 -> 10, of which waited for: 3 -> 2; matrix products, arithmetic and copies ran while one was open for 0% -> 0% of each run, Pallas kernels for 47% -> 56%
where the time goes in v1:
time: 108 us; the launch traced here: 107 us
  Pallas kernels  70.7 us (65%)
  starting transfers between devices  30.6 us (28%)
  waiting for transfers between devices  3.46 us (3%)
  between operations  1.44 us (1%)
    pallas_call x2, Pallas kernels, bin_atoms(): pl.pallas_call(functools.partial(bin_kernel, block, faces), grid=(slots /...  27 us
    ppermute x4, starting transfers between devices, to_both_sides(): lax.ppermute(head, axis, [((i + 1) % count, i) for i in range(count)])  16.4 us
    pallas_call x1, Pallas kernels, read_atoms(): pl.pallas_call(functools.partial(read_kernel, block), grid=(slots // bloc...  16.3 us
    all_to_all x2, starting transfers between devices, exchanged(): return lax.all_to_all(blocks, 'gy', split_axis=0, concat_axis=0, tiled=True)  11.4 us
    pallas_call x1, Pallas kernels, first_interior(): pl.pallas_call(functools.partial(first_interior_kernel, parts), out_shape...  9.12 us
    pallas_call x1, Pallas kernels, second_interior(): pl.pallas_call(second_interior_kernel, out_shape=f32(CX, ROWS, NZ), in_sp...  7.32 us
    pallas_call x2, Pallas kernels, bands(): pl.pallas_call(functools.partial(bands_kernel, last), out_shape=shapes, i...  6.96 us
    ppermute x4, starting transfers between devices, to_both_sides(): lax.ppermute(tail, axis, [(i, (i + 1) % count) for i in range(count)])  2.83 us
  transfers between devices with their start and end apart: 10, of which 2 were waited for; matrix products, arithmetic and copies ran while one was open for 0% of the time, Pallas kernels for 56%

profile of v1, /device:TPU:4, one launch (start us, length us, event | category | flops | bytes accessed | tf_op | source)
XLA Modules:
  0.0 107.2 jit_solution(4487548077630001006)
XLA Ops:
  0.6 2.7 %widen.1 = f32[8,12,40,128]{3,2,1,0:T(8,128)} custom-call(f32[6,256,128]{2,1,0:T(8,128)} %te.1, f32[6,256,128]{2,1,0:T(8,128)} %source.1), custom_call_target="tpu_custom_call" | custom-call | bytes 4000000 | tf_op jit(solution)/shard_map/widen/pallas_call | solution.py:322
  3.4 6.0 %all-to-all-start = ((f32[96,40,128]{2,1,0:T(8,128)}), f32[96,40,128]{2,1,0:T(8,128)}, u32[]{:S(2)}, u32[]{:S(2)}) async-start(f32[96,40,128]{2,1,0:T(8,128)} %bitcast.25), calls=%async_computation | async-start | bytes 3932160 | tf_op jit(solution)/shard_map/all_to_all | solution.py:511
  10.0 0.0 copy-start.2
  10.0 0.0 copy-start.4
  10.0 0.0 copy-start.5
  10.0 9.4 %bin_faces.1 = (f32[48,8,128]{2,1,0:T(8,128)}, f32[48,8,128]{2,1,0:T(8,128)}) custom-call(s32[1,1]{1,0:T(1,128)S(6)} %copy.11.count, s32[1,16384]{1,0:T(1,128)} %bitcast.19, s32[1,16384]{1,0:T(1,128)} %bitcast.22, f32[3,1,16384]{2,1,0:T(1,128)} %bitcast.15), custom_call_target="tpu_custom_call" | custom-call | flops 4831838208 | bytes 4000000 | tf_op jit(solution)/shard_map/bin_faces/pallas_call | solution.py:448
  19.4 2.0 %collective-permute-start = (f32[48,8,128]{2,1,0:T(8,128)}, f32[48,8,128]{2,1,0:T(8,128)S(1)}, u32[]{:S(2)}, u32[]{:S(2)}) collective-permute-start(f32[48,8,128]{2,1,0:T(8,128)} %get-tuple-element.19.refs_1_.own_tail), channel_id=1, source_target_pairs={{0,1},{1,2},{2,3},{3,4},{4,5},{5,6},{6,7},{7,0},{8,9},{9,10},{10,1... | collective-permute-start | bytes 589832 | tf_op jit(solution)/shard_map/ppermute | solution.py:505
  21.4 0.0 copy-start
  21.4 0.0 copy-start.1
  21.4 2.2 %collective-permute-start.1 = (f32[48,8,128]{2,1,0:T(8,128)}, f32[48,8,128]{2,1,0:T(8,128)S(1)}, u32[]{:S(2)}, u32[]{:S(2)}) collective-permute-start(f32[48,8,128]{2,1,0:T(8,128)} %get-tuple-element.18.refs_0_.own_head), channel_id=1, source_target_pairs={{1,0},{2,1},{3,2},{4,3},{5,4},{6,5},{7,6},{0,7},{9,8},{10,9},{11,1... | collective-permute-start | bytes 589832 | tf_op jit(solution)/shard_map/ppermute | solution.py:506
  23.6 0.0 copy-done.2
  23.6 0.0 copy-done.4
  23.6 0.0 copy-done.5
  23.6 17.6 %bin_inner.1 = (f32[48,24,128]{2,1,0:T(8,128)S(1)}, f32[48,24,128]{2,1,0:T(8,128)S(1)}) custom-call(s32[1,1]{1,0:T(1,128)S(6)} %copy.11.count, s32[1,16384]{1,0:T(1,128)S(1)} %bitcast.20, s32[1,16384]{1,0:T(1,128)S(1)} %bitcast.23, f32[3,1,16384]{2,1,0:T(1,128)S(1)} %bitcast.16), custom_call_target="tpu_custom_call" | custom-call | flops 14495514624 | bytes 4000000 | tf_op jit(solution)/shard_map/bin_inner/pallas_call | solution.py:448
  41.2 0.0 collective-permute-done.refs_4_.before
  41.3 0.8 collective-permute-done.1.refs_5_.after
  42.1 0.0 all-to-all-done.refs_6_.fields
  42.1 0.0 copy-done
  42.1 0.0 copy-done.1
  42.1 1.2 %edges.1 = (f32[16,40,128]{2,1,0:T(8,128)S(1)}, f32[10,40,128]{2,1,0:T(8,128)S(1)}, f32[10,40,128]{2,1,0:T(8,128)S(1)}) custom-call(f32[48,8,128]{2,1,0:T(8,128)S(1)} %copy-done, f32[48,8,128]{2,1,0:T(8,128)S(1)} %copy-done.1, f32[48,24,128]{2,1,0:T(8,128)S(1)} %get-tuple-element.20.refs_2_.load_in, f32[48,24,128]{2,1,0:T(8,128)S(1)} %get-tuple-element.21.refs_3_.kinetic, ...), custom_call_target="tpu_custom_call" | custom-call | bytes 2000000 | tf_op jit(solution)/shard_map/edges/pallas_call | solution.py:275
  43.3 0.1 collective-permute-start.2
  43.4 5.3 %collective-permute-start.3 = (f32[10,40,128]{2,1,0:T(8,128)S(1)}, f32[10,40,128]{2,1,0:T(8,128)S(1)}, u32[]{:S(2)}, u32[]{:S(2)}) collective-permute-start(f32[10,40,128]{2,1,0:T(8,128)S(1)} %get-tuple-element.26), channel_id=1, source_target_pairs={{8,0},{16,8},{24,16},{32,24},{40,32},{48,40},{56,48},{64,56},{72,6... | collective-permute-start | bytes 614408 | tf_op jit(solution)/shard_map/ppermute | solution.py:506
  48.8 0.1 add_convert_fusion.place
  48.8 9.1 %first_interior.1 = (f32[48,40,128]{2,1,0:T(8,128)S(1)}, f32[48,40,128]{2,1,0:T(8,128)S(1)}, f32[48,40,128]{2,1,0:T(8,128)S(1)}) custom-call(f32[48,8,128]{2,1,0:T(8,128)S(1)} %copy-done, f32[48,8,128]{2,1,0:T(8,128)S(1)} %copy-done.1, f32[48,24,128]{2,1,0:T(8,128)S(1)} %get-tuple-element.20.refs_2_.load_in, ...), custom_call_target="tpu_custom_call" | custom-call | bytes 30000000 | tf_op jit(solution)/shard_map/first_interior/pallas_call | solution.py:148
  58.0 0.0 collective-permute-done.2.te_lo.lo
  58.0 0.0 collective-permute-done.3.te_hi.hi
  58.0 3.1 %bands.2 = (f32[48,32,128]{2,1,0:T(8,128)S(1)}, f32[24,8,128]{2,1,0:T(8,128)S(1)}, f32[24,8,128]{2,1,0:T(8,128)S(1)}) custom-call(s32[2]{0:T(128)S(1)} %add_convert_fusion.place, f32[16,40,128]{2,1,0:T(8,128)S(1)} %get-tuple-element.22.te, f32[48,40,128]{2,1,0:T(8,128)S(1)} %get-tuple-element.23.heat, f32[48,40,128]{2,1,0:T(8,128)S(1)} %get-tuple-element.24.load, ...), custom_call_target="tpu_custom_call" | custom-call | bytes 8000000 | tf_op jit(solution)/shard_map/bands/pallas_call | solution.py:219
  61.0 0.7 collective-permute-start.4
  61.7 3.5 %collective-permute-start.5 = (f32[24,8,128]{2,1,0:T(8,128)S(1)}, f32[24,8,128]{2,1,0:T(8,128)S(1)}, u32[]{:S(2)}, u32[]{:S(2)}) collective-permute-start(f32[24,8,128]{2,1,0:T(8,128)S(1)} %get-tuple-element.30), channel_id=1, source_target_pairs={{1,0},{2,1},{3,2},{4,3},{5,4},{6,5},{7,6},{0,7},{9,8},{10,9},{11,1... | collective-permute-start | bytes 294920 | tf_op jit(solution)/shard_map/ppermute | solution.py:506
  65.3 2.6 %collective-permute-done.4.before = f32[24,8,128]{2,1,0:T(8,128)S(1)} collective-permute-done((f32[24,8,128]{2,1,0:T(8,128)S(1)}, f32[24,8,128]{2,1,0:T(8,128)S(1)}, u32[]{:S(2)}, u32[]{:S(2)}) %collective-permute-start.4) | collective-permute-done | bytes 98336 | tf_op jit(solution)/shard_map/ppermute | solution.py:505
  67.8 0.0 collective-permute-done.5.after
  67.8 0.1 second_brick.1
  67.9 0.1 collective-permute-start.6
  68.0 5.3 %collective-permute-start.7 = (f32[4,40,128]{2,1,0:T(8,128)S(1)}, f32[4,40,128]{2,1,0:T(8,128)S(1)}, u32[]{:S(2)}, u32[]{:S(2)}) collective-permute-start(f32[4,40,128]{2,1,0:T(8,128)S(1)} %get-tuple-element.33), channel_id=1, source_target_pairs={{8,0},{16,8},{24,16},{32,24},{40,32},{48,40},{56,48},{64,56},{72,6... | collective-permute-start | bytes 245768 | tf_op jit(solution)/shard_map/ppermute | solution.py:506
  73.4 7.3 %interior.1.inner = f32[48,40,128]{2,1,0:T(8,128)S(1)} custom-call(f32[48,40,128]{2,1,0:T(8,128)S(1)} %get-tuple-element.31.te, f32[48,40,128]{2,1,0:T(8,128)S(1)} %get-tuple-element.23.heat, f32[48,40,128]{2,1,0:T(8,128)S(1)} %get-tuple-element.24.load), custom_call_target="tpu_custom_call" | custom-call | bytes 25000000 | tf_op jit(solution)/shard_map/interior/pallas_call | solution.py:98
  80.7 0.0 copy-start.3
  80.7 0.0 collective-permute-done.6.te_lo
  80.7 0.0 collective-permute-done.7.te_hi
  80.7 3.9 %bands.3 = f32[48,32,128]{2,1,0:T(8,128)} custom-call(s32[2]{0:T(128)S(1)} %add_convert_fusion.place, f32[48,40,128]{2,1,0:T(8,128)S(1)} %get-tuple-element.31.te, f32[48,40,128]{2,1,0:T(8,128)S(1)} %get-tuple-element.23.heat, f32[48,40,128]{2,1,0:T(8,128)S(1)} %get-tuple-element.24.load, f32[4,40,128]{2,1,0:T(8,128)S(1)} %collective-permute-done.6.te_lo, ...), custom_call_target="tpu_custom_call" | custom-call | bytes 8000000 | tf_op jit(solution)/shard_map/bands/pallas_call | solution.py:219
  84.6 5.4 %all-to-all-start.1 = ((f32[48,32,128]{2,1,0:T(8,128)}), f32[48,32,128]{2,1,0:T(8,128)S(1)}, u32[]{:S(2)}, u32[]{:S(2)}) async-start(f32[48,32,128]{2,1,0:T(8,128)} %bands.3), calls=%async_computation.1 | async-start | bytes 1572864 | tf_op jit(solution)/shard_map/all_to_all | solution.py:511
  90.0 0.0 copy-done.3
  90.0 16.3 %read_atoms.1 = f32[3,1,16384]{2,1,0:T(1,128)} custom-call(s32[1,1]{1,0:T(1,128)S(6)} %copy.11.count, f32[1536,128]{1,0:T(8,128)} %bitcast.9.te, s32[1,16384]{1,0:T(1,128)S(1)} %bitcast.21, s32[1,16384]{1,0:T(1,128)S(1)} %bitcast.24, f32[3,1,16384]{2,1,0:T(1,128)S(1)} %bitcast.17, f32[3,1,16384]{2,1,0:T(1,128)S(1)} %bitcast.18), custom_call_target="tpu_custom_call" | custom-call | flops 12884901888 | bytes 4000000 | tf_op jit(solution)/shard_map/read_atoms/pallas_call | solution.py:481
  106.3 0.0 all-to-all-done.1
  106.3 0.9 copy.9
Async XLA Ops:
  3.4 38.8 %all-to-all-start = ((f32[96,40,128]{2,1,0:T(8,128)}), f32[96,40,128]{2,1,0:T(8,128)}, u32[]{:S(2)}, u32[]{:S(2)}) async-start(f32[96,40,128]{2,1,0:T(8,128)} %bitcast.25), calls=%async_computation | async-start | bytes 3932160 | tf_op jit(solution)/shard_map/all_to_all | solution.py:511
  10.0 13.6 %copy-start.2 = (f32[3,1,1,16384]{3,2,1,0:T(1,128)S(1)}, f32[3,1,1,16384]{3,2,1,0:T(1,128)}, u32[]{:S(2)}) copy-start(f32[3,1,1,16384]{3,2,1,0:T(1,128)} %param.9) | copy-start | bytes 589828
  10.0 13.6 %copy-start.4 = (s32[1,1,16384]{2,1,0:T(1,128)S(1)}, s32[1,1,16384]{2,1,0:T(1,128)}, u32[]{:S(2)}) copy-start(s32[1,1,16384]{2,1,0:T(1,128)} %param.11) | copy-start | bytes 196612
  10.0 13.6 %copy-start.5 = (s32[1,1,16384]{2,1,0:T(1,128)S(1)}, s32[1,1,16384]{2,1,0:T(1,128)}, u32[]{:S(2)}) copy-start(s32[1,1,16384]{2,1,0:T(1,128)} %param.12) | copy-start | bytes 196612
  19.4 21.9 %collective-permute-start = (f32[48,8,128]{2,1,0:T(8,128)}, f32[48,8,128]{2,1,0:T(8,128)S(1)}, u32[]{:S(2)}, u32[]{:S(2)}) collective-permute-start(f32[48,8,128]{2,1,0:T(8,128)} %get-tuple-element.19.refs_1_.own_tail), channel_id=1, source_target_pairs={{0,1},{1,2},{2,3},{3,4},{4,5},{5,6},{6,7},{7,0},{8,9},{9,10},{10,1... | collective-permute-start | bytes 589832 | tf_op jit(solution)/shard_map/ppermute | solution.py:505
  21.4 20.7 %copy-start = (f32[48,8,128]{2,1,0:T(8,128)S(1)}, f32[48,8,128]{2,1,0:T(8,128)}, u32[]{:S(2)}) copy-start(f32[48,8,128]{2,1,0:T(8,128)} %get-tuple-element.18.refs_0_.own_head) | copy-start | bytes 589828
  21.4 20.7 %copy-start.1 = (f32[48,8,128]{2,1,0:T(8,128)S(1)}, f32[48,8,128]{2,1,0:T(8,128)}, u32[]{:S(2)}) copy-start(f32[48,8,128]{2,1,0:T(8,128)} %get-tuple-element.19.refs_1_.own_tail) | copy-start | bytes 589828
  21.4 20.7 %collective-permute-start.1 = (f32[48,8,128]{2,1,0:T(8,128)}, f32[48,8,128]{2,1,0:T(8,128)S(1)}, u32[]{:S(2)}, u32[]{:S(2)}) collective-permute-start(f32[48,8,128]{2,1,0:T(8,128)} %get-tuple-element.18.refs_0_.own_head), channel_id=1, source_target_pairs={{1,0},{2,1},{3,2},{4,3},{5,4},{6,5},{7,6},{0,7},{9,8},{10,9},{11,1... | collective-permute-start | bytes 589832 | tf_op jit(solution)/shard_map/ppermute | solution.py:506
  43.3 14.6 %collective-permute-start.2 = (f32[10,40,128]{2,1,0:T(8,128)S(1)}, f32[10,40,128]{2,1,0:T(8,128)S(1)}, u32[]{:S(2)}, u32[]{:S(2)}) collective-permute-start(f32[10,40,128]{2,1,0:T(8,128)S(1)} %get-tuple-element.25), channel_id=1, source_target_pairs={{0,8},{8,16},{16,24},{24,32},{32,40},{40,48},{48,56},{56,64},{64,7... | collective-permute-start | bytes 614408 | tf_op jit(solution)/shard_map/ppermute | solution.py:505
  43.4 14.6 %collective-permute-start.3 = (f32[10,40,128]{2,1,0:T(8,128)S(1)}, f32[10,40,128]{2,1,0:T(8,128)S(1)}, u32[]{:S(2)}, u32[]{:S(2)}) collective-permute-start(f32[10,40,128]{2,1,0:T(8,128)S(1)} %get-tuple-element.26), channel_id=1, source_target_pairs={{8,0},{16,8},{24,16},{32,24},{40,32},{48,40},{56,48},{64,56},{72,6... | collective-permute-start | bytes 614408 | tf_op jit(solution)/shard_map/ppermute | solution.py:506
  61.0 6.8 %collective-permute-start.4 = (f32[24,8,128]{2,1,0:T(8,128)S(1)}, f32[24,8,128]{2,1,0:T(8,128)S(1)}, u32[]{:S(2)}, u32[]{:S(2)}) collective-permute-start(f32[24,8,128]{2,1,0:T(8,128)S(1)} %get-tuple-element.29), channel_id=1, source_target_pairs={{0,1},{1,2},{2,3},{3,4},{4,5},{5,6},{6,7},{7,0},{8,9},{9,10},{10,1... | collective-permute-start | bytes 294920 | tf_op jit(solution)/shard_map/ppermute | solution.py:505
  61.7 6.1 %collective-permute-start.5 = (f32[24,8,128]{2,1,0:T(8,128)S(1)}, f32[24,8,128]{2,1,0:T(8,128)S(1)}, u32[]{:S(2)}, u32[]{:S(2)}) collective-permute-start(f32[24,8,128]{2,1,0:T(8,128)S(1)} %get-tuple-element.30), channel_id=1, source_target_pairs={{1,0},{2,1},{3,2},{4,3},{5,4},{6,5},{7,6},{0,7},{9,8},{10,9},{11,1... | collective-permute-start | bytes 294920 | tf_op jit(solution)/shard_map/ppermute | solution.py:506
  67.9 12.8 %collective-permute-start.6 = (f32[4,40,128]{2,1,0:T(8,128)S(1)}, f32[4,40,128]{2,1,0:T(8,128)S(1)}, u32[]{:S(2)}, u32[]{:S(2)}) collective-permute-start(f32[4,40,128]{2,1,0:T(8,128)S(1)} %get-tuple-element.32), channel_id=1, source_target_pairs={{0,8},{8,16},{16,24},{24,32},{32,40},{40,48},{48,56},{56,64},{64,7... | collective-permute-start | bytes 245768 | tf_op jit(solution)/shard_map/ppermute | solution.py:505
  68.0 12.7 %collective-permute-start.7 = (f32[4,40,128]{2,1,0:T(8,128)S(1)}, f32[4,40,128]{2,1,0:T(8,128)S(1)}, u32[]{:S(2)}, u32[]{:S(2)}) collective-permute-start(f32[4,40,128]{2,1,0:T(8,128)S(1)} %get-tuple-element.33), channel_id=1, source_target_pairs={{8,0},{16,8},{24,16},{32,24},{40,32},{48,40},{56,48},{64,56},{72,6... | collective-permute-start | bytes 245768 | tf_op jit(solution)/shard_map/ppermute | solution.py:506
  80.7 9.3 %copy-start.3 = (f32[3,1,1,16384]{3,2,1,0:T(1,128)S(1)}, f32[3,1,1,16384]{3,2,1,0:T(1,128)}, u32[]{:S(2)}) copy-start(f32[3,1,1,16384]{3,2,1,0:T(1,128)} %param.10) | copy-start | bytes 589828
  84.6 21.7 %all-to-all-start.1 = ((f32[48,32,128]{2,1,0:T(8,128)}), f32[48,32,128]{2,1,0:T(8,128)S(1)}, u32[]{:S(2)}, u32[]{:S(2)}) async-start(f32[48,32,128]{2,1,0:T(8,128)} %bands.3), calls=%async_computation.1 | async-start | bytes 1572864 | tf_op jit(solution)/shard_map/all_to_all | solution.py:511

commit v2 on v1

--- a/solution.py
+++ b/solution.py
@@ -18,7 +18,6 @@
 NEAR = HALO - 1
 ROWS = CY + 2 * HALO
 COLS = CX * CY
-GROUP = 6
 BLOCK = 4096
 MIB = 1024 * 1024
 
@@ -57,16 +56,16 @@
 
 
 def interior_steps(first, second, heat, load, out):
-    def step(source, target, shift):
-        below_u = source[0]
+    def step(source, target, shift, spoiled, group):
+        below_u = source[spoiled]
         _, below_r = with_root(below_u)
-        u = source[1]
+        u = source[spoiled + 1]
         c, r = with_root(u)
 
         def turn(i, carry):
             u, c, r, below = carry
-            for g in range(GROUP):
-                layer = i * GROUP + g
+            for g in range(group):
+                layer = i * group + (spoiled + g)
                 v = source[layer + 2]
                 cv, rv = with_root(v)
                 above = flux(u, r, v, rv)
@@ -74,15 +73,16 @@
                 u, c, r, below = v, cv, rv, above
             return u, c, r, below
 
-        lax.fori_loop(0, CX // GROUP, turn, (u, c, r, flux(below_u, below_r, u, r)))
+        turns = (CX - 2 * spoiled) // group
+        lax.fori_loop(0, turns, turn, (u, c, r, flux(below_u, below_r, u, r)))
 
     for buffer in (first, second):
         buffer[0] = first[1]
         buffer[CX + 1] = first[CX]
-    step(first, second, 1)
-    step(second, first, 1)
-    step(first, second, 1)
-    step(second, out, 0)
+    step(first, second, 1, 0, 8)
+    step(second, first, 1, 0, 8)
+    step(first, second, 1, NEAR, 7)
+    step(second, out, 0, HALO, 8)
 
 
 def padded_brick():
@@ -463,13 +463,16 @@
 def read_kernel(block, count, te, column, lane, velocities, noise, forces, pair):
     @pl.when(pl.program_id(0) == 0)
     def _():
-        table = te[...].T
-        high = table.astype(jnp.bfloat16)
-        pair[:NZ] = high
-        pair[NZ:] = (table - high.astype(jnp.float32)).astype(jnp.bfloat16)
-
-    rows = jnp.dot(pair[...], column_hot(column[...], COLS), preferred_element_type=jnp.float32)
-    picked = jnp.where(lane_mask(lane[...]), rows[:NZ] + rows[NZ:], 0.0)
+        rest = te[...].T * 8.0
+        for k in range(3):
+            piece = rest.astype(jnp.float8_e4m3fn)
+            pair[k * NZ : (k + 1) * NZ] = piece
+            rest = (rest - piece.astype(jnp.float32)) * 16.0
+
+    hot = column_hot(column[...], COLS).astype(jnp.float8_e4m3fn)
+    rows = jnp.dot(pair[...], hot, preferred_element_type=jnp.float32)
+    value = rows[:NZ] * 0.125 + (rows[NZ : 2 * NZ] * (1 / 128) + rows[2 * NZ :] * (1 / 2048))
+    picked = jnp.where(lane_mask(lane[...]), value, 0.0)
     te_atom = jnp.sum(picked, axis=0, keepdims=True)
     drive = jnp.sqrt(2.0 * FRICTION * te_atom)
     forces[...] = living_of(count, block) * (-FRICTION * velocities[...] + drive * noise[...])
@@ -491,7 +494,7 @@
             blocks_of((3, 1), block),
         ],
         out_specs=blocks_of((3, 1), block),
-        scratch_shapes=[pltpu.VMEM((2 * NZ, COLS), jnp.bfloat16)],
+        scratch_shapes=[pltpu.VMEM((3 * NZ, COLS), jnp.float8_e4m3fn)],
         compiler_params=params(48),
         cost_estimate=pl.CostEstimate(
             flops=4 * slots * COLS * NZ, bytes_accessed=4_000_000, transcendentals=0

time: 108 us -> 105 us (0.972)
  Pallas kernels: 70.7 us -> 66.6 us
    pallas_call x1, Pallas kernels: 16.3 us -> 14.1 us  [read_atoms(): pl.pallas_call(functools.partial(read_kernel, block), grid=(slots // bloc...]
  transfers between devices with their start and end apart: 10 -> 10, of which waited for: 2 -> 2; matrix products, arithmetic and copies ran while one was open for 0% -> 0% of each run, Pallas kernels for 56% -> 54%
where the time goes in v2:
time: 105 us; the launch traced here: 103 us
  Pallas kernels  66.6 us (63%)
  starting transfers between devices  30.8 us (29%)
  waiting for transfers between devices  3.46 us (3%)
  between operations  1.44 us (1%)
    pallas_call x2, Pallas kernels, bin_atoms(): pl.pallas_call(functools.partial(bin_kernel, block, faces), grid=(slots /...  27 us
    ppermute x4, starting transfers between devices, to_both_sides(): lax.ppermute(head, axis, [((i + 1) % count, i) for i in range(count)])  16.4 us
    pallas_call x1, Pallas kernels, read_atoms(): pl.pallas_call(functools.partial(read_kernel, block), grid=(slots // bloc...  14.1 us
    all_to_all x2, starting transfers between devices, exchanged(): return lax.all_to_all(blocks, 'gy', split_axis=0, concat_axis=0, tiled=True)  11.4 us
    pallas_call x1, Pallas kernels, first_interior(): pl.pallas_call(functools.partial(first_interior_kernel, parts), out_shape...  8.18 us
    pallas_call x2, Pallas kernels, bands(): pl.pallas_call(functools.partial(bands_kernel, last), out_shape=shapes, i...  6.96 us
    pallas_call x1, Pallas kernels, second_interior(): pl.pallas_call(second_interior_kernel, out_shape=f32(CX, ROWS, NZ), in_sp...  6.39 us
    ppermute x4, starting transfers between devices, to_both_sides(): lax.ppermute(tail, axis, [(i, (i + 1) % count) for i in range(count)])  3.01 us
  transfers between devices with their start and end apart: 10, of which 2 were waited for; matrix products, arithmetic and copies ran while one was open for 0% of the time, Pallas kernels for 54%

profile of v2, /device:TPU:4, one launch (start us, length us, event | category | flops | bytes accessed | tf_op | source)
XLA Modules:
  0.0 103.4 jit_solution(43981414035631415)
XLA Ops:
  0.6 2.7 %widen.1 = f32[8,12,40,128]{3,2,1,0:T(8,128)} custom-call(f32[6,256,128]{2,1,0:T(8,128)} %te.1, f32[6,256,128]{2,1,0:T(8,128)} %source.1), custom_call_target="tpu_custom_call" | custom-call | bytes 4000000 | tf_op jit(solution)/shard_map/widen/pallas_call | solution.py:322
  3.4 6.0 %all-to-all-start = ((f32[96,40,128]{2,1,0:T(8,128)}), f32[96,40,128]{2,1,0:T(8,128)}, u32[]{:S(2)}, u32[]{:S(2)}) async-start(f32[96,40,128]{2,1,0:T(8,128)} %bitcast.25), calls=%async_computation | async-start | bytes 3932160 | tf_op jit(solution)/shard_map/all_to_all | solution.py:514
  10.0 0.0 copy-start.2
  10.0 0.0 copy-start.4
  10.0 0.0 copy-start.5
  10.0 9.4 %bin_faces.1 = (f32[48,8,128]{2,1,0:T(8,128)}, f32[48,8,128]{2,1,0:T(8,128)}) custom-call(s32[1,1]{1,0:T(1,128)S(6)} %copy.11.count, s32[1,16384]{1,0:T(1,128)} %bitcast.19, s32[1,16384]{1,0:T(1,128)} %bitcast.22, f32[3,1,16384]{2,1,0:T(1,128)} %bitcast.15), custom_call_target="tpu_custom_call" | custom-call | flops 4831838208 | bytes 4000000 | tf_op jit(solution)/shard_map/bin_faces/pallas_call | solution.py:448
  19.4 2.0 %collective-permute-start = (f32[48,8,128]{2,1,0:T(8,128)}, f32[48,8,128]{2,1,0:T(8,128)S(1)}, u32[]{:S(2)}, u32[]{:S(2)}) collective-permute-start(f32[48,8,128]{2,1,0:T(8,128)} %get-tuple-element.19.refs_1_.own_tail), channel_id=1, source_target_pairs={{0,1},{1,2},{2,3},{3,4},{4,5},{5,6},{6,7},{7,0},{8,9},{9,10},{10,1... | collective-permute-start | bytes 589832 | tf_op jit(solution)/shard_map/ppermute | solution.py:508
  21.4 0.0 copy-start
  21.4 0.0 copy-start.1
  21.4 2.2 %collective-permute-start.1 = (f32[48,8,128]{2,1,0:T(8,128)}, f32[48,8,128]{2,1,0:T(8,128)S(1)}, u32[]{:S(2)}, u32[]{:S(2)}) collective-permute-start(f32[48,8,128]{2,1,0:T(8,128)} %get-tuple-element.18.refs_0_.own_head), channel_id=1, source_target_pairs={{1,0},{2,1},{3,2},{4,3},{5,4},{6,5},{7,6},{0,7},{9,8},{10,9},{11,1... | collective-permute-start | bytes 589832 | tf_op jit(solution)/shard_map/ppermute | solution.py:509
  23.6 0.0 copy-done.2
  23.6 0.0 copy-done.4
  23.6 0.0 copy-done.5
  23.6 17.6 %bin_inner.1 = (f32[48,24,128]{2,1,0:T(8,128)S(1)}, f32[48,24,128]{2,1,0:T(8,128)S(1)}) custom-call(s32[1,1]{1,0:T(1,128)S(6)} %copy.11.count, s32[1,16384]{1,0:T(1,128)S(1)} %bitcast.20, s32[1,16384]{1,0:T(1,128)S(1)} %bitcast.23, f32[3,1,16384]{2,1,0:T(1,128)S(1)} %bitcast.16), custom_call_target="tpu_custom_call" | custom-call | flops 14495514624 | bytes 4000000 | tf_op jit(solution)/shard_map/bin_inner/pallas_call | solution.py:448
  41.2 0.0 collective-permute-done.refs_4_.before
  41.3 0.8 collective-permute-done.1.refs_5_.after
  42.1 0.0 all-to-all-done.refs_6_.fields
  42.1 0.0 copy-done
  42.1 0.0 copy-done.1
  42.1 1.2 %edges.1 = (f32[16,40,128]{2,1,0:T(8,128)S(1)}, f32[10,40,128]{2,1,0:T(8,128)S(1)}, f32[10,40,128]{2,1,0:T(8,128)S(1)}) custom-call(f32[48,8,128]{2,1,0:T(8,128)S(1)} %copy-done, f32[48,8,128]{2,1,0:T(8,128)S(1)} %copy-done.1, f32[48,24,128]{2,1,0:T(8,128)S(1)} %get-tuple-element.20.refs_2_.load_in, f32[48,24,128]{2,1,0:T(8,128)S(1)} %get-tuple-element.21.refs_3_.kinetic, ...), custom_call_target="tpu_custom_call" | custom-call | bytes 2000000 | tf_op jit(solution)/shard_map/edges/pallas_call | solution.py:275
  43.3 0.1 collective-permute-start.2
  43.4 5.3 %collective-permute-start.3 = (f32[10,40,128]{2,1,0:T(8,128)S(1)}, f32[10,40,128]{2,1,0:T(8,128)S(1)}, u32[]{:S(2)}, u32[]{:S(2)}) collective-permute-start(f32[10,40,128]{2,1,0:T(8,128)S(1)} %get-tuple-element.26), channel_id=1, source_target_pairs={{8,0},{16,8},{24,16},{32,24},{40,32},{48,40},{56,48},{64,56},{72,6... | collective-permute-start | bytes 614408 | tf_op jit(solution)/shard_map/ppermute | solution.py:509
  48.8 0.1 add_convert_fusion.place
  48.8 8.2 %first_interior.1 = (f32[48,40,128]{2,1,0:T(8,128)S(1)}, f32[48,40,128]{2,1,0:T(8,128)S(1)}, f32[48,40,128]{2,1,0:T(8,128)S(1)}) custom-call(f32[48,8,128]{2,1,0:T(8,128)S(1)} %copy-done, f32[48,8,128]{2,1,0:T(8,128)S(1)} %copy-done.1, f32[48,24,128]{2,1,0:T(8,128)S(1)} %get-tuple-element.20.refs_2_.load_in, ...), custom_call_target="tpu_custom_call" | custom-call | bytes 30000000 | tf_op jit(solution)/shard_map/first_interior/pallas_call | solution.py:148
  57.0 0.0 collective-permute-done.2.te_lo.lo
  57.0 0.0 collective-permute-done.3.te_hi.hi
  57.0 3.1 %bands.2 = (f32[48,32,128]{2,1,0:T(8,128)S(1)}, f32[24,8,128]{2,1,0:T(8,128)S(1)}, f32[24,8,128]{2,1,0:T(8,128)S(1)}) custom-call(s32[2]{0:T(128)S(1)} %add_convert_fusion.place, f32[16,40,128]{2,1,0:T(8,128)S(1)} %get-tuple-element.22.te, f32[48,40,128]{2,1,0:T(8,128)S(1)} %get-tuple-element.23.heat, f32[48,40,128]{2,1,0:T(8,128)S(1)} %get-tuple-element.24.load, ...), custom_call_target="tpu_custom_call" | custom-call | bytes 8000000 | tf_op jit(solution)/shard_map/bands/pallas_call | solution.py:219
  60.1 0.7 collective-permute-start.4
  60.8 3.5 %collective-permute-start.5 = (f32[24,8,128]{2,1,0:T(8,128)S(1)}, f32[24,8,128]{2,1,0:T(8,128)S(1)}, u32[]{:S(2)}, u32[]{:S(2)}) collective-permute-start(f32[24,8,128]{2,1,0:T(8,128)S(1)} %get-tuple-element.30), channel_id=1, source_target_pairs={{1,0},{2,1},{3,2},{4,3},{5,4},{6,5},{7,6},{0,7},{9,8},{10,9},{11,1... | collective-permute-start | bytes 294920 | tf_op jit(solution)/shard_map/ppermute | solution.py:509
  64.3 2.6 %collective-permute-done.4.before = f32[24,8,128]{2,1,0:T(8,128)S(1)} collective-permute-done((f32[24,8,128]{2,1,0:T(8,128)S(1)}, f32[24,8,128]{2,1,0:T(8,128)S(1)}, u32[]{:S(2)}, u32[]{:S(2)}) %collective-permute-start.4) | collective-permute-done | bytes 98336 | tf_op jit(solution)/shard_map/ppermute | solution.py:508
  66.9 0.0 collective-permute-done.5.after
  66.9 0.1 second_brick.1
  67.0 0.3 collective-permute-start.6
  67.3 5.3 %collective-permute-start.7 = (f32[4,40,128]{2,1,0:T(8,128)S(1)}, f32[4,40,128]{2,1,0:T(8,128)S(1)}, u32[]{:S(2)}, u32[]{:S(2)}) collective-permute-start(f32[4,40,128]{2,1,0:T(8,128)S(1)} %get-tuple-element.33), channel_id=1, source_target_pairs={{8,0},{16,8},{24,16},{32,24},{40,32},{48,40},{56,48},{64,56},{72,6... | collective-permute-start | bytes 245768 | tf_op jit(solution)/shard_map/ppermute | solution.py:509
  72.6 6.4 %interior.1.inner = f32[48,40,128]{2,1,0:T(8,128)S(1)} custom-call(f32[48,40,128]{2,1,0:T(8,128)S(1)} %get-tuple-element.31.te, f32[48,40,128]{2,1,0:T(8,128)S(1)} %get-tuple-element.23.heat, f32[48,40,128]{2,1,0:T(8,128)S(1)} %get-tuple-element.24.load), custom_call_target="tpu_custom_call" | custom-call | bytes 25000000 | tf_op jit(solution)/shard_map/interior/pallas_call | solution.py:98
  79.0 0.0 copy-start.3
  79.0 0.0 collective-permute-done.6.te_lo
  79.0 0.0 collective-permute-done.7.te_hi
  79.0 3.9 %bands.3 = f32[48,32,128]{2,1,0:T(8,128)} custom-call(s32[2]{0:T(128)S(1)} %add_convert_fusion.place, f32[48,40,128]{2,1,0:T(8,128)S(1)} %get-tuple-element.31.te, f32[48,40,128]{2,1,0:T(8,128)S(1)} %get-tuple-element.23.heat, f32[48,40,128]{2,1,0:T(8,128)S(1)} %get-tuple-element.24.load, f32[4,40,128]{2,1,0:T(8,128)S(1)} %collective-permute-done.6.te_lo, ...), custom_call_target="tpu_custom_call" | custom-call | bytes 8000000 | tf_op jit(solution)/shard_map/bands/pallas_call | solution.py:219
  82.9 5.4 %all-to-all-start.1 = ((f32[48,32,128]{2,1,0:T(8,128)}), f32[48,32,128]{2,1,0:T(8,128)S(1)}, u32[]{:S(2)}, u32[]{:S(2)}) async-start(f32[48,32,128]{2,1,0:T(8,128)} %bands.3), calls=%async_computation.1 | async-start | bytes 1572864 | tf_op jit(solution)/shard_map/all_to_all | solution.py:514
  88.3 0.0 copy-done.3
  88.3 14.1 %read_atoms.1 = f32[3,1,16384]{2,1,0:T(1,128)} custom-call(s32[1,1]{1,0:T(1,128)S(6)} %copy.11.count, f32[1536,128]{1,0:T(8,128)} %bitcast.9.te, s32[1,16384]{1,0:T(1,128)S(1)} %bitcast.21, s32[1,16384]{1,0:T(1,128)S(1)} %bitcast.24, f32[3,1,16384]{2,1,0:T(1,128)S(1)} %bitcast.17, f32[3,1,16384]{2,1,0:T(1,128)S(1)} %bitcast.18), custom_call_target="tpu_custom_call" | custom-call | flops 12884901888 | bytes 4000000 | tf_op jit(solution)/shard_map/read_atoms/pallas_call | solution.py:484
  102.4 0.0 all-to-all-done.1
  102.4 0.9 copy.9
Async XLA Ops:
  3.4 38.8 %all-to-all-start = ((f32[96,40,128]{2,1,0:T(8,128)}), f32[96,40,128]{2,1,0:T(8,128)}, u32[]{:S(2)}, u32[]{:S(2)}) async-start(f32[96,40,128]{2,1,0:T(8,128)} %bitcast.25), calls=%async_computation | async-start | bytes 3932160 | tf_op jit(solution)/shard_map/all_to_all | solution.py:514
  10.0 13.6 %copy-start.2 = (f32[3,1,1,16384]{3,2,1,0:T(1,128)S(1)}, f32[3,1,1,16384]{3,2,1,0:T(1,128)}, u32[]{:S(2)}) copy-start(f32[3,1,1,16384]{3,2,1,0:T(1,128)} %param.9) | copy-start | bytes 589828
  10.0 13.6 %copy-start.4 = (s32[1,1,16384]{2,1,0:T(1,128)S(1)}, s32[1,1,16384]{2,1,0:T(1,128)}, u32[]{:S(2)}) copy-start(s32[1,1,16384]{2,1,0:T(1,128)} %param.11) | copy-start | bytes 196612
  10.0 13.6 %copy-start.5 = (s32[1,1,16384]{2,1,0:T(1,128)S(1)}, s32[1,1,16384]{2,1,0:T(1,128)}, u32[]{:S(2)}) copy-start(s32[1,1,16384]{2,1,0:T(1,128)} %param.12) | copy-start | bytes 196612
  19.4 21.9 %collective-permute-start = (f32[48,8,128]{2,1,0:T(8,128)}, f32[48,8,128]{2,1,0:T(8,128)S(1)}, u32[]{:S(2)}, u32[]{:S(2)}) collective-permute-start(f32[48,8,128]{2,1,0:T(8,128)} %get-tuple-element.19.refs_1_.own_tail), channel_id=1, source_target_pairs={{0,1},{1,2},{2,3},{3,4},{4,5},{5,6},{6,7},{7,0},{8,9},{9,10},{10,1... | collective-permute-start | bytes 589832 | tf_op jit(solution)/shard_map/ppermute | solution.py:508
  21.4 20.7 %copy-start = (f32[48,8,128]{2,1,0:T(8,128)S(1)}, f32[48,8,128]{2,1,0:T(8,128)}, u32[]{:S(2)}) copy-start(f32[48,8,128]{2,1,0:T(8,128)} %get-tuple-element.18.refs_0_.own_head) | copy-start | bytes 589828
  21.4 20.7 %copy-start.1 = (f32[48,8,128]{2,1,0:T(8,128)S(1)}, f32[48,8,128]{2,1,0:T(8,128)}, u32[]{:S(2)}) copy-start(f32[48,8,128]{2,1,0:T(8,128)} %get-tuple-element.19.refs_1_.own_tail) | copy-start | bytes 589828
  21.4 20.7 %collective-permute-start.1 = (f32[48,8,128]{2,1,0:T(8,128)}, f32[48,8,128]{2,1,0:T(8,128)S(1)}, u32[]{:S(2)}, u32[]{:S(2)}) collective-permute-start(f32[48,8,128]{2,1,0:T(8,128)} %get-tuple-element.18.refs_0_.own_head), channel_id=1, source_target_pairs={{1,0},{2,1},{3,2},{4,3},{5,4},{6,5},{7,6},{0,7},{9,8},{10,9},{11,1... | collective-permute-start | bytes 589832 | tf_op jit(solution)/shard_map/ppermute | solution.py:509
  43.3 13.7 %collective-permute-start.2 = (f32[10,40,128]{2,1,0:T(8,128)S(1)}, f32[10,40,128]{2,1,0:T(8,128)S(1)}, u32[]{:S(2)}, u32[]{:S(2)}) collective-permute-start(f32[10,40,128]{2,1,0:T(8,128)S(1)} %get-tuple-element.25), channel_id=1, source_target_pairs={{0,8},{8,16},{16,24},{24,32},{32,40},{40,48},{48,56},{56,64},{64,7... | collective-permute-start | bytes 614408 | tf_op jit(solution)/shard_map/ppermute | solution.py:508
  43.4 13.6 %collective-permute-start.3 = (f32[10,40,128]{2,1,0:T(8,128)S(1)}, f32[10,40,128]{2,1,0:T(8,128)S(1)}, u32[]{:S(2)}, u32[]{:S(2)}) collective-permute-start(f32[10,40,128]{2,1,0:T(8,128)S(1)} %get-tuple-element.26), channel_id=1, source_target_pairs={{8,0},{16,8},{24,16},{32,24},{40,32},{48,40},{56,48},{64,56},{72,6... | collective-permute-start | bytes 614408 | tf_op jit(solution)/shard_map/ppermute | solution.py:509
  60.1 6.8 %collective-permute-start.4 = (f32[24,8,128]{2,1,0:T(8,128)S(1)}, f32[24,8,128]{2,1,0:T(8,128)S(1)}, u32[]{:S(2)}, u32[]{:S(2)}) collective-permute-start(f32[24,8,128]{2,1,0:T(8,128)S(1)} %get-tuple-element.29), channel_id=1, source_target_pairs={{0,1},{1,2},{2,3},{3,4},{4,5},{5,6},{6,7},{7,0},{8,9},{9,10},{10,1... | collective-permute-start | bytes 294920 | tf_op jit(solution)/shard_map/ppermute | solution.py:508
  60.8 6.1 %collective-permute-start.5 = (f32[24,8,128]{2,1,0:T(8,128)S(1)}, f32[24,8,128]{2,1,0:T(8,128)S(1)}, u32[]{:S(2)}, u32[]{:S(2)}) collective-permute-start(f32[24,8,128]{2,1,0:T(8,128)S(1)} %get-tuple-element.30), channel_id=1, source_target_pairs={{1,0},{2,1},{3,2},{4,3},{5,4},{6,5},{7,6},{0,7},{9,8},{10,9},{11,1... | collective-permute-start | bytes 294920 | tf_op jit(solution)/shard_map/ppermute | solution.py:509
  67.0 12.0 %collective-permute-start.6 = (f32[4,40,128]{2,1,0:T(8,128)S(1)}, f32[4,40,128]{2,1,0:T(8,128)S(1)}, u32[]{:S(2)}, u32[]{:S(2)}) collective-permute-start(f32[4,40,128]{2,1,0:T(8,128)S(1)} %get-tuple-element.32), channel_id=1, source_target_pairs={{0,8},{8,16},{16,24},{24,32},{32,40},{40,48},{48,56},{56,64},{64,7... | collective-permute-start | bytes 245768 | tf_op jit(solution)/shard_map/ppermute | solution.py:508
  67.3 11.8 %collective-permute-start.7 = (f32[4,40,128]{2,1,0:T(8,128)S(1)}, f32[4,40,128]{2,1,0:T(8,128)S(1)}, u32[]{:S(2)}, u32[]{:S(2)}) collective-permute-start(f32[4,40,128]{2,1,0:T(8,128)S(1)} %get-tuple-element.33), channel_id=1, source_target_pairs={{8,0},{16,8},{24,16},{32,24},{40,32},{48,40},{56,48},{64,56},{72,6... | collective-permute-start | bytes 245768 | tf_op jit(solution)/shard_map/ppermute | solution.py:509
  79.0 9.3 %copy-start.3 = (f32[3,1,1,16384]{3,2,1,0:T(1,128)S(1)}, f32[3,1,1,16384]{3,2,1,0:T(1,128)}, u32[]{:S(2)}) copy-start(f32[3,1,1,16384]{3,2,1,0:T(1,128)} %param.10) | copy-start | bytes 589828
  82.9 19.5 %all-to-all-start.1 = ((f32[48,32,128]{2,1,0:T(8,128)}), f32[48,32,128]{2,1,0:T(8,128)S(1)}, u32[]{:S(2)}, u32[]{:S(2)}) async-start(f32[48,32,128]{2,1,0:T(8,128)} %bands.3), calls=%async_computation.1 | async-start | bytes 1572864 | tf_op jit(solution)/shard_map/all_to_all | solution.py:514

commit v3 on v2

--- a/solution.py
+++ b/solution.py
@@ -108,7 +108,7 @@
 
 
 def first_interior_kernel(
-    parts, own_head, own_tail, load_in, kinetic, before, after, fields, out, heat, load, *scratch
+    parts, own_head, own_tail, load_in, kinetic, halo, fields, out, heat, load, *scratch
 ):
     first, second, source, sems = scratch
     layers = CX // parts
@@ -124,22 +124,21 @@
         fetch.start()
     for i in range(parts):
         span = pl.ds(i * layers, layers)
-        load[span] = side_by_side(own_head, load_in, own_tail, after, before, span, 0)
+        load[span] = side_by_side(own_head, load_in, own_tail, halo, span, 0)
     for fetch in fetches:
         fetch.wait()
     for i in range(parts):
         span = pl.ds(i * layers, layers)
         heat[span] = source[span] + side_by_side(
-            own_head, kinetic, own_tail, after, before, span, HALO
+            own_head, kinetic, own_tail, halo, span, 1
         )
     interior_steps(first, second, heat, load, out)
 
 
-def side_by_side(own_head, inner, own_tail, after, before, span, row):
-    rows = slice(row, row + HALO)
+def side_by_side(own_head, inner, own_tail, halo, span, field):
+    rows = slice(field * HALO, field * HALO + HALO)
     return jnp.concatenate(
-        [own_head[span, rows], inner[span], own_tail[span, rows], after[span, rows], before[span, rows]],
-        1,
+        [own_head[span, rows], inner[span], own_tail[span, rows], halo[field, span]], 1
     )
 
 
@@ -148,7 +147,7 @@
     return pl.pallas_call(
         functools.partial(first_interior_kernel, parts),
         out_shape=[whole] * 3,
-        in_specs=[VMEM] * 6 + [ANY],
+        in_specs=[VMEM] * 5 + [ANY],
         out_specs=[VMEM] * 3,
         scratch_shapes=[padded_brick()] * 2
         + [pltpu.VMEM((CX, ROWS, NZ), jnp.float32)]
@@ -228,7 +227,8 @@
 
 
 def edges_kernel(parts, *refs):
-    inside, (fields, ends, head, tail, here, source, sems) = refs[:6], refs[6:]
+    inside, (fields, ends, head, tail, halo, here, source, sems) = refs[:6], refs[6:]
+    own_head, own_tail, load_in, kinetic, before, after = inside
     layers = CX // parts
     many = 2 * HALO
     fetches = []
@@ -254,18 +254,22 @@
             there = fields.at[pl.ds(layer + (part + 1) * layers, count)]
             fetch(there, source.at[k, pl.ds(layer - first, count)])
             layer += count
+    before, after = unpack(before), unpack(after)
+    gap = jnp.zeros((CX, 2 * HALO - 2 * NEAR, NZ), jnp.float32)
+    for field in range(2):
+        rows = slice(field * NEAR, field * NEAR + NEAR)
+        halo[field] = jnp.concatenate([after[:, rows], gap, before[:, rows]], 1)
     for copy in fetches:
         copy.wait()
     ends[...] = here[...]
     for k, (target, at) in enumerate(((head, 0), (tail, 2 * many - HALO))):
-        own_head, own_tail, load_in, kinetic, before, after = inside
         span = pl.ds((0, CX - NEAR)[k], NEAR)
         target[:HALO] = here[pl.ds(at, HALO)]
         target[pl.ds(HALO, NEAR)] = source[k] + side_by_side(
-            own_head, kinetic, own_tail, after, before, span, HALO
+            own_head, kinetic, own_tail, halo, span, 1
         )
         target[pl.ds(HALO + NEAR, NEAR)] = side_by_side(
-            own_head, load_in, own_tail, after, before, span, 0
+            own_head, load_in, own_tail, halo, span, 0
         )
 
 
@@ -274,9 +278,9 @@
     ends = (4 * HALO, ROWS, NZ)
     return pl.pallas_call(
         functools.partial(edges_kernel, parts),
-        out_shape=[f32(*ends), edge, edge],
+        out_shape=[f32(*ends), edge, edge, f32(2, CX, 2 * HALO, NZ)],
         in_specs=[VMEM] * 6 + [ANY],
-        out_specs=[VMEM] * 3,
+        out_specs=[VMEM] * 4,
         scratch_shapes=[
             pltpu.VMEM(ends, jnp.float32),
             pltpu.VMEM((2, NEAR, ROWS, NZ), jnp.float32),
@@ -388,7 +392,9 @@
     return jnp.where(slot < count[0, 0], 1.0, 0.0)
 
 
-def bin_kernel(block, faces, count, column, lane, velocities, first, second, sums):
+def bin_kernel(block, faces, count, column, lane, velocities, first, second, *rest):
+    *sends, sums = rest
+
     @pl.when(pl.program_id(0) == 0)
     def _():
         sums[...] = jnp.zeros_like(sums)
@@ -427,9 +433,28 @@
                 for target, side in ((first, slice(0, HALO)), (second, slice(HALO, 2 * HALO))):
                     target[span, :HALO] = load[:, side]
                     target[span, HALO:] = kinetic[:, side]
+                for target, side in (
+                    (sends[0], slice(0, NEAR)),
+                    (sends[1], slice(2 * HALO - NEAR, 2 * HALO)),
+                ):
+                    pack(target, layer // 4, jnp.concatenate([load[:, side], kinetic[:, side]], 1))
             else:
                 first[span] = load
                 second[span] = kinetic
+
+
+def pack(target, first, rows):
+    fours = rows.reshape(rows.shape[0] // 4, 4, 2 * NEAR, NZ)
+    span = pl.ds(first, fours.shape[0])
+    for k in range(3):
+        target[span, k] = jnp.concatenate([fours[:, k], fours[:, 3, 2 * k : 2 * k + 2]], 1)
+
+
+def unpack(tiles):
+    kept = [tiles[:, k] for k in range(3)]
+    fourth = jnp.concatenate([tile[:, 2 * NEAR :] for tile in kept], 1)
+    fours = jnp.stack([tile[:, : 2 * NEAR] for tile in kept] + [fourth], 1)
+    return fours.reshape(4 * fours.shape[0], 2 * NEAR, NZ)
 
 
 def blocks_of(shape, block):
@@ -445,12 +470,14 @@
     block = min(BLOCK, slots)
     rows = 2 * HALO if faces else INNER
     result = (CX, rows, NZ)
+    send = (CX // 4, 3, 2 * HALO, NZ)
+    results = [result] * 2 + ([send] * 2 if faces else [])
     return pl.pallas_call(
         functools.partial(bin_kernel, block, faces),
         grid=(slots // block,),
-        out_shape=[f32(*result)] * 2,
+        out_shape=[f32(*shape) for shape in results],
         in_specs=[SMEM, blocks_of((1,), block), blocks_of((1,), block), blocks_of((3, 1), block)],
-        out_specs=[whole_of(*result)] * 2,
+        out_specs=[whole_of(*shape) for shape in results],
         scratch_shapes=[pltpu.VMEM((2 * NZ, CX * rows), jnp.float32)],
         compiler_params=params(63 if faces else 48),
         cost_estimate=pl.CostEstimate(
@@ -523,17 +550,18 @@
     column = cell_index[0]
     lane = cell_lane[0]
     moving = velocities[:, 0]
-    own_head, own_tail = bin_atoms(True, brick_atoms, column, lane, moving)
-    before, after = to_both_sides(own_head, own_tail, "gy")
+    own_head, own_tail, head, tail = bin_atoms(True, brick_atoms, column, lane, moving)
+    before, after = to_both_sides(head, tail, "gy")
     load, kinetic = bin_atoms(False, brick_atoms, column, lane, moving)
 
     position = lax.axis_index("gx")
     final = lax.axis_size("gx") - 1
     place = jnp.stack([position == 0, position == final]).astype(jnp.int32)
-    arrays = (own_head, own_tail, load, kinetic, before, after, fields)
-    ends, head, tail = edges(parts, *arrays)
+    ends, head, tail, halo = edges(
+        parts, own_head, own_tail, load, kinetic, before, after, fields
+    )
     lo, hi = to_both_sides(head, tail, "gx")
-    inner, heat, load = first_interior(parts, *arrays)
+    inner, heat, load = first_interior(parts, own_head, own_tail, load, kinetic, halo, fields)
     middle, head, tail = bands(False, place, ends, heat, load, lo, hi, lo, hi, inner)
 
     before, after = to_both_sides(head, tail, "gy")

time: 105 us -> 104 us (level)
  transfers between devices with their start and end apart: 10 -> 10, of which waited for: 2 -> 1; matrix products, arithmetic and copies ran while one was open for 0% -> 0% of each run, Pallas kernels for 54% -> 54%
where the time goes in v3:
time: 104 us; the launch traced here: 103 us
  Pallas kernels  66.7 us (64%)
  starting transfers between devices  30.8 us (30%)
  waiting for transfers between devices  2.61 us (3%)
  between operations  1.47 us (1%)
    pallas_call x2, Pallas kernels, bin_atoms(): pl.pallas_call(functools.partial(bin_kernel, block, faces), grid=(slots /...  27.1 us
    ppermute x4, starting transfers between devices, to_both_sides(): lax.ppermute(head, axis, [((i + 1) % count, i) for i in range(count)])  17 us
    pallas_call x1, Pallas kernels, read_atoms(): pl.pallas_call(functools.partial(read_kernel, block), grid=(slots // bloc...  14.1 us
    all_to_all x2, starting transfers between devices, exchanged(): return lax.all_to_all(blocks, 'gy', split_axis=0, concat_axis=0, tiled=True)  11.4 us
    pallas_call x1, Pallas kernels, first_interior(): pl.pallas_call(functools.partial(first_interior_kernel, parts), out_shape...  8.17 us
    pallas_call x2, Pallas kernels, bands(): pl.pallas_call(functools.partial(bands_kernel, last), out_shape=shapes, i...  6.95 us
    pallas_call x1, Pallas kernels, second_interior(): pl.pallas_call(second_interior_kernel, out_shape=f32(CX, ROWS, NZ), in_sp...  6.39 us
    pallas_call x1, Pallas kernels, widened(): pl.pallas_call(functools.partial(widen_kernel, parts), out_shape=f32(part...  2.72 us
  transfers between devices with their start and end apart: 10, of which 1 were waited for; matrix products, arithmetic and copies ran while one was open for 0% of the time, Pallas kernels for 54%

profile of v3, /device:TPU:4, one launch (start us, length us, event | category | flops | bytes accessed | tf_op | source)
XLA Modules:
  0.0 102.6 jit_solution(1817125079287274384)
XLA Ops:
  0.6 2.7 %widen.1 = f32[8,12,40,128]{3,2,1,0:T(8,128)} custom-call(f32[6,256,128]{2,1,0:T(8,128)} %te.1, f32[6,256,128]{2,1,0:T(8,128)} %source.1), custom_call_target="tpu_custom_call" | custom-call | bytes 4000000 | tf_op jit(solution)/shard_map/widen/pallas_call | solution.py:326
  3.4 6.0 %all-to-all-start = ((f32[96,40,128]{2,1,0:T(8,128)}), f32[96,40,128]{2,1,0:T(8,128)}, u32[]{:S(2)}, u32[]{:S(2)}) async-start(f32[96,40,128]{2,1,0:T(8,128)} %bitcast.25), calls=%async_computation | async-start | bytes 3932160 | tf_op jit(solution)/shard_map/all_to_all | solution.py:541
  10.0 0.0 copy-start.2
  10.0 0.0 copy-start.4
  10.0 0.0 copy-start.5
  10.0 9.5 %bin_faces.1 = (f32[48,8,128]{2,1,0:T(8,128)}, f32[48,8,128]{2,1,0:T(8,128)}, f32[12,3,8,128]{3,2,1,0:T(8,128)}, f32[12,3,8,128]{3,2,1,0:T(8,128)}) custom-call(s32[1,1]{1,0:T(1,128)S(6)} %copy.11.count, s32[1,16384]{1,0:T(1,128)} %bitcast.19, s32[1,16384]{1,0:T(1,128)} %bitcast.22, f32[3,1,16384]{2,1,0:T(1,128)} %bitcast.15), custom_call_target="tpu_custom_call" | custom-call | flops 4831838208 | bytes 4000000 | tf_op jit(solution)/shard_map/bin_faces/pallas_call | solution.py:475
  19.5 2.0 %collective-permute-start = (f32[12,3,8,128]{3,2,1,0:T(8,128)}, f32[12,3,8,128]{3,2,1,0:T(8,128)S(1)}, u32[]{:S(2)}, u32[]{:S(2)}) collective-permute-start(f32[12,3,8,128]{3,2,1,0:T(8,128)} %get-tuple-element.25), channel_id=1, source_target_pairs={{0,1},{1,2},{2,3},{3,4},{4,5},{5,6},{6,7},{7,0},{8,9},{9,10},{10,1... | collective-permute-start | bytes 442376 | tf_op jit(solution)/shard_map/ppermute | solution.py:535
  21.5 0.0 copy-start
  21.5 0.0 copy-start.1
  21.5 2.2 %collective-permute-start.1 = (f32[12,3,8,128]{3,2,1,0:T(8,128)}, f32[12,3,8,128]{3,2,1,0:T(8,128)S(1)}, u32[]{:S(2)}, u32[]{:S(2)}) collective-permute-start(f32[12,3,8,128]{3,2,1,0:T(8,128)} %get-tuple-element.26), channel_id=1, source_target_pairs={{1,0},{2,1},{3,2},{4,3},{5,4},{6,5},{7,6},{0,7},{9,8},{10,9},{11,1... | collective-permute-start | bytes 442376 | tf_op jit(solution)/shard_map/ppermute | solution.py:536
  23.7 0.0 copy-done.2
  23.7 0.0 copy-done.4
  23.7 0.0 copy-done.5
  23.7 17.6 %bin_inner.1 = (f32[48,24,128]{2,1,0:T(8,128)S(1)}, f32[48,24,128]{2,1,0:T(8,128)S(1)}) custom-call(s32[1,1]{1,0:T(1,128)S(6)} %copy.11.count, s32[1,16384]{1,0:T(1,128)S(1)} %bitcast.20, s32[1,16384]{1,0:T(1,128)S(1)} %bitcast.23, f32[3,1,16384]{2,1,0:T(1,128)S(1)} %bitcast.16), custom_call_target="tpu_custom_call" | custom-call | flops 14495514624 | bytes 4000000 | tf_op jit(solution)/shard_map/bin_inner/pallas_call | solution.py:475
  41.4 0.0 collective-permute-done.refs_4_
  41.4 0.0 collective-permute-done.1.refs_5_
  41.4 0.0 all-to-all-done.refs_6_.fields
  41.4 0.0 copy-done
  41.4 0.0 copy-done.1
  41.4 1.2 %edges.1 = (f32[16,40,128]{2,1,0:T(8,128)S(1)}, f32[10,40,128]{2,1,0:T(8,128)S(1)}, f32[10,40,128]{2,1,0:T(8,128)S(1)}, f32[2,48,8,128]{3,2,1,0:T(8,128)S(1)}) custom-call(f32[48,8,128]{2,1,0:T(8,128)S(1)} %copy-done, f32[48,8,128]{2,1,0:T(8,128)S(1)} %copy-done.1, f32[48,24,128]{2,1,0:T(8,128)S(1)} %get-tuple-element.23.refs_2_.load_in, ...), custom_call_target="tpu_custom_call" | custom-call | bytes 2000000 | tf_op jit(solution)/shard_map/edges/pallas_call | solution.py:279
  42.6 0.1 collective-permute-start.2
  42.7 5.3 %collective-permute-start.3 = (f32[10,40,128]{2,1,0:T(8,128)S(1)}, f32[10,40,128]{2,1,0:T(8,128)S(1)}, u32[]{:S(2)}, u32[]{:S(2)}) collective-permute-start(f32[10,40,128]{2,1,0:T(8,128)S(1)} %get-tuple-element.32), channel_id=1, source_target_pairs={{8,0},{16,8},{24,16},{32,24},{40,32},{48,40},{56,48},{64,56},{72,6... | collective-permute-start | bytes 614408 | tf_op jit(solution)/shard_map/ppermute | solution.py:536
  48.1 0.1 add_convert_fusion.place
  48.1 8.2 %first_interior.1 = (f32[48,40,128]{2,1,0:T(8,128)S(1)}, f32[48,40,128]{2,1,0:T(8,128)S(1)}, f32[48,40,128]{2,1,0:T(8,128)S(1)}) custom-call(f32[48,8,128]{2,1,0:T(8,128)S(1)} %copy-done, f32[48,8,128]{2,1,0:T(8,128)S(1)} %copy-done.1, f32[48,24,128]{2,1,0:T(8,128)S(1)} %get-tuple-element.23.refs_2_.load_in, ...), custom_call_target="tpu_custom_call" | custom-call | bytes 30000000 | tf_op jit(solution)/shard_map/first_interior/pallas_call | solution.py:147
  56.3 0.0 collective-permute-done.2.te_lo.lo
  56.3 0.0 collective-permute-done.3.te_hi.hi
  56.3 3.1 %bands.2 = (f32[48,32,128]{2,1,0:T(8,128)S(1)}, f32[24,8,128]{2,1,0:T(8,128)S(1)}, f32[24,8,128]{2,1,0:T(8,128)S(1)}) custom-call(s32[2]{0:T(128)S(1)} %add_convert_fusion.place, f32[16,40,128]{2,1,0:T(8,128)S(1)} %get-tuple-element.27.te, f32[48,40,128]{2,1,0:T(8,128)S(1)} %get-tuple-element.29.heat, f32[48,40,128]{2,1,0:T(8,128)S(1)} %get-tuple-element.30.load, ...), custom_call_target="tpu_custom_call" | custom-call | bytes 8000000 | tf_op jit(solution)/shard_map/bands/pallas_call | solution.py:218
  59.4 0.1 collective-permute-start.4
  59.5 4.1 %collective-permute-start.5 = (f32[24,8,128]{2,1,0:T(8,128)S(1)}, f32[24,8,128]{2,1,0:T(8,128)S(1)}, u32[]{:S(2)}, u32[]{:S(2)}) collective-permute-start(f32[24,8,128]{2,1,0:T(8,128)S(1)} %get-tuple-element.36), channel_id=1, source_target_pairs={{1,0},{2,1},{3,2},{4,3},{5,4},{6,5},{7,6},{0,7},{9,8},{10,9},{11,1... | collective-permute-start | bytes 294920 | tf_op jit(solution)/shard_map/ppermute | solution.py:536
  63.6 2.6 %collective-permute-done.4.before = f32[24,8,128]{2,1,0:T(8,128)S(1)} collective-permute-done((f32[24,8,128]{2,1,0:T(8,128)S(1)}, f32[24,8,128]{2,1,0:T(8,128)S(1)}, u32[]{:S(2)}, u32[]{:S(2)}) %collective-permute-start.4) | collective-permute-done | bytes 98336 | tf_op jit(solution)/shard_map/ppermute | solution.py:535
  66.2 0.0 collective-permute-done.5.after
  66.2 0.1 second_brick.1
  66.3 0.3 collective-permute-start.6
  66.5 5.3 %collective-permute-start.7 = (f32[4,40,128]{2,1,0:T(8,128)S(1)}, f32[4,40,128]{2,1,0:T(8,128)S(1)}, u32[]{:S(2)}, u32[]{:S(2)}) collective-permute-start(f32[4,40,128]{2,1,0:T(8,128)S(1)} %get-tuple-element.39), channel_id=1, source_target_pairs={{8,0},{16,8},{24,16},{32,24},{40,32},{48,40},{56,48},{64,56},{72,6... | collective-permute-start | bytes 245768 | tf_op jit(solution)/shard_map/ppermute | solution.py:536
  71.9 6.4 %interior.1.inner = f32[48,40,128]{2,1,0:T(8,128)S(1)} custom-call(f32[48,40,128]{2,1,0:T(8,128)S(1)} %get-tuple-element.37.te, f32[48,40,128]{2,1,0:T(8,128)S(1)} %get-tuple-element.29.heat, f32[48,40,128]{2,1,0:T(8,128)S(1)} %get-tuple-element.30.load), custom_call_target="tpu_custom_call" | custom-call | bytes 25000000 | tf_op jit(solution)/shard_map/interior/pallas_call | solution.py:98
  78.3 0.0 copy-start.3
  78.3 0.0 collective-permute-done.6.te_lo
  78.3 0.0 collective-permute-done.7.te_hi
  78.3 3.9 %bands.3 = f32[48,32,128]{2,1,0:T(8,128)} custom-call(s32[2]{0:T(128)S(1)} %add_convert_fusion.place, f32[48,40,128]{2,1,0:T(8,128)S(1)} %get-tuple-element.37.te, f32[48,40,128]{2,1,0:T(8,128)S(1)} %get-tuple-element.29.heat, f32[48,40,128]{2,1,0:T(8,128)S(1)} %get-tuple-element.30.load, f32[4,40,128]{2,1,0:T(8,128)S(1)} %collective-permute-done.6.te_lo, ...), custom_call_target="tpu_custom_call" | custom-call | bytes 8000000 | tf_op jit(solution)/shard_map/bands/pallas_call | solution.py:218
  82.2 5.4 %all-to-all-start.1 = ((f32[48,32,128]{2,1,0:T(8,128)}), f32[48,32,128]{2,1,0:T(8,128)S(1)}, u32[]{:S(2)}, u32[]{:S(2)}) async-start(f32[48,32,128]{2,1,0:T(8,128)} %bands.3), calls=%async_computation.1 | async-start | bytes 1572864 | tf_op jit(solution)/shard_map/all_to_all | solution.py:541
  87.6 0.0 copy-done.3
  87.6 14.1 %read_atoms.1 = f32[3,1,16384]{2,1,0:T(1,128)} custom-call(s32[1,1]{1,0:T(1,128)S(6)} %copy.11.count, f32[1536,128]{1,0:T(8,128)} %bitcast.9.te, s32[1,16384]{1,0:T(1,128)S(1)} %bitcast.21, s32[1,16384]{1,0:T(1,128)S(1)} %bitcast.24, f32[3,1,16384]{2,1,0:T(1,128)S(1)} %bitcast.17, f32[3,1,16384]{2,1,0:T(1,128)S(1)} %bitcast.18), custom_call_target="tpu_custom_call" | custom-call | flops 12884901888 | bytes 4000000 | tf_op jit(solution)/shard_map/read_atoms/pallas_call | solution.py:511
  101.7 0.0 all-to-all-done.1
  101.7 0.9 copy.9
Async XLA Ops:
  3.4 38.0 %all-to-all-start = ((f32[96,40,128]{2,1,0:T(8,128)}), f32[96,40,128]{2,1,0:T(8,128)}, u32[]{:S(2)}, u32[]{:S(2)}) async-start(f32[96,40,128]{2,1,0:T(8,128)} %bitcast.25), calls=%async_computation | async-start | bytes 3932160 | tf_op jit(solution)/shard_map/all_to_all | solution.py:541
  10.0 13.7 %copy-start.2 = (f32[3,1,1,16384]{3,2,1,0:T(1,128)S(1)}, f32[3,1,1,16384]{3,2,1,0:T(1,128)}, u32[]{:S(2)}) copy-start(f32[3,1,1,16384]{3,2,1,0:T(1,128)} %param.9) | copy-start | bytes 589828
  10.0 13.7 %copy-start.4 = (s32[1,1,16384]{2,1,0:T(1,128)S(1)}, s32[1,1,16384]{2,1,0:T(1,128)}, u32[]{:S(2)}) copy-start(s32[1,1,16384]{2,1,0:T(1,128)} %param.11) | copy-start | bytes 196612
  10.0 13.7 %copy-start.5 = (s32[1,1,16384]{2,1,0:T(1,128)S(1)}, s32[1,1,16384]{2,1,0:T(1,128)}, u32[]{:S(2)}) copy-start(s32[1,1,16384]{2,1,0:T(1,128)} %param.12) | copy-start | bytes 196612
  19.5 21.9 %collective-permute-start = (f32[12,3,8,128]{3,2,1,0:T(8,128)}, f32[12,3,8,128]{3,2,1,0:T(8,128)S(1)}, u32[]{:S(2)}, u32[]{:S(2)}) collective-permute-start(f32[12,3,8,128]{3,2,1,0:T(8,128)} %get-tuple-element.25), channel_id=1, source_target_pairs={{0,1},{1,2},{2,3},{3,4},{4,5},{5,6},{6,7},{7,0},{8,9},{9,10},{10,1... | collective-permute-start | bytes 442376 | tf_op jit(solution)/shard_map/ppermute | solution.py:535
  21.5 19.9 %copy-start = (f32[48,8,128]{2,1,0:T(8,128)S(1)}, f32[48,8,128]{2,1,0:T(8,128)}, u32[]{:S(2)}) copy-start(f32[48,8,128]{2,1,0:T(8,128)} %get-tuple-element.21.refs_0_.own_head) | copy-start | bytes 589828
  21.5 19.9 %copy-start.1 = (f32[48,8,128]{2,1,0:T(8,128)S(1)}, f32[48,8,128]{2,1,0:T(8,128)}, u32[]{:S(2)}) copy-start(f32[48,8,128]{2,1,0:T(8,128)} %get-tuple-element.22.refs_1_.own_tail) | copy-start | bytes 589828
  21.5 19.8 %collective-permute-start.1 = (f32[12,3,8,128]{3,2,1,0:T(8,128)}, f32[12,3,8,128]{3,2,1,0:T(8,128)S(1)}, u32[]{:S(2)}, u32[]{:S(2)}) collective-permute-start(f32[12,3,8,128]{3,2,1,0:T(8,128)} %get-tuple-element.26), channel_id=1, source_target_pairs={{1,0},{2,1},{3,2},{4,3},{5,4},{6,5},{7,6},{0,7},{9,8},{10,9},{11,1... | collective-permute-start | bytes 442376 | tf_op jit(solution)/shard_map/ppermute | solution.py:536
  42.6 13.7 %collective-permute-start.2 = (f32[10,40,128]{2,1,0:T(8,128)S(1)}, f32[10,40,128]{2,1,0:T(8,128)S(1)}, u32[]{:S(2)}, u32[]{:S(2)}) collective-permute-start(f32[10,40,128]{2,1,0:T(8,128)S(1)} %get-tuple-element.31), channel_id=1, source_target_pairs={{0,8},{8,16},{16,24},{24,32},{32,40},{40,48},{48,56},{56,64},{64,7... | collective-permute-start | bytes 614408 | tf_op jit(solution)/shard_map/ppermute | solution.py:535
  42.7 13.6 %collective-permute-start.3 = (f32[10,40,128]{2,1,0:T(8,128)S(1)}, f32[10,40,128]{2,1,0:T(8,128)S(1)}, u32[]{:S(2)}, u32[]{:S(2)}) collective-permute-start(f32[10,40,128]{2,1,0:T(8,128)S(1)} %get-tuple-element.32), channel_id=1, source_target_pairs={{8,0},{16,8},{24,16},{32,24},{40,32},{48,40},{56,48},{64,56},{72,6... | collective-permute-start | bytes 614408 | tf_op jit(solution)/shard_map/ppermute | solution.py:536
  59.4 6.8 %collective-permute-start.4 = (f32[24,8,128]{2,1,0:T(8,128)S(1)}, f32[24,8,128]{2,1,0:T(8,128)S(1)}, u32[]{:S(2)}, u32[]{:S(2)}) collective-permute-start(f32[24,8,128]{2,1,0:T(8,128)S(1)} %get-tuple-element.35), channel_id=1, source_target_pairs={{0,1},{1,2},{2,3},{3,4},{4,5},{5,6},{6,7},{7,0},{8,9},{9,10},{10,1... | collective-permute-start | bytes 294920 | tf_op jit(solution)/shard_map/ppermute | solution.py:535
  59.5 6.7 %collective-permute-start.5 = (f32[24,8,128]{2,1,0:T(8,128)S(1)}, f32[24,8,128]{2,1,0:T(8,128)S(1)}, u32[]{:S(2)}, u32[]{:S(2)}) collective-permute-start(f32[24,8,128]{2,1,0:T(8,128)S(1)} %get-tuple-element.36), channel_id=1, source_target_pairs={{1,0},{2,1},{3,2},{4,3},{5,4},{6,5},{7,6},{0,7},{9,8},{10,9},{11,1... | collective-permute-start | bytes 294920 | tf_op jit(solution)/shard_map/ppermute | solution.py:536
  66.3 12.0 %collective-permute-start.6 = (f32[4,40,128]{2,1,0:T(8,128)S(1)}, f32[4,40,128]{2,1,0:T(8,128)S(1)}, u32[]{:S(2)}, u32[]{:S(2)}) collective-permute-start(f32[4,40,128]{2,1,0:T(8,128)S(1)} %get-tuple-element.38), channel_id=1, source_target_pairs={{0,8},{8,16},{16,24},{24,32},{32,40},{40,48},{48,56},{56,64},{64,7... | collective-permute-start | bytes 245768 | tf_op jit(solution)/shard_map/ppermute | solution.py:535
  66.5 11.8 %collective-permute-start.7 = (f32[4,40,128]{2,1,0:T(8,128)S(1)}, f32[4,40,128]{2,1,0:T(8,128)S(1)}, u32[]{:S(2)}, u32[]{:S(2)}) collective-permute-start(f32[4,40,128]{2,1,0:T(8,128)S(1)} %get-tuple-element.39), channel_id=1, source_target_pairs={{8,0},{16,8},{24,16},{32,24},{40,32},{48,40},{56,48},{64,56},{72,6... | collective-permute-start | bytes 245768 | tf_op jit(solution)/shard_map/ppermute | solution.py:536
  78.3 9.3 %copy-start.3 = (f32[3,1,1,16384]{3,2,1,0:T(1,128)S(1)}, f32[3,1,1,16384]{3,2,1,0:T(1,128)}, u32[]{:S(2)}) copy-start(f32[3,1,1,16384]{3,2,1,0:T(1,128)} %param.10) | copy-start | bytes 589828
  82.2 19.5 %all-to-all-start.1 = ((f32[48,32,128]{2,1,0:T(8,128)}), f32[48,32,128]{2,1,0:T(8,128)S(1)}, u32[]{:S(2)}, u32[]{:S(2)}) async-start(f32[48,32,128]{2,1,0:T(8,128)} %bands.3), calls=%async_computation.1 | async-start | bytes 1572864 | tf_op jit(solution)/shard_map/all_to_all | solution.py:541

commit v4 on v3

--- a/solution.py
+++ b/solution.py
@@ -19,6 +19,7 @@
 ROWS = CY + 2 * HALO
 COLS = CX * CY
 BLOCK = 4096
+FLOAT8 = jnp.float8_e4m3fn
 MIB = 1024 * 1024
 
 VMEM = pl.BlockSpec(memory_space=pltpu.VMEM)
@@ -402,23 +403,25 @@
     living = living_of(count, block)
     moving = velocities[...]
     energy = living * (moving[0] * moving[0] + moving[1] * moving[1] + moving[2] * moving[2]) / 3.0
-    lanes = lax.broadcasted_iota(jnp.int16, (NZ, block), 0)
-    mask = lanes == lane[...].astype(jnp.int16)
-    high = energy.astype(jnp.bfloat16)
-    low = (energy - high.astype(jnp.float32)).astype(jnp.bfloat16)
-    weighted = jnp.concatenate(
-        [jnp.where(mask, w, jnp.bfloat16(0)) for w in (living.astype(jnp.bfloat16), high, low)], 0
-    )
+    mask = lane_mask(lane[...])
+    rows = [jnp.where(mask, living, 0.0).astype(FLOAT8)]
+    rest = jnp.where(mask, 8.0 * energy, 0.0)
+    for _ in range(3):
+        piece = rest.astype(FLOAT8)
+        rows.append(piece)
+        rest = 16.0 * (rest - piece.astype(jnp.float32))
+    weighted = jnp.concatenate(rows, 0)
     columns = sums.shape[1]
     place = face_column(column[...]) if faces else inner_column(column[...])
     term = lax.dot_general(
         weighted,
-        column_hot(place, columns),
+        column_hot(place, columns).astype(FLOAT8),
         (((1,), (1,)), ((), ())),
         preferred_element_type=jnp.float32,
     )
     sums[:NZ] += term[:NZ]
-    sums[NZ:] += term[NZ : 2 * NZ] + term[2 * NZ :]
+    small = term[2 * NZ : 3 * NZ] * (1 / 128) + term[3 * NZ :] * (1 / 2048)
+    sums[NZ:] += term[NZ : 2 * NZ] * 0.125 + small
 
     @pl.when(pl.program_id(0) == pl.num_programs(0) - 1)
     def _():
@@ -492,11 +495,11 @@
     def _():
         rest = te[...].T * 8.0
         for k in range(3):
-            piece = rest.astype(jnp.float8_e4m3fn)
+            piece = rest.astype(FLOAT8)
             pair[k * NZ : (k + 1) * NZ] = piece
             rest = (rest - piece.astype(jnp.float32)) * 16.0
 
-    hot = column_hot(column[...], COLS).astype(jnp.float8_e4m3fn)
+    hot = column_hot(column[...], COLS).astype(FLOAT8)
     rows = jnp.dot(pair[...], hot, preferred_element_type=jnp.float32)
     value = rows[:NZ] * 0.125 + (rows[NZ : 2 * NZ] * (1 / 128) + rows[2 * NZ :] * (1 / 2048))
     picked = jnp.where(lane_mask(lane[...]), value, 0.0)
@@ -521,7 +524,7 @@
             blocks_of((3, 1), block),
         ],
         out_specs=blocks_of((3, 1), block),
-        scratch_shapes=[pltpu.VMEM((3 * NZ, COLS), jnp.float8_e4m3fn)],
+        scratch_shapes=[pltpu.VMEM((3 * NZ, COLS), FLOAT8)],
         compiler_params=params(48),
         cost_estimate=pl.CostEstimate(
             flops=4 * slots * COLS * NZ, bytes_accessed=4_000_000, transcendentals=0

time: 104 us -> 102 us (0.981)
  Pallas kernels: 66.7 us -> 62.2 us
  waiting for transfers between devices: 2.61 us -> 5.71 us
    pallas_call x2, Pallas kernels: 27.1 us -> 22.7 us  [bin_atoms(): pl.pallas_call(functools.partial(bin_kernel, block, faces), grid=(slots /...]
    ppermute x4, waiting for transfers between devices: 2.6 us -> 5.21 us  [to_both_sides(): lax.ppermute(tail, axis, [(i, (i + 1) % count) for i in range(count)])]
  transfers between devices with their start and end apart: 10 -> 10, of which waited for: 1 -> 3; matrix products, arithmetic and copies ran while one was open for 0% -> 0% of each run, Pallas kernels for 54% -> 51%
where the time goes in v4:
time: 102 us; the launch traced here: 101 us
  Pallas kernels  62.2 us (61%)
  starting transfers between devices  30.8 us (30%)
  waiting for transfers between devices  5.71 us (6%)
  between operations  1.43 us (1%)
    pallas_call x2, Pallas kernels, bin_atoms(): pl.pallas_call(functools.partial(bin_kernel, block, faces), grid=(slots /...  22.7 us
    ppermute x4, starting transfers between devices, to_both_sides(): lax.ppermute(head, axis, [((i + 1) % count, i) for i in range(count)])  16.4 us
    pallas_call x1, Pallas kernels, read_atoms(): pl.pallas_call(functools.partial(read_kernel, block), grid=(slots // bloc...  14.1 us
    all_to_all x2, starting transfers between devices, exchanged(): return lax.all_to_all(blocks, 'gy', split_axis=0, concat_axis=0, tiled=True)  11.4 us
    pallas_call x1, Pallas kernels, first_interior(): pl.pallas_call(functools.partial(first_interior_kernel, parts), out_shape...  8.17 us
    pallas_call x2, Pallas kernels, bands(): pl.pallas_call(functools.partial(bands_kernel, last), out_shape=shapes, i...  6.95 us
    pallas_call x1, Pallas kernels, second_interior(): pl.pallas_call(second_interior_kernel, out_shape=f32(CX, ROWS, NZ), in_sp...  6.39 us
    ppermute x4, waiting for transfers between devices, to_both_sides(): lax.ppermute(tail, axis, [(i, (i + 1) % count) for i in range(count)])  5.21 us
  transfers between devices with their start and end apart: 10, of which 3 were waited for; matrix products, arithmetic and copies ran while one was open for 0% of the time, Pallas kernels for 51%

profile of v4, /device:TPU:4, one launch (start us, length us, event | category | flops | bytes accessed | tf_op | source)
XLA Modules:
  0.0 101.2 jit_solution(15636698119833187907)
XLA Ops:
  0.6 2.7 %widen.1 = f32[8,12,40,128]{3,2,1,0:T(8,128)} custom-call(f32[6,256,128]{2,1,0:T(8,128)} %te.1, f32[6,256,128]{2,1,0:T(8,128)} %source.1), custom_call_target="tpu_custom_call" | custom-call | bytes 4000000 | tf_op jit(solution)/shard_map/widen/pallas_call | solution.py:327
  3.4 6.0 %all-to-all-start = ((f32[96,40,128]{2,1,0:T(8,128)}), f32[96,40,128]{2,1,0:T(8,128)}, u32[]{:S(2)}, u32[]{:S(2)}) async-start(f32[96,40,128]{2,1,0:T(8,128)} %bitcast.25), calls=%async_computation | async-start | bytes 3932160 | tf_op jit(solution)/shard_map/all_to_all | solution.py:544
  10.0 0.0 copy-start.2
  10.0 0.0 copy-start.4
  10.0 0.0 copy-start.5
  10.0 7.9 %bin_faces.1 = (f32[48,8,128]{2,1,0:T(8,128)}, f32[48,8,128]{2,1,0:T(8,128)}, f32[12,3,8,128]{3,2,1,0:T(8,128)}, f32[12,3,8,128]{3,2,1,0:T(8,128)}) custom-call(s32[1,1]{1,0:T(1,128)S(6)} %copy.11.count, s32[1,16384]{1,0:T(1,128)} %bitcast.19, s32[1,16384]{1,0:T(1,128)} %bitcast.22, f32[3,1,16384]{2,1,0:T(1,128)} %bitcast.15), custom_call_target="tpu_custom_call" | custom-call | flops 4831838208 | bytes 4000000 | tf_op jit(solution)/shard_map/bin_faces/pallas_call | solution.py:478
  17.9 2.0 %collective-permute-start = (f32[12,3,8,128]{3,2,1,0:T(8,128)}, f32[12,3,8,128]{3,2,1,0:T(8,128)S(1)}, u32[]{:S(2)}, u32[]{:S(2)}) collective-permute-start(f32[12,3,8,128]{3,2,1,0:T(8,128)} %get-tuple-element.25), channel_id=1, source_target_pairs={{0,1},{1,2},{2,3},{3,4},{4,5},{5,6},{6,7},{7,0},{8,9},{9,10},{10,1... | collective-permute-start | bytes 442376 | tf_op jit(solution)/shard_map/ppermute | solution.py:538
  20.0 0.0 copy-start
  20.0 0.0 copy-start.1
  20.0 2.2 %collective-permute-start.1 = (f32[12,3,8,128]{3,2,1,0:T(8,128)}, f32[12,3,8,128]{3,2,1,0:T(8,128)S(1)}, u32[]{:S(2)}, u32[]{:S(2)}) collective-permute-start(f32[12,3,8,128]{3,2,1,0:T(8,128)} %get-tuple-element.26), channel_id=1, source_target_pairs={{1,0},{2,1},{3,2},{4,3},{5,4},{6,5},{7,6},{0,7},{9,8},{10,9},{11,1... | collective-permute-start | bytes 442376 | tf_op jit(solution)/shard_map/ppermute | solution.py:539
  22.2 0.0 copy-done.2
  22.2 0.0 copy-done.4
  22.2 0.0 copy-done.5
  22.2 14.7 %bin_inner.1 = (f32[48,24,128]{2,1,0:T(8,128)S(1)}, f32[48,24,128]{2,1,0:T(8,128)S(1)}) custom-call(s32[1,1]{1,0:T(1,128)S(6)} %copy.11.count, s32[1,16384]{1,0:T(1,128)S(1)} %bitcast.20, s32[1,16384]{1,0:T(1,128)S(1)} %bitcast.23, f32[3,1,16384]{2,1,0:T(1,128)S(1)} %bitcast.16), custom_call_target="tpu_custom_call" | custom-call | flops 14495514624 | bytes 4000000 | tf_op jit(solution)/shard_map/bin_inner/pallas_call | solution.py:478
  36.9 2.6 %collective-permute-done.refs_4_ = f32[12,3,8,128]{3,2,1,0:T(8,128)S(1)} collective-permute-done((f32[12,3,8,128]{3,2,1,0:T(8,128)}, f32[12,3,8,128]{3,2,1,0:T(8,128)S(1)}, u32[]{:S(2)}, u32[]{:S(2)}) %collective-permute-start) | collective-permute-done | bytes 147488 | tf_op jit(solution)/shard_map/ppermute | solution.py:538
  39.5 0.5 collective-permute-done.1.refs_5_
  40.0 0.0 all-to-all-done.refs_6_.fields
  40.0 0.0 copy-done
  40.0 0.0 copy-done.1
  40.0 1.2 %edges.1 = (f32[16,40,128]{2,1,0:T(8,128)S(1)}, f32[10,40,128]{2,1,0:T(8,128)S(1)}, f32[10,40,128]{2,1,0:T(8,128)S(1)}, f32[2,48,8,128]{3,2,1,0:T(8,128)S(1)}) custom-call(f32[48,8,128]{2,1,0:T(8,128)S(1)} %copy-done, f32[48,8,128]{2,1,0:T(8,128)S(1)} %copy-done.1, f32[48,24,128]{2,1,0:T(8,128)S(1)} %get-tuple-element.23.refs_2_.load_in, ...), custom_call_target="tpu_custom_call" | custom-call | bytes 2000000 | tf_op jit(solution)/shard_map/edges/pallas_call | solution.py:280
  41.2 0.1 collective-permute-start.2
  41.3 5.3 %collective-permute-start.3 = (f32[10,40,128]{2,1,0:T(8,128)S(1)}, f32[10,40,128]{2,1,0:T(8,128)S(1)}, u32[]{:S(2)}, u32[]{:S(2)}) collective-permute-start(f32[10,40,128]{2,1,0:T(8,128)S(1)} %get-tuple-element.32), channel_id=1, source_target_pairs={{8,0},{16,8},{24,16},{32,24},{40,32},{48,40},{56,48},{64,56},{72,6... | collective-permute-start | bytes 614408 | tf_op jit(solution)/shard_map/ppermute | solution.py:539
  46.7 0.1 add_convert_fusion.place
  46.7 8.2 %first_interior.1 = (f32[48,40,128]{2,1,0:T(8,128)S(1)}, f32[48,40,128]{2,1,0:T(8,128)S(1)}, f32[48,40,128]{2,1,0:T(8,128)S(1)}) custom-call(f32[48,8,128]{2,1,0:T(8,128)S(1)} %copy-done, f32[48,8,128]{2,1,0:T(8,128)S(1)} %copy-done.1, f32[48,24,128]{2,1,0:T(8,128)S(1)} %get-tuple-element.23.refs_2_.load_in, ...), custom_call_target="tpu_custom_call" | custom-call | bytes 30000000 | tf_op jit(solution)/shard_map/first_interior/pallas_call | solution.py:148
  54.9 0.0 collective-permute-done.2.te_lo.lo
  54.9 0.0 collective-permute-done.3.te_hi.hi
  54.9 3.1 %bands.2 = (f32[48,32,128]{2,1,0:T(8,128)S(1)}, f32[24,8,128]{2,1,0:T(8,128)S(1)}, f32[24,8,128]{2,1,0:T(8,128)S(1)}) custom-call(s32[2]{0:T(128)S(1)} %add_convert_fusion.place, f32[16,40,128]{2,1,0:T(8,128)S(1)} %get-tuple-element.27.te, f32[48,40,128]{2,1,0:T(8,128)S(1)} %get-tuple-element.29.heat, f32[48,40,128]{2,1,0:T(8,128)S(1)} %get-tuple-element.30.load, ...), custom_call_target="tpu_custom_call" | custom-call | bytes 8000000 | tf_op jit(solution)/shard_map/bands/pallas_call | solution.py:219
  58.0 0.7 collective-permute-start.4
  58.7 3.5 %collective-permute-start.5 = (f32[24,8,128]{2,1,0:T(8,128)S(1)}, f32[24,8,128]{2,1,0:T(8,128)S(1)}, u32[]{:S(2)}, u32[]{:S(2)}) collective-permute-start(f32[24,8,128]{2,1,0:T(8,128)S(1)} %get-tuple-element.36), channel_id=1, source_target_pairs={{1,0},{2,1},{3,2},{4,3},{5,4},{6,5},{7,6},{0,7},{9,8},{10,9},{11,1... | collective-permute-start | bytes 294920 | tf_op jit(solution)/shard_map/ppermute | solution.py:539
  62.2 2.6 %collective-permute-done.4.before = f32[24,8,128]{2,1,0:T(8,128)S(1)} collective-permute-done((f32[24,8,128]{2,1,0:T(8,128)S(1)}, f32[24,8,128]{2,1,0:T(8,128)S(1)}, u32[]{:S(2)}, u32[]{:S(2)}) %collective-permute-start.4) | collective-permute-done | bytes 98336 | tf_op jit(solution)/shard_map/ppermute | solution.py:538
  64.8 0.0 collective-permute-done.5.after
  64.8 0.1 second_brick.1
  64.9 0.3 collective-permute-start.6
  65.1 5.3 %collective-permute-start.7 = (f32[4,40,128]{2,1,0:T(8,128)S(1)}, f32[4,40,128]{2,1,0:T(8,128)S(1)}, u32[]{:S(2)}, u32[]{:S(2)}) collective-permute-start(f32[4,40,128]{2,1,0:T(8,128)S(1)} %get-tuple-element.39), channel_id=1, source_target_pairs={{8,0},{16,8},{24,16},{32,24},{40,32},{48,40},{56,48},{64,56},{72,6... | collective-permute-start | bytes 245768 | tf_op jit(solution)/shard_map/ppermute | solution.py:539
  70.5 6.4 %interior.1.inner = f32[48,40,128]{2,1,0:T(8,128)S(1)} custom-call(f32[48,40,128]{2,1,0:T(8,128)S(1)} %get-tuple-element.37.te, f32[48,40,128]{2,1,0:T(8,128)S(1)} %get-tuple-element.29.heat, f32[48,40,128]{2,1,0:T(8,128)S(1)} %get-tuple-element.30.load), custom_call_target="tpu_custom_call" | custom-call | bytes 25000000 | tf_op jit(solution)/shard_map/interior/pallas_call | solution.py:99
  76.9 0.0 copy-start.3
  76.9 0.0 collective-permute-done.6.te_lo
  76.9 0.0 collective-permute-done.7.te_hi
  76.9 3.9 %bands.3 = f32[48,32,128]{2,1,0:T(8,128)} custom-call(s32[2]{0:T(128)S(1)} %add_convert_fusion.place, f32[48,40,128]{2,1,0:T(8,128)S(1)} %get-tuple-element.37.te, f32[48,40,128]{2,1,0:T(8,128)S(1)} %get-tuple-element.29.heat, f32[48,40,128]{2,1,0:T(8,128)S(1)} %get-tuple-element.30.load, f32[4,40,128]{2,1,0:T(8,128)S(1)} %collective-permute-done.6.te_lo, ...), custom_call_target="tpu_custom_call" | custom-call | bytes 8000000 | tf_op jit(solution)/shard_map/bands/pallas_call | solution.py:219
  80.8 5.4 %all-to-all-start.1 = ((f32[48,32,128]{2,1,0:T(8,128)}), f32[48,32,128]{2,1,0:T(8,128)S(1)}, u32[]{:S(2)}, u32[]{:S(2)}) async-start(f32[48,32,128]{2,1,0:T(8,128)} %bands.3), calls=%async_computation.1 | async-start | bytes 1572864 | tf_op jit(solution)/shard_map/all_to_all | solution.py:544
  86.2 0.0 copy-done.3
  86.2 14.1 %read_atoms.1 = f32[3,1,16384]{2,1,0:T(1,128)} custom-call(s32[1,1]{1,0:T(1,128)S(6)} %copy.11.count, f32[1536,128]{1,0:T(8,128)} %bitcast.9.te, s32[1,16384]{1,0:T(1,128)S(1)} %bitcast.21, s32[1,16384]{1,0:T(1,128)S(1)} %bitcast.24, f32[3,1,16384]{2,1,0:T(1,128)S(1)} %bitcast.17, f32[3,1,16384]{2,1,0:T(1,128)S(1)} %bitcast.18), custom_call_target="tpu_custom_call" | custom-call | flops 12884901888 | bytes 4000000 | tf_op jit(solution)/shard_map/read_atoms/pallas_call | solution.py:514
  100.3 0.0 all-to-all-done.1
  100.3 0.9 copy.9
Async XLA Ops:
  3.4 36.6 %all-to-all-start = ((f32[96,40,128]{2,1,0:T(8,128)}), f32[96,40,128]{2,1,0:T(8,128)}, u32[]{:S(2)}, u32[]{:S(2)}) async-start(f32[96,40,128]{2,1,0:T(8,128)} %bitcast.25), calls=%async_computation | async-start | bytes 3932160 | tf_op jit(solution)/shard_map/all_to_all | solution.py:544
  10.0 12.2 %copy-start.2 = (f32[3,1,1,16384]{3,2,1,0:T(1,128)S(1)}, f32[3,1,1,16384]{3,2,1,0:T(1,128)}, u32[]{:S(2)}) copy-start(f32[3,1,1,16384]{3,2,1,0:T(1,128)} %param.9) | copy-start | bytes 589828
  10.0 12.2 %copy-start.4 = (s32[1,1,16384]{2,1,0:T(1,128)S(1)}, s32[1,1,16384]{2,1,0:T(1,128)}, u32[]{:S(2)}) copy-start(s32[1,1,16384]{2,1,0:T(1,128)} %param.11) | copy-start | bytes 196612
  10.0 12.2 %copy-start.5 = (s32[1,1,16384]{2,1,0:T(1,128)S(1)}, s32[1,1,16384]{2,1,0:T(1,128)}, u32[]{:S(2)}) copy-start(s32[1,1,16384]{2,1,0:T(1,128)} %param.12) | copy-start | bytes 196612
  17.9 21.6 %collective-permute-start = (f32[12,3,8,128]{3,2,1,0:T(8,128)}, f32[12,3,8,128]{3,2,1,0:T(8,128)S(1)}, u32[]{:S(2)}, u32[]{:S(2)}) collective-permute-start(f32[12,3,8,128]{3,2,1,0:T(8,128)} %get-tuple-element.25), channel_id=1, source_target_pairs={{0,1},{1,2},{2,3},{3,4},{4,5},{5,6},{6,7},{7,0},{8,9},{9,10},{10,1... | collective-permute-start | bytes 442376 | tf_op jit(solution)/shard_map/ppermute | solution.py:538
  20.0 20.0 %copy-start = (f32[48,8,128]{2,1,0:T(8,128)S(1)}, f32[48,8,128]{2,1,0:T(8,128)}, u32[]{:S(2)}) copy-start(f32[48,8,128]{2,1,0:T(8,128)} %get-tuple-element.21.refs_0_.own_head) | copy-start | bytes 589828
  20.0 20.0 %copy-start.1 = (f32[48,8,128]{2,1,0:T(8,128)S(1)}, f32[48,8,128]{2,1,0:T(8,128)}, u32[]{:S(2)}) copy-start(f32[48,8,128]{2,1,0:T(8,128)} %get-tuple-element.22.refs_1_.own_tail) | copy-start | bytes 589828
  20.0 20.0 %collective-permute-start.1 = (f32[12,3,8,128]{3,2,1,0:T(8,128)}, f32[12,3,8,128]{3,2,1,0:T(8,128)S(1)}, u32[]{:S(2)}, u32[]{:S(2)}) collective-permute-start(f32[12,3,8,128]{3,2,1,0:T(8,128)} %get-tuple-element.26), channel_id=1, source_target_pairs={{1,0},{2,1},{3,2},{4,3},{5,4},{6,5},{7,6},{0,7},{9,8},{10,9},{11,1... | collective-permute-start | bytes 442376 | tf_op jit(solution)/shard_map/ppermute | solution.py:539
  41.2 13.7 %collective-permute-start.2 = (f32[10,40,128]{2,1,0:T(8,128)S(1)}, f32[10,40,128]{2,1,0:T(8,128)S(1)}, u32[]{:S(2)}, u32[]{:S(2)}) collective-permute-start(f32[10,40,128]{2,1,0:T(8,128)S(1)} %get-tuple-element.31), channel_id=1, source_target_pairs={{0,8},{8,16},{16,24},{24,32},{32,40},{40,48},{48,56},{56,64},{64,7... | collective-permute-start | bytes 614408 | tf_op jit(solution)/shard_map/ppermute | solution.py:538
  41.3 13.6 %collective-permute-start.3 = (f32[10,40,128]{2,1,0:T(8,128)S(1)}, f32[10,40,128]{2,1,0:T(8,128)S(1)}, u32[]{:S(2)}, u32[]{:S(2)}) collective-permute-start(f32[10,40,128]{2,1,0:T(8,128)S(1)} %get-tuple-element.32), channel_id=1, source_target_pairs={{8,0},{16,8},{24,16},{32,24},{40,32},{48,40},{56,48},{64,56},{72,6... | collective-permute-start | bytes 614408 | tf_op jit(solution)/shard_map/ppermute | solution.py:539
  58.0 6.8 %collective-permute-start.4 = (f32[24,8,128]{2,1,0:T(8,128)S(1)}, f32[24,8,128]{2,1,0:T(8,128)S(1)}, u32[]{:S(2)}, u32[]{:S(2)}) collective-permute-start(f32[24,8,128]{2,1,0:T(8,128)S(1)} %get-tuple-element.35), channel_id=1, source_target_pairs={{0,1},{1,2},{2,3},{3,4},{4,5},{5,6},{6,7},{7,0},{8,9},{9,10},{10,1... | collective-permute-start | bytes 294920 | tf_op jit(solution)/shard_map/ppermute | solution.py:538
  58.7 6.1 %collective-permute-start.5 = (f32[24,8,128]{2,1,0:T(8,128)S(1)}, f32[24,8,128]{2,1,0:T(8,128)S(1)}, u32[]{:S(2)}, u32[]{:S(2)}) collective-permute-start(f32[24,8,128]{2,1,0:T(8,128)S(1)} %get-tuple-element.36), channel_id=1, source_target_pairs={{1,0},{2,1},{3,2},{4,3},{5,4},{6,5},{7,6},{0,7},{9,8},{10,9},{11,1... | collective-permute-start | bytes 294920 | tf_op jit(solution)/shard_map/ppermute | solution.py:539
  64.9 12.0 %collective-permute-start.6 = (f32[4,40,128]{2,1,0:T(8,128)S(1)}, f32[4,40,128]{2,1,0:T(8,128)S(1)}, u32[]{:S(2)}, u32[]{:S(2)}) collective-permute-start(f32[4,40,128]{2,1,0:T(8,128)S(1)} %get-tuple-element.38), channel_id=1, source_target_pairs={{0,8},{8,16},{16,24},{24,32},{32,40},{40,48},{48,56},{56,64},{64,7... | collective-permute-start | bytes 245768 | tf_op jit(solution)/shard_map/ppermute | solution.py:538
  65.1 11.8 %collective-permute-start.7 = (f32[4,40,128]{2,1,0:T(8,128)S(1)}, f32[4,40,128]{2,1,0:T(8,128)S(1)}, u32[]{:S(2)}, u32[]{:S(2)}) collective-permute-start(f32[4,40,128]{2,1,0:T(8,128)S(1)} %get-tuple-element.39), channel_id=1, source_target_pairs={{8,0},{16,8},{24,16},{32,24},{40,32},{48,40},{56,48},{64,56},{72,6... | collective-permute-start | bytes 245768 | tf_op jit(solution)/shard_map/ppermute | solution.py:539
  76.9 9.3 %copy-start.3 = (f32[3,1,1,16384]{3,2,1,0:T(1,128)S(1)}, f32[3,1,1,16384]{3,2,1,0:T(1,128)}, u32[]{:S(2)}) copy-start(f32[3,1,1,16384]{3,2,1,0:T(1,128)} %param.10) | copy-start | bytes 589828
  80.8 19.5 %all-to-all-start.1 = ((f32[48,32,128]{2,1,0:T(8,128)}), f32[48,32,128]{2,1,0:T(8,128)S(1)}, u32[]{:S(2)}, u32[]{:S(2)}) async-start(f32[48,32,128]{2,1,0:T(8,128)} %bands.3), calls=%async_computation.1 | async-start | bytes 1572864 | tf_op jit(solution)/shard_map/all_to_all | solution.py:544

commit v5 on v4

--- a/solution.py
+++ b/solution.py
@@ -109,30 +109,13 @@
 
 
 def first_interior_kernel(
-    parts, own_head, own_tail, load_in, kinetic, halo, fields, out, heat, load, *scratch
+    own_head, own_tail, load_in, kinetic, halo, te, source, out, heat, load, first, second
 ):
-    first, second, source, sems = scratch
-    layers = CX // parts
-    fetches = []
-    for j in range(parts):
-        at = 2 * j * layers
-        te_here = first.at[pl.ds(1 + j * layers, layers)]
-        source_here = source.at[pl.ds(j * layers, layers)]
-        for k, here in enumerate((te_here, source_here)):
-            there = fields.at[pl.ds(at + k * layers, layers)]
-            fetches.append(pltpu.make_async_copy(there, here, sems.at[2 * j + k]))
-    for fetch in fetches:
-        fetch.start()
-    for i in range(parts):
-        span = pl.ds(i * layers, layers)
+    first[pl.ds(1, CX)] = te[...]
+    for i in range(CX // 8):
+        span = pl.ds(8 * i, 8)
         load[span] = side_by_side(own_head, load_in, own_tail, halo, span, 0)
-    for fetch in fetches:
-        fetch.wait()
-    for i in range(parts):
-        span = pl.ds(i * layers, layers)
-        heat[span] = source[span] + side_by_side(
-            own_head, kinetic, own_tail, halo, span, 1
-        )
+        heat[span] = source[span] + side_by_side(own_head, kinetic, own_tail, halo, span, 1)
     interior_steps(first, second, heat, load, out)
 
 
@@ -143,16 +126,14 @@
     )
 
 
-def first_interior(parts, *arrays):
+def first_interior(*arrays):
     whole = f32(CX, ROWS, NZ)
     return pl.pallas_call(
-        functools.partial(first_interior_kernel, parts),
+        first_interior_kernel,
         out_shape=[whole] * 3,
-        in_specs=[VMEM] * 5 + [ANY],
+        in_specs=[VMEM] * 7,
         out_specs=[VMEM] * 3,
-        scratch_shapes=[padded_brick()] * 2
-        + [pltpu.VMEM((CX, ROWS, NZ), jnp.float32)]
-        + [pltpu.SemaphoreType.DMA((2 * parts,))],
+        scratch_shapes=[padded_brick()] * 2,
         compiler_params=params(32),
         cost_estimate=pl.CostEstimate(flops=0, bytes_accessed=30_000_000, transcendentals=0),
         name="first_interior",
@@ -227,46 +208,44 @@
     )(place, te, heat, load, te_lo, te_hi, lo, hi, inner)
 
 
-def edges_kernel(parts, *refs):
-    inside, (fields, ends, head, tail, halo, here, source, sems) = refs[:6], refs[6:]
-    own_head, own_tail, load_in, kinetic, before, after = inside
+def unmix_kernel(parts, fields, te, source, sems):
     layers = CX // parts
-    many = 2 * HALO
     fetches = []
-
-    def fetch(there, here):
-        copy = pltpu.make_async_copy(there, here, sems.at[len(fetches)])
-        copy.start()
-        fetches.append(copy)
-
-    for k, first in enumerate((0, CX - many)):
-        layer = first
-        while layer < first + many:
-            part = layer // layers
-            count = min(first + many, (part + 1) * layers) - layer
-            there = fields.at[pl.ds(layer + part * layers, count)]
-            fetch(there, here.at[pl.ds(k * many + layer - first, count)])
-            layer += count
-    for k, first in enumerate((0, CX - NEAR)):
-        layer = first
-        while layer < first + NEAR:
-            part = layer // layers
-            count = min(first + NEAR, (part + 1) * layers) - layer
-            there = fields.at[pl.ds(layer + (part + 1) * layers, count)]
-            fetch(there, source.at[k, pl.ds(layer - first, count)])
-            layer += count
+    for j in range(parts):
+        for k, here in enumerate((te, source)):
+            there = fields.at[pl.ds((2 * j + k) * layers, layers)]
+            fetch = pltpu.make_async_copy(there, here.at[pl.ds(j * layers, layers)], sems.at[j, k])
+            fetch.start()
+            fetches.append(fetch)
+    for fetch in fetches:
+        fetch.wait()
+
+
+def unmixed(parts, fields):
+    return pl.pallas_call(
+        functools.partial(unmix_kernel, parts),
+        out_shape=[f32(CX, ROWS, NZ)] * 2,
+        in_specs=[ANY],
+        out_specs=[VMEM] * 2,
+        scratch_shapes=[pltpu.SemaphoreType.DMA((parts, 2))],
+        compiler_params=params(32),
+        cost_estimate=pl.CostEstimate(flops=0, bytes_accessed=4_000_000, transcendentals=0),
+        name="unmix",
+    )(fields)
+
+
+def edges_kernel(
+    own_head, own_tail, load_in, kinetic, before, after, te, source, head, tail, halo
+):
     before, after = unpack(before), unpack(after)
     gap = jnp.zeros((CX, 2 * HALO - 2 * NEAR, NZ), jnp.float32)
     for field in range(2):
         rows = slice(field * NEAR, field * NEAR + NEAR)
         halo[field] = jnp.concatenate([after[:, rows], gap, before[:, rows]], 1)
-    for copy in fetches:
-        copy.wait()
-    ends[...] = here[...]
-    for k, (target, at) in enumerate(((head, 0), (tail, 2 * many - HALO))):
-        span = pl.ds((0, CX - NEAR)[k], NEAR)
-        target[:HALO] = here[pl.ds(at, HALO)]
-        target[pl.ds(HALO, NEAR)] = source[k] + side_by_side(
+    for target, first, near in ((head, 0, 0), (tail, CX - HALO, CX - NEAR)):
+        span = pl.ds(near, NEAR)
+        target[:HALO] = te[pl.ds(first, HALO)]
+        target[pl.ds(HALO, NEAR)] = source[span] + side_by_side(
             own_head, kinetic, own_tail, halo, span, 1
         )
         target[pl.ds(HALO + NEAR, NEAR)] = side_by_side(
@@ -274,19 +253,13 @@
         )
 
 
-def edges(parts, *arrays):
+def edges(*arrays):
     edge = f32(HALO + 2 * NEAR, ROWS, NZ)
-    ends = (4 * HALO, ROWS, NZ)
-    return pl.pallas_call(
-        functools.partial(edges_kernel, parts),
-        out_shape=[f32(*ends), edge, edge, f32(2, CX, 2 * HALO, NZ)],
-        in_specs=[VMEM] * 6 + [ANY],
-        out_specs=[VMEM] * 4,
-        scratch_shapes=[
-            pltpu.VMEM(ends, jnp.float32),
-            pltpu.VMEM((2, NEAR, ROWS, NZ), jnp.float32),
-            pltpu.SemaphoreType.DMA((16,)),
-        ],
+    return pl.pallas_call(
+        edges_kernel,
+        out_shape=[edge, edge, f32(2, CX, 2 * HALO, NZ)],
+        in_specs=[VMEM] * 8,
+        out_specs=[VMEM] * 3,
         compiler_params=params(32),
         cost_estimate=pl.CostEstimate(flops=0, bytes_accessed=2_000_000, transcendentals=0),
         name="edges",
@@ -560,12 +533,11 @@
     position = lax.axis_index("gx")
     final = lax.axis_size("gx") - 1
     place = jnp.stack([position == 0, position == final]).astype(jnp.int32)
-    ends, head, tail, halo = edges(
-        parts, own_head, own_tail, load, kinetic, before, after, fields
-    )
+    te, source = unmixed(parts, fields)
+    head, tail, halo = edges(own_head, own_tail, load, kinetic, before, after, te, source)
     lo, hi = to_both_sides(head, tail, "gx")
-    inner, heat, load = first_interior(parts, own_head, own_tail, load, kinetic, halo, fields)
-    middle, head, tail = bands(False, place, ends, heat, load, lo, hi, lo, hi, inner)
+    inner, heat, load = first_interior(own_head, own_tail, load, kinetic, halo, te, source)
+    middle, head, tail = bands(False, place, te, heat, load, lo, hi, lo, hi, inner)
 
     before, after = to_both_sides(head, tail, "gy")
     te, head, tail = second_brick(middle, before, after)

time: 102 us -> 105 us (1.029)
  local copies, waits for them, and re-layouts: 0.98 us -> 4.59 us
  waiting for transfers between devices: 5.71 us -> 4.08 us
    unnamed x12 -> x26, local copies, waits for them, and re-layouts: 0.03 us -> 3.65 us
    ppermute x4, waiting for transfers between devices: 5.21 us -> 3.58 us  [to_both_sides(): lax.ppermute(tail, axis, [(i, (i + 1) % count) for i in range(count)])]
    pallas_call x2 -> x3, Pallas kernels: 9.38 us -> 10.2 us  [the longest x1 6.59 us: first_interior(): pl.pallas_call(first_interior_kernel, out_shape=[whole] * 3, in_specs=[VM...]
  transfers between devices with their start and end apart: 10 -> 10, of which waited for: 3 -> 3; matrix products, arithmetic and copies ran while one was open for 0% -> 0% of each run, Pallas kernels for 51% -> 49%
where the time goes in v5:
time: 105 us; the launch traced here: 104 us
  Pallas kernels  63 us (60%)
  starting transfers between devices  30.7 us (29%)
  local copies, waits for them, and re-layouts  4.59 us (4%)
  waiting for transfers between devices  4.08 us (4%)
  between operations  1.49 us (1%)
    pallas_call x2, Pallas kernels, bin_atoms(): pl.pallas_call(functools.partial(bin_kernel, block, faces), grid=(slots /...  22.7 us
    ppermute x4, starting transfers between devices, to_both_sides(): lax.ppermute(head, axis, [((i + 1) % count, i) for i in range(count)])  16.4 us
    pallas_call x1, Pallas kernels, read_atoms(): pl.pallas_call(functools.partial(read_kernel, block), grid=(slots // bloc...  14 us
    all_to_all x2, starting transfers between devices, exchanged(): return lax.all_to_all(blocks, 'gy', split_axis=0, concat_axis=0, tiled=True)  11.4 us
    pallas_call x2, Pallas kernels, bands(): pl.pallas_call(functools.partial(bands_kernel, last), out_shape=shapes, i...  6.96 us
    pallas_call x1, Pallas kernels, first_interior(): pl.pallas_call(first_interior_kernel, out_shape=[whole] * 3, in_specs=[VM...  6.59 us
    pallas_call x1, Pallas kernels, second_interior(): pl.pallas_call(second_interior_kernel, out_shape=f32(CX, ROWS, NZ), in_sp...  6.39 us
    unnamed x26, local copies, waits for them, and re-layouts  3.65 us
  transfers between devices with their start and end apart: 10, of which 3 were waited for; matrix products, arithmetic and copies ran while one was open for 0% of the time, Pallas kernels for 49%

profile of v5, /device:TPU:4, one launch (start us, length us, event | category | flops | bytes accessed | tf_op | source)
XLA Modules:
  0.0 104.0 jit_solution(4941517355161887931)
XLA Ops:
  0.6 2.7 %widen.1 = f32[8,12,40,128]{3,2,1,0:T(8,128)} custom-call(f32[6,256,128]{2,1,0:T(8,128)} %te.1, f32[6,256,128]{2,1,0:T(8,128)} %source.1), custom_call_target="tpu_custom_call" | custom-call | bytes 4000000 | tf_op jit(solution)/shard_map/widen/pallas_call | solution.py:300
  3.4 6.0 %all-to-all-start = ((f32[96,40,128]{2,1,0:T(8,128)}), f32[96,40,128]{2,1,0:T(8,128)}, u32[]{:S(2)}, u32[]{:S(2)}) async-start(f32[96,40,128]{2,1,0:T(8,128)} %bitcast.25), calls=%async_computation | async-start | bytes 3932160 | tf_op jit(solution)/shard_map/all_to_all | solution.py:517
  10.0 0.0 copy-start.6
  10.0 0.0 copy-start.9
  10.0 0.0 copy-start.11
  10.0 8.0 %bin_faces.1 = (f32[48,8,128]{2,1,0:T(8,128)}, f32[48,8,128]{2,1,0:T(8,128)}, f32[12,3,8,128]{3,2,1,0:T(8,128)}, f32[12,3,8,128]{3,2,1,0:T(8,128)}) custom-call(s32[1,1]{1,0:T(1,128)S(6)} %copy.11.count, s32[1,16384]{1,0:T(1,128)} %bitcast.19, s32[1,16384]{1,0:T(1,128)} %bitcast.22, f32[3,1,16384]{2,1,0:T(1,128)} %bitcast.15), custom_call_target="tpu_custom_call" | custom-call | flops 4831838208 | bytes 4000000 | tf_op jit(solution)/shard_map/bin_faces/pallas_call | solution.py:451
  18.0 2.0 %collective-permute-start = (f32[12,3,8,128]{3,2,1,0:T(8,128)}, f32[12,3,8,128]{3,2,1,0:T(8,128)}, u32[]{:S(2)}, u32[]{:S(2)}) collective-permute-start(f32[12,3,8,128]{3,2,1,0:T(8,128)} %get-tuple-element.27), channel_id=1, source_target_pairs={{0,1},{1,2},{2,3},{3,4},{4,5},{5,6},{6,7},{7,0},{8,9},{9,10},{10,1... | collective-permute-start | bytes 442376 | tf_op jit(solution)/shard_map/ppermute | solution.py:511
  20.0 2.1 %collective-permute-start.1 = (f32[12,3,8,128]{3,2,1,0:T(8,128)}, f32[12,3,8,128]{3,2,1,0:T(8,128)}, u32[]{:S(2)}, u32[]{:S(2)}) collective-permute-start(f32[12,3,8,128]{3,2,1,0:T(8,128)} %get-tuple-element.28), channel_id=1, source_target_pairs={{1,0},{2,1},{3,2},{4,3},{5,4},{6,5},{7,6},{0,7},{9,8},{10,9},{11,1... | collective-permute-start | bytes 442376 | tf_op jit(solution)/shard_map/ppermute | solution.py:512
  22.1 0.0 copy-done.6
  22.1 0.0 copy-done.9
  22.1 0.0 copy-done.11
  22.1 14.7 %bin_inner.1 = (f32[48,24,128]{2,1,0:T(8,128)S(1)}, f32[48,24,128]{2,1,0:T(8,128)S(1)}) custom-call(s32[1,1]{1,0:T(1,128)S(6)} %copy.11.count, s32[1,16384]{1,0:T(1,128)S(1)} %bitcast.20, s32[1,16384]{1,0:T(1,128)S(1)} %bitcast.23, f32[3,1,16384]{2,1,0:T(1,128)S(1)} %bitcast.16), custom_call_target="tpu_custom_call" | custom-call | flops 14495514624 | bytes 4000000 | tf_op jit(solution)/shard_map/bin_inner/pallas_call | solution.py:451
  36.8 0.0 copy-start
  36.8 0.0 copy-start.2
  36.9 0.0 all-to-all-done.fields
  36.9 1.8 %unmix.1 = (f32[48,40,128]{2,1,0:T(8,128)S(1)}, f32[48,40,128]{2,1,0:T(8,128)S(1)}) custom-call(f32[96,40,128]{2,1,0:T(8,128)} %all-to-all-done.fields), custom_call_target="tpu_custom_call" | custom-call | bytes 4000000 | tf_op jit(solution)/shard_map/unmix/pallas_call | solution.py:225
  38.6 1.0 collective-permute-done.before
  39.6 0.5 collective-permute-done.1.after
  40.1 0.0 copy-done
  40.1 0.0 copy-done.2
  40.1 1.8 %edges.1 = (f32[10,40,128]{2,1,0:T(8,128)}, f32[10,40,128]{2,1,0:T(8,128)}, f32[2,48,8,128]{3,2,1,0:T(8,128)S(1)}) custom-call(f32[48,8,128]{2,1,0:T(8,128)S(1)} %copy-done, f32[48,8,128]{2,1,0:T(8,128)S(1)} %copy-done.2, f32[48,24,128]{2,1,0:T(8,128)S(1)} %get-tuple-element.25.load_in, f32[48,24,128]{2,1,0:T(8,128)S(1)} %get-tuple-element.26.kinetic, ...), custom_call_target="tpu_custom_call" | custom-call | bytes 2000000 | tf_op jit(solution)/shard_map/edges/pallas_call | solution.py:258
  41.9 0.0 copy-start.4
  41.9 0.7 copy-done.4
  42.7 0.0 collective-permute-start.2
  42.7 5.4 %collective-permute-start.3 = (f32[10,40,128]{2,1,0:T(8,128)}, f32[10,40,128]{2,1,0:T(8,128)S(1)}, u32[]{:S(2)}, u32[]{:S(2)}) collective-permute-start(f32[10,40,128]{2,1,0:T(8,128)} %get-tuple-element.34), channel_id=1, source_target_pairs={{8,0},{16,8},{24,16},{32,24},{40,32},{48,40},{56,48},{64,56},{72,6... | collective-permute-start | bytes 614408 | tf_op jit(solution)/shard_map/ppermute | solution.py:512
  48.1 0.1 add_convert_fusion.place
  48.1 0.0 copy-start.1
  48.1 0.9 copy-done.1
  49.1 0.0 copy-start.3
  49.1 0.9 copy-done.3
  50.0 0.0 copy-start.5
  50.0 1.0 copy-done.5
  51.0 6.6 %first_interior.1 = (f32[48,40,128]{2,1,0:T(8,128)S(1)}, f32[48,40,128]{2,1,0:T(8,128)S(1)}, f32[48,40,128]{2,1,0:T(8,128)S(1)}) custom-call(f32[48,8,128]{2,1,0:T(8,128)S(1)} %copy-done.1, f32[48,8,128]{2,1,0:T(8,128)S(1)} %copy-done.3, f32[48,24,128]{2,1,0:T(8,128)S(1)} %get-tuple-element.25.load_in, f32[48,24,128]{2,1,0:T(8,128)S(1)} %get-tuple-element.26.kinetic, ...), custom_call_target="tpu_custom_call" | custom-call | bytes 30000000 | tf_op jit(solution)/shard_map/first_interior/pallas_call | solution.py:131
  57.6 0.0 collective-permute-done.2.te_lo.lo
  57.6 0.0 collective-permute-done.3.te_hi.hi
  57.6 3.1 %bands.2 = (f32[48,32,128]{2,1,0:T(8,128)S(1)}, f32[24,8,128]{2,1,0:T(8,128)S(1)}, f32[24,8,128]{2,1,0:T(8,128)S(1)}) custom-call(s32[2]{0:T(128)S(1)} %add_convert_fusion.place, f32[48,40,128]{2,1,0:T(8,128)S(1)} %get-tuple-element.22.te, f32[48,40,128]{2,1,0:T(8,128)S(1)} %get-tuple-element.31.heat, f32[48,40,128]{2,1,0:T(8,128)S(1)} %get-tuple-element.32.load, ...), custom_call_target="tpu_custom_call" | custom-call | bytes 8000000 | tf_op jit(solution)/shard_map/bands/pallas_call | solution.py:200
  60.7 0.7 collective-permute-start.4
  61.3 3.5 %collective-permute-start.5 = (f32[24,8,128]{2,1,0:T(8,128)S(1)}, f32[24,8,128]{2,1,0:T(8,128)S(1)}, u32[]{:S(2)}, u32[]{:S(2)}) collective-permute-start(f32[24,8,128]{2,1,0:T(8,128)S(1)} %get-tuple-element.38), channel_id=1, source_target_pairs={{1,0},{2,1},{3,2},{4,3},{5,4},{6,5},{7,6},{0,7},{9,8},{10,9},{11,1... | collective-permute-start | bytes 294920 | tf_op jit(solution)/shard_map/ppermute | solution.py:512
  64.9 2.6 %collective-permute-done.4.before = f32[24,8,128]{2,1,0:T(8,128)S(1)} collective-permute-done((f32[24,8,128]{2,1,0:T(8,128)S(1)}, f32[24,8,128]{2,1,0:T(8,128)S(1)}, u32[]{:S(2)}, u32[]{:S(2)}) %collective-permute-start.4) | collective-permute-done | bytes 98336 | tf_op jit(solution)/shard_map/ppermute | solution.py:511
  67.5 0.0 collective-permute-done.5.after
  67.5 0.1 second_brick.1
  67.5 0.3 collective-permute-start.6
  67.8 5.3 %collective-permute-start.7 = (f32[4,40,128]{2,1,0:T(8,128)S(1)}, f32[4,40,128]{2,1,0:T(8,128)S(1)}, u32[]{:S(2)}, u32[]{:S(2)}) collective-permute-start(f32[4,40,128]{2,1,0:T(8,128)S(1)} %get-tuple-element.41), channel_id=1, source_target_pairs={{8,0},{16,8},{24,16},{32,24},{40,32},{48,40},{56,48},{64,56},{72,6... | collective-permute-start | bytes 245768 | tf_op jit(solution)/shard_map/ppermute | solution.py:512
  73.2 6.4 %interior.1.inner = f32[48,40,128]{2,1,0:T(8,128)S(1)} custom-call(f32[48,40,128]{2,1,0:T(8,128)S(1)} %get-tuple-element.39.te, f32[48,40,128]{2,1,0:T(8,128)S(1)} %get-tuple-element.31.heat, f32[48,40,128]{2,1,0:T(8,128)S(1)} %get-tuple-element.32.load), custom_call_target="tpu_custom_call" | custom-call | bytes 25000000 | tf_op jit(solution)/shard_map/interior/pallas_call | solution.py:99
  79.6 0.0 copy-start.7
  79.6 0.0 copy-start.8
  79.6 0.0 copy-start.10
  79.6 0.0 copy-start.12
  79.6 0.0 collective-permute-done.6.te_lo
  79.6 0.0 collective-permute-done.7.te_hi
  79.6 3.9 %bands.3 = f32[48,32,128]{2,1,0:T(8,128)} custom-call(s32[2]{0:T(128)S(1)} %add_convert_fusion.place, f32[48,40,128]{2,1,0:T(8,128)S(1)} %get-tuple-element.39.te, f32[48,40,128]{2,1,0:T(8,128)S(1)} %get-tuple-element.31.heat, f32[48,40,128]{2,1,0:T(8,128)S(1)} %get-tuple-element.32.load, f32[4,40,128]{2,1,0:T(8,128)S(1)} %collective-permute-done.6.te_lo, ...), custom_call_target="tpu_custom_call" | custom-call | bytes 8000000 | tf_op jit(solution)/shard_map/bands/pallas_call | solution.py:200
  83.5 5.4 %all-to-all-start.1 = ((f32[48,32,128]{2,1,0:T(8,128)}), f32[48,32,128]{2,1,0:T(8,128)S(1)}, u32[]{:S(2)}, u32[]{:S(2)}) async-start(f32[48,32,128]{2,1,0:T(8,128)} %bands.3), calls=%async_computation.1 | async-start | bytes 1572864 | tf_op jit(solution)/shard_map/all_to_all | solution.py:517
  88.9 0.0 copy-done.7
  88.9 0.0 copy-done.8
  88.9 0.0 copy-done.10
  89.0 0.0 copy-done.12
  89.0 14.0 %read_atoms.1 = f32[3,1,16384]{2,1,0:T(1,128)} custom-call(s32[1,1]{1,0:T(1,128)S(6)} %copy.11.count, f32[1536,128]{1,0:T(8,128)} %bitcast.9.te, s32[1,16384]{1,0:T(1,128)S(1)} %bitcast.21, s32[1,16384]{1,0:T(1,128)S(1)} %bitcast.24, f32[3,1,16384]{2,1,0:T(1,128)S(1)} %bitcast.17, f32[3,1,16384]{2,1,0:T(1,128)S(1)} %bitcast.18), custom_call_target="tpu_custom_call" | custom-call | flops 12884901888 | bytes 4000000 | tf_op jit(solution)/shard_map/read_atoms/pallas_call | solution.py:487
  103.0 0.0 all-to-all-done.1
  103.0 0.9 copy.9
Async XLA Ops:
  3.4 33.5 %all-to-all-start = ((f32[96,40,128]{2,1,0:T(8,128)}), f32[96,40,128]{2,1,0:T(8,128)}, u32[]{:S(2)}, u32[]{:S(2)}) async-start(f32[96,40,128]{2,1,0:T(8,128)} %bitcast.25), calls=%async_computation | async-start | bytes 3932160 | tf_op jit(solution)/shard_map/all_to_all | solution.py:517
  10.0 12.1 %copy-start.6 = (f32[3,1,1,16384]{3,2,1,0:T(1,128)S(1)}, f32[3,1,1,16384]{3,2,1,0:T(1,128)}, u32[]{:S(2)}) copy-start(f32[3,1,1,16384]{3,2,1,0:T(1,128)} %param.9) | copy-start | bytes 589828
  10.0 12.1 %copy-start.9 = (s32[1,1,16384]{2,1,0:T(1,128)S(1)}, s32[1,1,16384]{2,1,0:T(1,128)}, u32[]{:S(2)}) copy-start(s32[1,1,16384]{2,1,0:T(1,128)} %param.11) | copy-start | bytes 196612
  10.0 12.1 %copy-start.11 = (s32[1,1,16384]{2,1,0:T(1,128)S(1)}, s32[1,1,16384]{2,1,0:T(1,128)}, u32[]{:S(2)}) copy-start(s32[1,1,16384]{2,1,0:T(1,128)} %param.12) | copy-start | bytes 196612
  18.0 21.7 %collective-permute-start = (f32[12,3,8,128]{3,2,1,0:T(8,128)}, f32[12,3,8,128]{3,2,1,0:T(8,128)}, u32[]{:S(2)}, u32[]{:S(2)}) collective-permute-start(f32[12,3,8,128]{3,2,1,0:T(8,128)} %get-tuple-element.27), channel_id=1, source_target_pairs={{0,1},{1,2},{2,3},{3,4},{4,5},{5,6},{6,7},{7,0},{8,9},{9,10},{10,1... | collective-permute-start | bytes 442376 | tf_op jit(solution)/shard_map/ppermute | solution.py:511
  20.0 20.1 %collective-permute-start.1 = (f32[12,3,8,128]{3,2,1,0:T(8,128)}, f32[12,3,8,128]{3,2,1,0:T(8,128)}, u32[]{:S(2)}, u32[]{:S(2)}) collective-permute-start(f32[12,3,8,128]{3,2,1,0:T(8,128)} %get-tuple-element.28), channel_id=1, source_target_pairs={{1,0},{2,1},{3,2},{4,3},{5,4},{6,5},{7,6},{0,7},{9,8},{10,9},{11,1... | collective-permute-start | bytes 442376 | tf_op jit(solution)/shard_map/ppermute | solution.py:512
  36.8 3.3 %copy-start = (f32[48,8,128]{2,1,0:T(8,128)S(1)}, f32[48,8,128]{2,1,0:T(8,128)}, u32[]{:S(2)}) copy-start(f32[48,8,128]{2,1,0:T(8,128)} %get-tuple-element.23.own_head) | copy-start | bytes 589828
  36.8 3.3 %copy-start.2 = (f32[48,8,128]{2,1,0:T(8,128)S(1)}, f32[48,8,128]{2,1,0:T(8,128)}, u32[]{:S(2)}) copy-start(f32[48,8,128]{2,1,0:T(8,128)} %get-tuple-element.24.own_tail) | copy-start | bytes 589828
  41.9 0.7 copy-start.4
  42.7 14.9 %collective-permute-start.2 = (f32[10,40,128]{2,1,0:T(8,128)}, f32[10,40,128]{2,1,0:T(8,128)S(1)}, u32[]{:S(2)}, u32[]{:S(2)}) collective-permute-start(f32[10,40,128]{2,1,0:T(8,128)} %get-tuple-element.33), channel_id=1, source_target_pairs={{0,8},{8,16},{16,24},{24,32},{32,40},{40,48},{48,56},{56,64},{64,7... | collective-permute-start | bytes 614408 | tf_op jit(solution)/shard_map/ppermute | solution.py:511
  42.7 14.9 %collective-permute-start.3 = (f32[10,40,128]{2,1,0:T(8,128)}, f32[10,40,128]{2,1,0:T(8,128)S(1)}, u32[]{:S(2)}, u32[]{:S(2)}) collective-permute-start(f32[10,40,128]{2,1,0:T(8,128)} %get-tuple-element.34), channel_id=1, source_target_pairs={{8,0},{16,8},{24,16},{32,24},{40,32},{48,40},{56,48},{64,56},{72,6... | collective-permute-start | bytes 614408 | tf_op jit(solution)/shard_map/ppermute | solution.py:512
  48.1 0.9 copy-start.1
  49.1 0.9 copy-start.3
  50.0 1.0 copy-start.5
  60.7 6.8 %collective-permute-start.4 = (f32[24,8,128]{2,1,0:T(8,128)S(1)}, f32[24,8,128]{2,1,0:T(8,128)S(1)}, u32[]{:S(2)}, u32[]{:S(2)}) collective-permute-start(f32[24,8,128]{2,1,0:T(8,128)S(1)} %get-tuple-element.37), channel_id=1, source_target_pairs={{0,1},{1,2},{2,3},{3,4},{4,5},{5,6},{6,7},{7,0},{8,9},{9,10},{10,1... | collective-permute-start | bytes 294920 | tf_op jit(solution)/shard_map/ppermute | solution.py:511
  61.3 6.1 %collective-permute-start.5 = (f32[24,8,128]{2,1,0:T(8,128)S(1)}, f32[24,8,128]{2,1,0:T(8,128)S(1)}, u32[]{:S(2)}, u32[]{:S(2)}) collective-permute-start(f32[24,8,128]{2,1,0:T(8,128)S(1)} %get-tuple-element.38), channel_id=1, source_target_pairs={{1,0},{2,1},{3,2},{4,3},{5,4},{6,5},{7,6},{0,7},{9,8},{10,9},{11,1... | collective-permute-start | bytes 294920 | tf_op jit(solution)/shard_map/ppermute | solution.py:512
  67.5 12.1 %collective-permute-start.6 = (f32[4,40,128]{2,1,0:T(8,128)S(1)}, f32[4,40,128]{2,1,0:T(8,128)S(1)}, u32[]{:S(2)}, u32[]{:S(2)}) collective-permute-start(f32[4,40,128]{2,1,0:T(8,128)S(1)} %get-tuple-element.40), channel_id=1, source_target_pairs={{0,8},{8,16},{16,24},{24,32},{32,40},{40,48},{48,56},{56,64},{64,7... | collective-permute-start | bytes 245768 | tf_op jit(solution)/shard_map/ppermute | solution.py:511
  67.8 11.8 %collective-permute-start.7 = (f32[4,40,128]{2,1,0:T(8,128)S(1)}, f32[4,40,128]{2,1,0:T(8,128)S(1)}, u32[]{:S(2)}, u32[]{:S(2)}) collective-permute-start(f32[4,40,128]{2,1,0:T(8,128)S(1)} %get-tuple-element.41), channel_id=1, source_target_pairs={{8,0},{16,8},{24,16},{32,24},{40,32},{48,40},{56,48},{64,56},{72,6... | collective-permute-start | bytes 245768 | tf_op jit(solution)/shard_map/ppermute | solution.py:512
  79.6 9.4 %copy-start.7 = (f32[3,1,1,16384]{3,2,1,0:T(1,128)S(1)}, f32[3,1,1,16384]{3,2,1,0:T(1,128)}, u32[]{:S(2)}) copy-start(f32[3,1,1,16384]{3,2,1,0:T(1,128)} %param.9) | copy-start | bytes 589828
  79.6 9.4 %copy-start.8 = (f32[3,1,1,16384]{3,2,1,0:T(1,128)S(1)}, f32[3,1,1,16384]{3,2,1,0:T(1,128)}, u32[]{:S(2)}) copy-start(f32[3,1,1,16384]{3,2,1,0:T(1,128)} %param.10) | copy-start | bytes 589828
  79.6 9.4 %copy-start.10 = (s32[1,1,16384]{2,1,0:T(1,128)S(1)}, s32[1,1,16384]{2,1,0:T(1,128)}, u32[]{:S(2)}) copy-start(s32[1,1,16384]{2,1,0:T(1,128)} %param.11) | copy-start | bytes 196612
  79.6 9.4 %copy-start.12 = (s32[1,1,16384]{2,1,0:T(1,128)S(1)}, s32[1,1,16384]{2,1,0:T(1,128)}, u32[]{:S(2)}) copy-start(s32[1,1,16384]{2,1,0:T(1,128)} %param.12) | copy-start | bytes 196612
  83.5 19.5 %all-to-all-start.1 = ((f32[48,32,128]{2,1,0:T(8,128)}), f32[48,32,128]{2,1,0:T(8,128)S(1)}, u32[]{:S(2)}, u32[]{:S(2)}) async-start(f32[48,32,128]{2,1,0:T(8,128)} %bands.3), calls=%async_computation.1 | async-start | bytes 1572864 | tf_op jit(solution)/shard_map/all_to_all | solution.py:517

commit v6 on v4

--- a/solution.py
+++ b/solution.py
@@ -510,7 +510,7 @@
 
 def read_atoms(count, te, column, lane, velocities, noise):
     slots = column.shape[1]
-    block = min(BLOCK, slots)
+    block = min(2 * BLOCK, slots)
     return pl.pallas_call(
         functools.partial(read_kernel, block),
         grid=(slots // block,),
@@ -525,7 +525,7 @@
         ],
         out_specs=blocks_of((3, 1), block),
         scratch_shapes=[pltpu.VMEM((3 * NZ, COLS), FLOAT8)],
-        compiler_params=params(48),
+        compiler_params=params(60),
         cost_estimate=pl.CostEstimate(
             flops=4 * slots * COLS * NZ, bytes_accessed=4_000_000, transcendentals=0
         ),

time: 102 us -> 102 us (level)
  no operation moved by 1% of the time
where the time goes in v6:
time: 102 us; the launch traced here: 101 us
  Pallas kernels  62.2 us (61%)
  starting transfers between devices  30.8 us (30%)
  waiting for transfers between devices  5.71 us (6%)
  between operations  1.42 us (1%)
    pallas_call x2, Pallas kernels, bin_atoms(): pl.pallas_call(functools.partial(bin_kernel, block, faces), grid=(slots /...  22.7 us
    ppermute x4, starting transfers between devices, to_both_sides(): lax.ppermute(head, axis, [((i + 1) % count, i) for i in range(count)])  16.4 us
    pallas_call x1, Pallas kernels, read_atoms(): pl.pallas_call(functools.partial(read_kernel, block), grid=(slots // bloc...  14 us
    all_to_all x2, starting transfers between devices, exchanged(): return lax.all_to_all(blocks, 'gy', split_axis=0, concat_axis=0, tiled=True)  11.4 us
    pallas_call x1, Pallas kernels, first_interior(): pl.pallas_call(functools.partial(first_interior_kernel, parts), out_shape...  8.17 us
    pallas_call x2, Pallas kernels, bands(): pl.pallas_call(functools.partial(bands_kernel, last), out_shape=shapes, i...  6.95 us
    pallas_call x1, Pallas kernels, second_interior(): pl.pallas_call(second_interior_kernel, out_shape=f32(CX, ROWS, NZ), in_sp...  6.39 us
    ppermute x4, waiting for transfers between devices, to_both_sides(): lax.ppermute(tail, axis, [(i, (i + 1) % count) for i in range(count)])  5.21 us
  transfers between devices with their start and end apart: 10, of which 3 were waited for; matrix products, arithmetic and copies ran while one was open for 0% of the time, Pallas kernels for 51%

profile of v6, /device:TPU:4, one launch (start us, length us, event | category | flops | bytes accessed | tf_op | source)
XLA Modules:
  0.0 101.2 jit_solution(7562629206366422735)
XLA Ops:
  0.6 2.7 %widen.1 = f32[8,12,40,128]{3,2,1,0:T(8,128)} custom-call(f32[6,256,128]{2,1,0:T(8,128)} %te.1, f32[6,256,128]{2,1,0:T(8,128)} %source.1), custom_call_target="tpu_custom_call" | custom-call | bytes 4000000 | tf_op jit(solution)/shard_map/widen/pallas_call | solution.py:327
  3.3 6.0 %all-to-all-start = ((f32[96,40,128]{2,1,0:T(8,128)}), f32[96,40,128]{2,1,0:T(8,128)}, u32[]{:S(2)}, u32[]{:S(2)}) async-start(f32[96,40,128]{2,1,0:T(8,128)} %bitcast.24), calls=%async_computation | async-start | bytes 3932160 | tf_op jit(solution)/shard_map/all_to_all | solution.py:544
  9.9 0.0 copy-start.2
  10.0 0.0 copy-start.3
  10.0 0.0 copy-start.4
  10.0 7.9 %bin_faces.1 = (f32[48,8,128]{2,1,0:T(8,128)}, f32[48,8,128]{2,1,0:T(8,128)}, f32[12,3,8,128]{3,2,1,0:T(8,128)}, f32[12,3,8,128]{3,2,1,0:T(8,128)}) custom-call(s32[1,1]{1,0:T(1,128)S(6)} %copy.11.count, s32[1,16384]{1,0:T(1,128)} %bitcast.18, s32[1,16384]{1,0:T(1,128)} %bitcast.21, f32[3,1,16384]{2,1,0:T(1,128)} %bitcast.15), custom_call_target="tpu_custom_call" | custom-call | flops 4831838208 | bytes 4000000 | tf_op jit(solution)/shard_map/bin_faces/pallas_call | solution.py:478
  17.9 2.0 %collective-permute-start = (f32[12,3,8,128]{3,2,1,0:T(8,128)}, f32[12,3,8,128]{3,2,1,0:T(8,128)S(1)}, u32[]{:S(2)}, u32[]{:S(2)}) collective-permute-start(f32[12,3,8,128]{3,2,1,0:T(8,128)} %get-tuple-element.25), channel_id=1, source_target_pairs={{0,1},{1,2},{2,3},{3,4},{4,5},{5,6},{6,7},{7,0},{8,9},{9,10},{10,1... | collective-permute-start | bytes 442376 | tf_op jit(solution)/shard_map/ppermute | solution.py:538
  20.0 0.0 copy-start
  20.0 0.0 copy-start.1
  20.0 2.2 %collective-permute-start.1 = (f32[12,3,8,128]{3,2,1,0:T(8,128)}, f32[12,3,8,128]{3,2,1,0:T(8,128)S(1)}, u32[]{:S(2)}, u32[]{:S(2)}) collective-permute-start(f32[12,3,8,128]{3,2,1,0:T(8,128)} %get-tuple-element.26), channel_id=1, source_target_pairs={{1,0},{2,1},{3,2},{4,3},{5,4},{6,5},{7,6},{0,7},{9,8},{10,9},{11,1... | collective-permute-start | bytes 442376 | tf_op jit(solution)/shard_map/ppermute | solution.py:539
  22.2 0.0 copy-done.2
  22.2 0.0 copy-done.3
  22.2 0.0 copy-done.4
  22.2 14.7 %bin_inner.1 = (f32[48,24,128]{2,1,0:T(8,128)S(1)}, f32[48,24,128]{2,1,0:T(8,128)S(1)}) custom-call(s32[1,1]{1,0:T(1,128)S(6)} %copy.11.count, s32[1,16384]{1,0:T(1,128)S(1)} %bitcast.20, s32[1,16384]{1,0:T(1,128)S(1)} %bitcast.23, f32[3,1,16384]{2,1,0:T(1,128)S(1)} %bitcast.17), custom_call_target="tpu_custom_call" | custom-call | flops 14495514624 | bytes 4000000 | tf_op jit(solution)/shard_map/bin_inner/pallas_call | solution.py:478
  36.9 2.6 %collective-permute-done.refs_4_ = f32[12,3,8,128]{3,2,1,0:T(8,128)S(1)} collective-permute-done((f32[12,3,8,128]{3,2,1,0:T(8,128)}, f32[12,3,8,128]{3,2,1,0:T(8,128)S(1)}, u32[]{:S(2)}, u32[]{:S(2)}) %collective-permute-start) | collective-permute-done | bytes 147488 | tf_op jit(solution)/shard_map/ppermute | solution.py:538
  39.5 0.5 collective-permute-done.1.refs_5_
  40.0 0.0 all-to-all-done.refs_6_.fields
  40.0 0.0 copy-done
  40.0 0.0 copy-done.1
  40.0 1.2 %edges.1 = (f32[16,40,128]{2,1,0:T(8,128)S(1)}, f32[10,40,128]{2,1,0:T(8,128)S(1)}, f32[10,40,128]{2,1,0:T(8,128)S(1)}, f32[2,48,8,128]{3,2,1,0:T(8,128)S(1)}) custom-call(f32[48,8,128]{2,1,0:T(8,128)S(1)} %copy-done, f32[48,8,128]{2,1,0:T(8,128)S(1)} %copy-done.1, f32[48,24,128]{2,1,0:T(8,128)S(1)} %get-tuple-element.23.refs_2_.load_in, ...), custom_call_target="tpu_custom_call" | custom-call | bytes 2000000 | tf_op jit(solution)/shard_map/edges/pallas_call | solution.py:280
  41.2 0.1 collective-permute-start.2
  41.3 5.3 %collective-permute-start.3 = (f32[10,40,128]{2,1,0:T(8,128)S(1)}, f32[10,40,128]{2,1,0:T(8,128)S(1)}, u32[]{:S(2)}, u32[]{:S(2)}) collective-permute-start(f32[10,40,128]{2,1,0:T(8,128)S(1)} %get-tuple-element.32), channel_id=1, source_target_pairs={{8,0},{16,8},{24,16},{32,24},{40,32},{48,40},{56,48},{64,56},{72,6... | collective-permute-start | bytes 614408 | tf_op jit(solution)/shard_map/ppermute | solution.py:539
  46.6 0.1 add_convert_fusion.place
  46.7 8.2 %first_interior.1 = (f32[48,40,128]{2,1,0:T(8,128)S(1)}, f32[48,40,128]{2,1,0:T(8,128)S(1)}, f32[48,40,128]{2,1,0:T(8,128)S(1)}) custom-call(f32[48,8,128]{2,1,0:T(8,128)S(1)} %copy-done, f32[48,8,128]{2,1,0:T(8,128)S(1)} %copy-done.1, f32[48,24,128]{2,1,0:T(8,128)S(1)} %get-tuple-element.23.refs_2_.load_in, ...), custom_call_target="tpu_custom_call" | custom-call | bytes 30000000 | tf_op jit(solution)/shard_map/first_interior/pallas_call | solution.py:148
  54.9 0.0 collective-permute-done.2.te_lo.lo
  54.9 0.0 collective-permute-done.3.te_hi.hi
  54.9 3.1 %bands.2 = (f32[48,32,128]{2,1,0:T(8,128)S(1)}, f32[24,8,128]{2,1,0:T(8,128)S(1)}, f32[24,8,128]{2,1,0:T(8,128)S(1)}) custom-call(s32[2]{0:T(128)S(1)} %add_convert_fusion.place, f32[16,40,128]{2,1,0:T(8,128)S(1)} %get-tuple-element.27.te, f32[48,40,128]{2,1,0:T(8,128)S(1)} %get-tuple-element.29.heat, f32[48,40,128]{2,1,0:T(8,128)S(1)} %get-tuple-element.30.load, ...), custom_call_target="tpu_custom_call" | custom-call | bytes 8000000 | tf_op jit(solution)/shard_map/bands/pallas_call | solution.py:219
  58.0 0.7 collective-permute-start.4
  58.6 3.5 %collective-permute-start.5 = (f32[24,8,128]{2,1,0:T(8,128)S(1)}, f32[24,8,128]{2,1,0:T(8,128)S(1)}, u32[]{:S(2)}, u32[]{:S(2)}) collective-permute-start(f32[24,8,128]{2,1,0:T(8,128)S(1)} %get-tuple-element.36), channel_id=1, source_target_pairs={{1,0},{2,1},{3,2},{4,3},{5,4},{6,5},{7,6},{0,7},{9,8},{10,9},{11,1... | collective-permute-start | bytes 294920 | tf_op jit(solution)/shard_map/ppermute | solution.py:539
  62.2 2.6 %collective-permute-done.4.before = f32[24,8,128]{2,1,0:T(8,128)S(1)} collective-permute-done((f32[24,8,128]{2,1,0:T(8,128)S(1)}, f32[24,8,128]{2,1,0:T(8,128)S(1)}, u32[]{:S(2)}, u32[]{:S(2)}) %collective-permute-start.4) | collective-permute-done | bytes 98336 | tf_op jit(solution)/shard_map/ppermute | solution.py:538
  64.8 0.0 collective-permute-done.5.after
  64.8 0.1 second_brick.1
  64.9 0.3 collective-permute-start.6
  65.1 5.3 %collective-permute-start.7 = (f32[4,40,128]{2,1,0:T(8,128)S(1)}, f32[4,40,128]{2,1,0:T(8,128)S(1)}, u32[]{:S(2)}, u32[]{:S(2)}) collective-permute-start(f32[4,40,128]{2,1,0:T(8,128)S(1)} %get-tuple-element.39), channel_id=1, source_target_pairs={{8,0},{16,8},{24,16},{32,24},{40,32},{48,40},{56,48},{64,56},{72,6... | collective-permute-start | bytes 245768 | tf_op jit(solution)/shard_map/ppermute | solution.py:539
  70.5 6.4 %interior.1.inner = f32[48,40,128]{2,1,0:T(8,128)S(1)} custom-call(f32[48,40,128]{2,1,0:T(8,128)S(1)} %get-tuple-element.37.te, f32[48,40,128]{2,1,0:T(8,128)S(1)} %get-tuple-element.29.heat, f32[48,40,128]{2,1,0:T(8,128)S(1)} %get-tuple-element.30.load), custom_call_target="tpu_custom_call" | custom-call | bytes 25000000 | tf_op jit(solution)/shard_map/interior/pallas_call | solution.py:99
  76.9 0.0 collective-permute-done.6.te_lo
  76.9 0.0 collective-permute-done.7.te_hi
  76.9 3.9 %bands.3 = f32[48,32,128]{2,1,0:T(8,128)} custom-call(s32[2]{0:T(128)S(1)} %add_convert_fusion.place, f32[48,40,128]{2,1,0:T(8,128)S(1)} %get-tuple-element.37.te, f32[48,40,128]{2,1,0:T(8,128)S(1)} %get-tuple-element.29.heat, f32[48,40,128]{2,1,0:T(8,128)S(1)} %get-tuple-element.30.load, f32[4,40,128]{2,1,0:T(8,128)S(1)} %collective-permute-done.6.te_lo, ...), custom_call_target="tpu_custom_call" | custom-call | bytes 8000000 | tf_op jit(solution)/shard_map/bands/pallas_call | solution.py:219
  80.8 5.4 %all-to-all-start.1 = ((f32[48,32,128]{2,1,0:T(8,128)}), f32[48,32,128]{2,1,0:T(8,128)S(1)}, u32[]{:S(2)}, u32[]{:S(2)}) async-start(f32[48,32,128]{2,1,0:T(8,128)} %bands.3), calls=%async_computation.1 | async-start | bytes 1572864 | tf_op jit(solution)/shard_map/all_to_all | solution.py:544
  86.2 14.0 %read_atoms.1 = f32[3,1,16384]{2,1,0:T(1,128)} custom-call(s32[1,1]{1,0:T(1,128)S(6)} %copy.11.count, f32[1536,128]{1,0:T(8,128)} %bitcast.9.te, s32[1,16384]{1,0:T(1,128)} %bitcast.19, s32[1,16384]{1,0:T(1,128)} %bitcast.22, f32[3,1,16384]{2,1,0:T(1,128)} %bitcast.16, f32[3,1,16384]{2,1,0:T(1,128)} %bitcast.27), custom_call_target="tpu_custom_call" | custom-call | flops 12884901888 | bytes 4000000 | tf_op jit(solution)/shard_map/read_atoms/pallas_call | solution.py:514
  100.2 0.0 all-to-all-done.1
  100.2 0.9 copy.9
Async XLA Ops:
  3.3 36.6 %all-to-all-start = ((f32[96,40,128]{2,1,0:T(8,128)}), f32[96,40,128]{2,1,0:T(8,128)}, u32[]{:S(2)}, u32[]{:S(2)}) async-start(f32[96,40,128]{2,1,0:T(8,128)} %bitcast.24), calls=%async_computation | async-start | bytes 3932160 | tf_op jit(solution)/shard_map/all_to_all | solution.py:544
  9.9 12.2 %copy-start.2 = (f32[3,1,1,16384]{3,2,1,0:T(1,128)S(1)}, f32[3,1,1,16384]{3,2,1,0:T(1,128)}, u32[]{:S(2)}) copy-start(f32[3,1,1,16384]{3,2,1,0:T(1,128)} %param.9) | copy-start | bytes 589828
  10.0 12.2 %copy-start.3 = (s32[1,1,16384]{2,1,0:T(1,128)S(1)}, s32[1,1,16384]{2,1,0:T(1,128)}, u32[]{:S(2)}) copy-start(s32[1,1,16384]{2,1,0:T(1,128)} %param.11) | copy-start | bytes 196612
  10.0 12.2 %copy-start.4 = (s32[1,1,16384]{2,1,0:T(1,128)S(1)}, s32[1,1,16384]{2,1,0:T(1,128)}, u32[]{:S(2)}) copy-start(s32[1,1,16384]{2,1,0:T(1,128)} %param.12) | copy-start | bytes 196612
  17.9 21.6 %collective-permute-start = (f32[12,3,8,128]{3,2,1,0:T(8,128)}, f32[12,3,8,128]{3,2,1,0:T(8,128)S(1)}, u32[]{:S(2)}, u32[]{:S(2)}) collective-permute-start(f32[12,3,8,128]{3,2,1,0:T(8,128)} %get-tuple-element.25), channel_id=1, source_target_pairs={{0,1},{1,2},{2,3},{3,4},{4,5},{5,6},{6,7},{7,0},{8,9},{9,10},{10,1... | collective-permute-start | bytes 442376 | tf_op jit(solution)/shard_map/ppermute | solution.py:538
  20.0 20.0 %copy-start = (f32[48,8,128]{2,1,0:T(8,128)S(1)}, f32[48,8,128]{2,1,0:T(8,128)}, u32[]{:S(2)}) copy-start(f32[48,8,128]{2,1,0:T(8,128)} %get-tuple-element.21.refs_0_.own_head) | copy-start | bytes 589828
  20.0 20.0 %copy-start.1 = (f32[48,8,128]{2,1,0:T(8,128)S(1)}, f32[48,8,128]{2,1,0:T(8,128)}, u32[]{:S(2)}) copy-start(f32[48,8,128]{2,1,0:T(8,128)} %get-tuple-element.22.refs_1_.own_tail) | copy-start | bytes 589828
  20.0 20.0 %collective-permute-start.1 = (f32[12,3,8,128]{3,2,1,0:T(8,128)}, f32[12,3,8,128]{3,2,1,0:T(8,128)S(1)}, u32[]{:S(2)}, u32[]{:S(2)}) collective-permute-start(f32[12,3,8,128]{3,2,1,0:T(8,128)} %get-tuple-element.26), channel_id=1, source_target_pairs={{1,0},{2,1},{3,2},{4,3},{5,4},{6,5},{7,6},{0,7},{9,8},{10,9},{11,1... | collective-permute-start | bytes 442376 | tf_op jit(solution)/shard_map/ppermute | solution.py:539
  41.2 13.7 %collective-permute-start.2 = (f32[10,40,128]{2,1,0:T(8,128)S(1)}, f32[10,40,128]{2,1,0:T(8,128)S(1)}, u32[]{:S(2)}, u32[]{:S(2)}) collective-permute-start(f32[10,40,128]{2,1,0:T(8,128)S(1)} %get-tuple-element.31), channel_id=1, source_target_pairs={{0,8},{8,16},{16,24},{24,32},{32,40},{40,48},{48,56},{56,64},{64,7... | collective-permute-start | bytes 614408 | tf_op jit(solution)/shard_map/ppermute | solution.py:538
  41.3 13.6 %collective-permute-start.3 = (f32[10,40,128]{2,1,0:T(8,128)S(1)}, f32[10,40,128]{2,1,0:T(8,128)S(1)}, u32[]{:S(2)}, u32[]{:S(2)}) collective-permute-start(f32[10,40,128]{2,1,0:T(8,128)S(1)} %get-tuple-element.32), channel_id=1, source_target_pairs={{8,0},{16,8},{24,16},{32,24},{40,32},{48,40},{56,48},{64,56},{72,6... | collective-permute-start | bytes 614408 | tf_op jit(solution)/shard_map/ppermute | solution.py:539
  58.0 6.8 %collective-permute-start.4 = (f32[24,8,128]{2,1,0:T(8,128)S(1)}, f32[24,8,128]{2,1,0:T(8,128)S(1)}, u32[]{:S(2)}, u32[]{:S(2)}) collective-permute-start(f32[24,8,128]{2,1,0:T(8,128)S(1)} %get-tuple-element.35), channel_id=1, source_target_pairs={{0,1},{1,2},{2,3},{3,4},{4,5},{5,6},{6,7},{7,0},{8,9},{9,10},{10,1... | collective-permute-start | bytes 294920 | tf_op jit(solution)/shard_map/ppermute | solution.py:538
  58.6 6.1 %collective-permute-start.5 = (f32[24,8,128]{2,1,0:T(8,128)S(1)}, f32[24,8,128]{2,1,0:T(8,128)S(1)}, u32[]{:S(2)}, u32[]{:S(2)}) collective-permute-start(f32[24,8,128]{2,1,0:T(8,128)S(1)} %get-tuple-element.36), channel_id=1, source_target_pairs={{1,0},{2,1},{3,2},{4,3},{5,4},{6,5},{7,6},{0,7},{9,8},{10,9},{11,1... | collective-permute-start | bytes 294920 | tf_op jit(solution)/shard_map/ppermute | solution.py:539
  64.9 12.0 %collective-permute-start.6 = (f32[4,40,128]{2,1,0:T(8,128)S(1)}, f32[4,40,128]{2,1,0:T(8,128)S(1)}, u32[]{:S(2)}, u32[]{:S(2)}) collective-permute-start(f32[4,40,128]{2,1,0:T(8,128)S(1)} %get-tuple-element.38), channel_id=1, source_target_pairs={{0,8},{8,16},{16,24},{24,32},{32,40},{40,48},{48,56},{56,64},{64,7... | collective-permute-start | bytes 245768 | tf_op jit(solution)/shard_map/ppermute | solution.py:538
  65.1 11.8 %collective-permute-start.7 = (f32[4,40,128]{2,1,0:T(8,128)S(1)}, f32[4,40,128]{2,1,0:T(8,128)S(1)}, u32[]{:S(2)}, u32[]{:S(2)}) collective-permute-start(f32[4,40,128]{2,1,0:T(8,128)S(1)} %get-tuple-element.39), channel_id=1, source_target_pairs={{8,0},{16,8},{24,16},{32,24},{40,32},{48,40},{56,48},{64,56},{72,6... | collective-permute-start | bytes 245768 | tf_op jit(solution)/shard_map/ppermute | solution.py:539
  80.8 19.4 %all-to-all-start.1 = ((f32[48,32,128]{2,1,0:T(8,128)}), f32[48,32,128]{2,1,0:T(8,128)S(1)}, u32[]{:S(2)}, u32[]{:S(2)}) async-start(f32[48,32,128]{2,1,0:T(8,128)} %bands.3), calls=%async_computation.1 | async-start | bytes 1572864 | tf_op jit(solution)/shard_map/all_to_all | solution.py:544
